TPU v7x, 256 devices: a whole 4x4x8 slice. The times are simulated.
256 devices in a mesh: dp: 16 (over z, core), expert: 16 (over y, x).
Axes of the slice: x: 4, y: 4, z: 8, core: 2. Of those that a mesh axis runs over, the one named last changes fastest.
Arguments:
- tokens: bfloat16 [196608, 2048], P(('dp', 'expert')), may hold values from -6 to 6
- target: bfloat16 [196608, 2048], P(('dp', 'expert')), may hold values from -4 to 4
- route_index: int32 [16, 16, 16, 16], P('dp', None, 'expert'), may hold values from 0 to 767, as said below
- route_count: int32 [16, 16, 16], P('dp', None, 'expert'), may hold values from 1 to 16, as said below
- route_gate: float32 [16, 16, 16, 16], P('dp', None, 'expert'), may hold values from 0.1 to 1
- gate_weight: bfloat16 [2048, 16, 768], P('dp', 'expert'), may hold values from -0.125 to 0.125
- up_weight: bfloat16 [2048, 16, 768], P('dp', 'expert'), may hold values from -0.125 to 0.125
- down_weight: bfloat16 [2048, 16, 768], P('dp', 'expert'), may hold values from -0.21875 to 0.21875
Outputs:
- token_grad: bfloat16 [196608, 2048], P(('dp', 'expert'))
- gate_gradient: float32 [2048, 16, 768], P('dp', 'expert')
- up_gradient: float32 [2048, 16, 768], P('dp', 'expert')
- down_gradient: float32 [2048, 16, 768], P('dp', 'expert')
Inputs may be any that keep to these rules, and one draw needn't show every extreme that they name: `route_index`: within each list of 16 slots the indices are distinct; each names a token of the source device. `route_count`: in every group one expert has all 16 slots live from every source device; slots at or beyond the count are unused.
All inputs are finite; a program needn't handle non-finite values.
Results may differ from a plain program's by a relative error of at most 0.0059.
Values may be sent and summed in bfloat16 or wider, within the bound.
No kernel may reach another device: no remote copies, remote signals or barrier semaphores. Data moves between devices by JAX's collectives and lax.ppermute only.
A program may use at most 128 MiB of HBM per device.

v0:
```python
import jax
import jax.numpy as jnp
from jax import lax
from jax.sharding import PartitionSpec as P

F32 = jnp.float32
BF16 = jnp.bfloat16


def exchange(block):
    return lax.all_to_all(block, "expert", split_axis=0, concat_axis=0, tiled=True)


def dot(a, b, dims):
    return lax.dot_general(a, b, (dims, ((), ())), preferred_element_type=F32)


def on_device(
    tokens, target, route_index, route_count, route_gate, gate_weight, up_weight, down_weight
):
    groups = lax.axis_size("dp")
    sources = lax.axis_size("expert")
    local_index = route_index[0, :, 0, :]
    live_count = route_count[0, :, 0]
    per_source = local_index.shape[1]
    held, width = tokens.shape
    ff = gate_weight.shape[2]
    slots = sources * per_source

    with jax.named_scope("gather_weights"):
        own = jnp.concatenate([gate_weight[:, 0], up_weight[:, 0], down_weight[:, 0]], axis=1)
        full = lax.all_gather(own, "dp", axis=0, tiled=True)
        gate_up, down = full[:, : 2 * ff], full[:, 2 * ff :]

    with jax.named_scope("routing"):
        usable = jnp.arange(per_source, dtype=jnp.int32)[None, :] < live_count[:, None]
        flat_index = local_index.reshape(slots)
        live = usable.reshape(slots)
        weight = jnp.where(live, route_gate[0, :, 0, :].reshape(slots), 0.0)
        names = flat_index[:, None] == jnp.arange(held, dtype=jnp.int32)[None, :]
        pick = (names & live[:, None]).astype(BF16)
        same = flat_index[:, None] == flat_index[None, :]
        high = lax.reduce_precision(weight, 8, 7)
        low = weight - high
        mix_high = jnp.where(same, high[None, :], 0.0).astype(BF16)
        mix_low = jnp.where(same, low[None, :], 0.0).astype(BF16)

    with jax.named_scope("rows_out"):
        rows = dot(pick, tokens, ((1,), (0,))).astype(BF16)
        expert_rows = exchange(rows.reshape(sources, per_source, width)).reshape(slots, width)
        wanted = dot(pick, target, ((1,), (0,)))

    with jax.named_scope("forward"):
        pre = dot(expert_rows, gate_up, ((1,), (0,)))
        gate_pre, up_pre = pre[:, :ff], pre[:, ff:]
        sigma = jax.nn.sigmoid(gate_pre)
        active = gate_pre * sigma
        hidden = (active * up_pre).astype(BF16)
        expert_out = dot(hidden, down, ((1,), (1,))).astype(BF16)

    with jax.named_scope("combine"):
        returned = exchange(expert_out.reshape(sources, per_source, width)).reshape(slots, width)
        combined = dot(mix_high, returned, ((1,), (0,))) + dot(mix_low, returned, ((1,), (0,)))
        slot_grad = (weight[:, None] * (combined - wanted)).astype(BF16)
        owner_grad = exchange(slot_grad.reshape(sources, per_source, width)).reshape(slots, width)

    with jax.named_scope("backward"):
        hidden_grad = dot(owner_grad, down, ((1,), (0,)))
        gate_grad = (hidden_grad * up_pre * sigma * (1.0 + gate_pre * (1.0 - sigma))).astype(BF16)
        up_grad = (hidden_grad * active).astype(BF16)
        pre_grad = jnp.concatenate([gate_grad, up_grad], axis=1)

    with jax.named_scope("weight_gradients"):
        partial = jnp.concatenate(
            [
                dot(expert_rows, pre_grad, ((0,), (0,))).astype(BF16),
                dot(owner_grad, hidden, ((0,), (0,))).astype(BF16),
            ],
            axis=1,
        )
        summed = lax.psum_scatter(partial, "dp", scatter_dimension=0, tiled=True)
        scaled = summed.astype(F32) * (groups * sources * per_source) ** (-0.5)

    with jax.named_scope("token_gradient"):
        row_grad = dot(pre_grad, gate_up, ((1,), (1,))).astype(BF16)
        came_back = exchange(row_grad.reshape(sources, per_source, width)).reshape(slots, width)
        token_grad = dot(names.astype(BF16), came_back, ((0,), (0,))).astype(BF16)

    return (
        token_grad,
        scaled[:, None, :ff],
        scaled[:, None, ff : 2 * ff],
        scaled[:, None, 2 * ff :],
    )


def solution(mesh):
    return jax.shard_map(
        on_device,
        mesh=mesh,
        in_specs=(
            P(("dp", "expert"), None),
            P(("dp", "expert"), None),
            P("dp", None, "expert", None),
            P("dp", None, "expert"),
            P("dp", None, "expert", None),
            P("dp", "expert", None),
            P("dp", "expert", None),
            P("dp", "expert", None),
        ),
        out_specs=(
            P(("dp", "expert"), None),
            P("dp", "expert", None),
            P("dp", "expert", None),
            P("dp", "expert", None),
        ),
        check_vma=False,
    )
```

profile of v0, /device:TPU:2, one launch (start us, length us, event | category | flops | bytes accessed | tf_op | source)
XLA Modules:
  0.0 246.6 jit_solution(13958052397679693771)
XLA Ops:
  7.2 2.1 pad_maximum_fusion.2
  9.4 0.7 iota_compare_fusion.2
  10.2 0.5 broadcast.33
  10.7 1.4 reduce.6
  12.2 1.0 convolution_convert_fusion.3
  13.2 23.1 %all_to_all.20 = bf16[16,16,2048]{2,1,0:T(8,128)(2,1)S(1)} all-to-all(bf16[16,16,2048]{2,1,0:T(8,128)(2,1)S(1)} %bitcast.40), channel_id=1, replica_groups=mesh['dp'=16,'expert'=16] {'expert'}, dimensions={0} | all-to-all | bytes 2097152 | tf_op jit(solution)/shard_map/rows_out/all_to_all | solution.py:11
  36.3 38.0 %all-gather.2.cloned.1.call-done = bf16[2048,2304]{1,0:T(8,128)(2,1)} async-done(((bf16[128,2304]{1,0:T(8,128)(2,1)}), bf16[2048,2304]{1,0:T(8,128)(2,1)}) %all-gather.2.cloned.1.call-update) | async-done | bytes 9437200 | tf_op jit(solution)/shard_map/gather_weights/all_gather | solution.py:32
  74.3 4.6 %fusion.2 = f32[256,1536]{1,0:T(8,128)S(1)} fusion(bf16[256,2048]{1,0:T(8,128)(2,1)S(1)} %bitcast.34, bf16[2048,2304]{1,0:T(8,128)(2,1)} %all-gather.2.cloned.1.call-done), kind=kOutput, calls=%fused_computation.4 | convolution fusion | flops 1610612736 | bytes 8912896 | tf_op jit(solution)/shard_map/forward/dot_general | solution.py:15
  79.1 4.2 %fusion.13 = bf16[256,2048]{1,0:T(8,128)(2,1)} fusion(bf16[256,768]{1,0:T(8,128)(2,1)S(1)} %multiply_convert_fusion.2, bf16[2048,2304]{1,0:T(8,128)(2,1)} %all-gather.2.cloned.1.call-done), kind=kOutput, calls=%fused_computation.17 | convolution fusion | flops 805830656 | bytes 4587520 | tf_op jit(solution)/shard_map/forward/dot_general | solution.py:15
  83.3 7.3 %all-to-all-start.1 = ((bf16[16,16,2048]{2,1,0:T(8,128)(2,1)}), bf16[16,16,2048]{2,1,0:T(8,128)(2,1)S(1)}, u32[]{:S(2)}, u32[]{:S(2)}) async-start(bf16[16,16,2048]{2,1,0:T(8,128)(2,1)} %bitcast.38), calls=%async_computation.1 | async-start | bytes 2097152 | tf_op jit(solution)/shard_map/combine/all_to_all | solution.py:11
  90.6 0.5 broadcast.34
  91.1 0.7 reduce.7
  91.9 14.9 %all-to-all-done.1 = bf16[16,16,2048]{2,1,0:T(8,128)(2,1)S(1)} async-done(((bf16[16,16,2048]{2,1,0:T(8,128)(2,1)}), bf16[16,16,2048]{2,1,0:T(8,128)(2,1)S(1)}, u32[]{:S(2)}, u32[]{:S(2)}) %all-to-all-start.1) | async-done | bytes 1048608 | tf_op jit(solution)/shard_map/combine/all_to_all | solution.py:11
  107.3 0.5 convolution_add_fusion
  107.8 1.4 copy-done.4
  109.2 1.1 fusion.12
  110.3 20.8 %all_to_all.21 = bf16[16,16,2048]{2,1,0:T(8,128)(2,1)S(1)} all-to-all(bf16[16,16,2048]{2,1,0:T(8,128)(2,1)S(1)} %bitcast.36), channel_id=1, replica_groups=mesh['dp'=16,'expert'=16] {'expert'}, dimensions={0} | all-to-all | bytes 2097152 | tf_op jit(solution)/shard_map/combine/all_to_all | solution.py:11
  131.1 1.0 convolution_convert_fusion.1
  132.5 3.1 %multiply_convert_fusion.1 = (bf16[256,768]{1,0:T(8,128)(2,1)S(1)}, bf16[256,768]{1,0:T(8,128)(2,1)S(1)}) fusion(f32[256,1536]{1,0:T(8,128)S(1)} %copy-done.6, bf16[256,2048]{1,0:T(8,128)(2,1)S(1)} %bitcast.33, bf16[2048,2304]{1,0:T(8,128)(2,1)} %all-gather.2.cloned.1.call-done), kind=kOutput, calls=%fused_computation.22 | convolution fusion | flops 807862272 | bytes 6553600 | tf_op jit(solution)/shard_map/backward/dot_general | solution.py:15
  135.6 1.8 convolution_convert_fusion
  137.5 11.5 %pad_maximum_fusion = bf16[2048,2304]{0,1:T(8,128)(2,1)} fusion(bf16[2048,768]{0,1:T(8,128)(2,1)S(1)} %convolution_convert_fusion.1, bf16[2048,1536]{0,1:T(8,128)(2,1)S(1)} %convolution_convert_fusion), kind=kLoop, calls=%fused_computation | loop fusion | flops 18874368 | bytes 18874368 | tf_op jit(solution)/shard_map/weight_gradients/concatenate | solution.py:74
  149.0 12.7 %copy.18 = bf16[2048,2304]{1,0:T(8,128)(2,1)} copy(bf16[2048,2304]{0,1:T(8,128)(2,1)} %pad_maximum_fusion) | data formatting | bytes 18874368
  161.7 4.6 %fusion.9 = bf16[256,2048]{1,0:T(8,128)(2,1)S(1)} fusion(bf16[2048,2304]{1,0:T(8,128)(2,1)} %all-gather.2.cloned.1.call-done, bf16[256,768]{1,0:T(8,128)(2,1)S(1)} %get-tuple-element.15, bf16[256,768]{1,0:T(8,128)(2,1)S(1)} %get-tuple-element.14), kind=kOutput, calls=%fused_computation.15 | convolution fusion | flops 1612709888 | bytes 8126464 | tf_op jit(solution)/shard_map/token_gradient/dot_general | solution.py:15
  166.3 19.6 %all_to_all.22 = bf16[16,16,2048]{2,1,0:T(8,128)(2,1)S(1)} all-to-all(bf16[16,16,2048]{2,1,0:T(8,128)(2,1)S(1)} %bitcast.39), channel_id=1, replica_groups=mesh['dp'=16,'expert'=16] {'expert'}, dimensions={0} | all-to-all | bytes 2097152 | tf_op jit(solution)/shard_map/token_gradient/all_to_all | solution.py:11
  185.9 2.8 %convolution_convert_fusion.2 = bf16[768,2048]{1,0:T(8,128)(2,1)} fusion(bf16[256,2048]{1,0:T(8,128)(2,1)S(1)} %bitcast.37, s32[256]{0:T(256)S(1)} %eq.28), kind=kOutput, calls=%fused_computation.7 | convolution fusion | flops 807075840 | bytes 4195328 | tf_op jit(solution)/shard_map/token_gradient/dot_general | solution.py:15
  188.7 42.0 %reduce-scatter.4.cloned.1.call-done = bf16[128,2304]{1,0:T(8,128)(2,1)} async-done(((bf16[2048,2304]{1,0:T(8,128)(2,1)}), bf16[128,2304]{1,0:T(8,128)(2,1)}) %reduce-scatter.4.cloned.1.call-update) | async-done | bytes 589840
  230.6 2.3 copy.19
  232.9 1.1 convert_multiply_fusion
  234.1 1.0 slice_bitcast_fusion
  235.0 1.9 copy.17
  236.9 1.9 copy.16
  238.8 1.0 copy.15
  (26 shorter events, 1.5 us)
Async XLA Ops:
  7.2 5.0 %copy-start = (bf16[768,2048]{1,0:T(8,128)(2,1)S(1)}, bf16[768,2048]{1,0:T(8,128)(2,1)}, u32[]{:S(2)}) copy-start(bf16[768,2048]{1,0:T(8,128)(2,1)} %param.8) | copy-start | bytes 9437188
  7.2 67.1 %all-gather.2.cloned.1.call-start = ((), (), s32[]{:S(2)}) async-start(), calls=%async_computation.5 | async-start | bytes 10027008 | tf_op jit(solution)/shard_map/gather_weights/all_gather | solution.py:32
  36.3 42.6 %copy-start.2 = (bf16[16,16,2048]{2,1,0:T(8,128)(2,1)}, bf16[16,16,2048]{2,1,0:T(8,128)(2,1)S(1)}, u32[]{:S(2)}) copy-start(bf16[16,16,2048]{2,1,0:T(8,128)(2,1)S(1)} %all_to_all.20) | copy-start | bytes 3145732
  78.8 4.5 %copy-start.5 = (f32[256,1536]{1,0:T(8,128)}, f32[256,1536]{1,0:T(8,128)S(1)}, u32[]{:S(2)}) copy-start(f32[256,1536]{1,0:T(8,128)S(1)} %fusion.2) | copy-start | bytes 4718596
  79.1 12.1 %copy-start.7 = (f32[1,16,1,16]{3,2,1,0:T(1,128)S(1)}, f32[1,16,1,16]{3,2,1,0:T(1,128)}, u32[]{:S(2)}) copy-start(f32[1,16,1,16]{3,2,1,0:T(1,128)} %param.12) | copy-start | bytes 3076
  83.3 23.5 %all-to-all-start.1 = ((bf16[16,16,2048]{2,1,0:T(8,128)(2,1)}), bf16[16,16,2048]{2,1,0:T(8,128)(2,1)S(1)}, u32[]{:S(2)}, u32[]{:S(2)}) async-start(bf16[16,16,2048]{2,1,0:T(8,128)(2,1)} %bitcast.38), calls=%async_computation.1 | async-start | bytes 2097152 | tf_op jit(solution)/shard_map/combine/all_to_all | solution.py:11
  90.6 140.1 %reduce-scatter.4.cloned.1.call-start = ((), (), s32[]{:S(2)}) async-start(), calls=%async_computation.6 | async-start | bytes 10027008
  107.3 1.9 copy-start.4
  131.1 1.4 copy-start.6
  132.5 3.1 %copy-start.3 = (bf16[16,16,2048]{2,1,0:T(8,128)(2,1)S(1)}, bf16[16,16,2048]{2,1,0:T(8,128)(2,1)}, u32[]{:S(2)}) copy-start(bf16[16,16,2048]{2,1,0:T(8,128)(2,1)} %copy-done.2) | copy-start | bytes 3145732
  230.6 9.1 %copy-start.1 = (bf16[768,2048]{1,0:T(8,128)(2,1)S(1)}, bf16[768,2048]{1,0:T(8,128)(2,1)}, u32[]{:S(2)}) copy-start(bf16[768,2048]{1,0:T(8,128)(2,1)} %param.8) | copy-start | bytes 9437188
Sparse Core Ops, SparseCore 0:
  10.4 63.7 all-gather.1
  161.8 68.7 reduce-scatter.3
where the time goes:
time: 247 us
  waiting for transfers between devices  94.9 us (38%)
  blocking collectives  63.4 us (26%)
  matrix products  25.2 us (10%)
  local copies, waits for them, and re-layouts  23.8 us (10%)
  other arithmetic  17.8 us (7%)
  between operations  14.2 us (6%)
  starting transfers between devices  7.35 us (3%)
    all_to_all x3, blocking collectives, exchange(): lax.all_to_all(block, 'expert', split_axis=0, concat_axis=0, tiled=True)  63.4 us
    unnamed x3, waiting for transfers between devices  42 us
    all_gather x1, waiting for transfers between devices, on_device(): full = lax.all_gather(own, 'dp', axis=0, tiled=True)  38 us
    dot_general x11, matrix products, dot(): return lax.dot_general(a, b, (dims, ((), ())), preferred_element_type=F32)  25.2 us
    unnamed x23, local copies, waits for them, and re-layouts  22.6 us
    all_to_all x1, waiting for transfers between devices, exchange(): lax.all_to_all(block, 'expert', split_axis=0, concat_axis=0, tiled=True)  14.9 us
    concatenate x1, other arithmetic, on_device(): jnp.concatenate([dot(expert_rows, pre_grad, ((0,), (0,))).astype(BF16), d...  11.5 us
    all_to_all x1, starting transfers between devices, exchange(): lax.all_to_all(block, 'expert', split_axis=0, concat_axis=0, tiled=True)  7.27 us
  transfers between devices with their start and end apart: 3, of which 3 were waited for; matrix products, arithmetic and copies ran while one was open for 5% of the time, Pallas kernels for 0%

commit v1 on v0

v1 whole, which is shorter than its diff:
```python
import jax
import jax.numpy as jnp
from jax import lax
from jax.experimental import pallas as pl
from jax.experimental.pallas import tpu as pltpu
from jax.sharding import PartitionSpec as P

F32 = jnp.float32
BF16 = jnp.bfloat16
ROW_BY_ROW = ((1,), (0,))
OVER_LAST = ((1,), (1,))
OVER_FIRST = ((0,), (0,))
VMEM_LIMIT = 40 * 1024 * 1024


def exchange(block):
    return lax.all_to_all(block, "expert", split_axis=0, concat_axis=0, tiled=True)


def dot(a, b, dims):
    return lax.dot_general(a, b, (dims, ((), ())), preferred_element_type=F32)


def call(body, grid, in_specs, out_specs, out_shape, flops, moved, prefetch=0):
    return pl.pallas_call(
        body,
        grid_spec=pltpu.PrefetchScalarGridSpec(
            num_scalar_prefetch=prefetch, grid=grid, in_specs=in_specs, out_specs=out_specs
        ),
        out_shape=out_shape,
        compiler_params=pltpu.CompilerParams(vmem_limit_bytes=VMEM_LIMIT),
        cost_estimate=pl.CostEstimate(flops=flops, bytes_accessed=moved, transcendentals=0),
    )


def shape(rows, columns, dtype):
    return jax.ShapeDtypeStruct((rows, columns), dtype)


def project_in(rows, full, ff):
    slots, width = rows.shape
    wide = 256
    steps = ff // wide

    def body(x, wg, wu, gate_pre, up_pre, hidden):
        g = dot(x[...], wg[...], ROW_BY_ROW)
        u = dot(x[...], wu[...], ROW_BY_ROW)
        gate_pre[...] = g
        up_pre[...] = u
        hidden[...] = (g * jax.nn.sigmoid(g) * u).astype(BF16)

    part = pl.BlockSpec((slots, wide), lambda j: (0, j))
    return call(
        body,
        (steps,),
        [
            pl.BlockSpec((slots, width), lambda j: (0, 0)),
            pl.BlockSpec((width, wide), lambda j: (0, j)),
            pl.BlockSpec((width, wide), lambda j: (0, steps + j)),
        ],
        [part, part, part],
        [shape(slots, ff, F32), shape(slots, ff, F32), shape(slots, ff, BF16)],
        4 * slots * width * ff,
        4 * width * ff + 2 * slots * width + 10 * slots * ff,
    )(rows, full, full)


def project_out(hidden, full, ff):
    slots, width = hidden.shape[0], full.shape[0]
    tall = 512

    def body(h, wd, out):
        out[...] = dot(h[...], wd[...], OVER_LAST).astype(BF16)

    return call(
        body,
        (width // tall,),
        [
            pl.BlockSpec((slots, ff), lambda j: (0, 0)),
            pl.BlockSpec((tall, ff), lambda j: (j, 2)),
        ],
        pl.BlockSpec((slots, tall), lambda j: (0, j)),
        shape(slots, width, BF16),
        2 * slots * width * ff,
        2 * width * ff + 2 * slots * (width + ff),
    )(hidden, full)


def back_in(owner_grad, full, gate_pre, up_pre, ff):
    slots, width = owner_grad.shape
    wide = 256
    steps = ff // wide

    def body(x, wd, gate_ref, up_ref, gate_grad, up_grad):
        h = dot(x[...], wd[...], ROW_BY_ROW)
        g = gate_ref[...]
        sig = jax.nn.sigmoid(g)
        gate_grad[...] = (h * up_ref[...] * sig * (1.0 + g * (1.0 - sig))).astype(BF16)
        up_grad[...] = (h * (g * sig)).astype(BF16)

    part = pl.BlockSpec((slots, wide), lambda j: (0, j))
    return call(
        body,
        (steps,),
        [
            pl.BlockSpec((slots, width), lambda j: (0, 0)),
            pl.BlockSpec((width, wide), lambda j: (0, 2 * steps + j)),
            part,
            part,
        ],
        [part, part],
        [shape(slots, ff, BF16), shape(slots, ff, BF16)],
        2 * slots * width * ff,
        2 * width * ff + 2 * slots * width + 12 * slots * ff,
    )(owner_grad, full, gate_pre, up_pre)


def back_out(gate_grad, up_grad, full, ff):
    slots, width = gate_grad.shape[0], full.shape[0]
    tall = 512

    def body(g, u, wg, wu, out):
        out[...] = (
            dot(g[...], wg[...], OVER_LAST) + dot(u[...], wu[...], OVER_LAST)
        ).astype(BF16)

    return call(
        body,
        (width // tall,),
        [
            pl.BlockSpec((slots, ff), lambda j: (0, 0)),
            pl.BlockSpec((slots, ff), lambda j: (0, 0)),
            pl.BlockSpec((tall, ff), lambda j: (j, 0)),
            pl.BlockSpec((tall, ff), lambda j: (j, 1)),
        ],
        pl.BlockSpec((slots, tall), lambda j: (0, j)),
        shape(slots, width, BF16),
        4 * slots * width * ff,
        4 * width * ff + 2 * slots * (width + 2 * ff),
    )(gate_grad, up_grad, full, full)


def chip_gradient(blocks, own, other, dtype):
    count = blocks.shape[0]
    slots, ff = own[1].shape
    tall = 128

    def body(names, xa, ga, ua, oa, ha, xb, gb, ub, ob, hb, out):
        xa, xb, oa, ob = xa[...], xb[...], oa[...], ob[...]
        gate = dot(xa, ga[...], OVER_FIRST) + dot(xb, gb[...], OVER_FIRST)
        up = dot(xa, ua[...], OVER_FIRST) + dot(xb, ub[...], OVER_FIRST)
        down = dot(oa, ha[...], OVER_FIRST) + dot(ob, hb[...], OVER_FIRST)
        out[0, :, :ff] = gate.astype(dtype)
        out[0, :, ff : 2 * ff] = up.astype(dtype)
        out[0, :, 2 * ff :] = down.astype(dtype)

    column = pl.BlockSpec((slots, tall), lambda i, names: (0, names[i]))
    whole = pl.BlockSpec((slots, ff), lambda i, names: (0, 0))
    return call(
        body,
        (count,),
        [column, whole, whole, column, whole] * 2,
        pl.BlockSpec((1, tall, 3 * ff), lambda i, names: (i, 0, 0)),
        jax.ShapeDtypeStruct((count, tall, 3 * ff), dtype),
        12 * count * slots * tall * ff,
        12 * slots * ff + count * (8 * slots * tall + 12 * tall * ff),
        prefetch=1,
    )(blocks, *own, *other)


def last_sum(first, second, mine, ff, factor):
    tall = mine.shape[0]

    def body(a, b, c, gate, up, down):
        s = (a[...].astype(F32) + b[...].astype(F32) + c[...]) * factor
        gate[...] = s[:, :ff]
        up[...] = s[:, ff : 2 * ff]
        down[...] = s[:, 2 * ff :]

    block = pl.BlockSpec((tall, 3 * ff), lambda i: (0, 0))
    part = pl.BlockSpec((tall, ff), lambda i: (0, 0))
    return call(
        body, (1,), [block] * 3, [part] * 3, [shape(tall, ff, F32)] * 3, 12 * tall * ff, 36 * tall * ff
    )(first, second, mine)


def on_device(
    tokens, target, route_index, route_count, route_gate, gate_weight, up_weight, down_weight
):
    groups = lax.axis_size("dp")
    sources = lax.axis_size("expert")
    chips = groups // 2
    local_index = route_index[0, :, 0, :]
    live_count = route_count[0, :, 0]
    per_source = local_index.shape[1]
    held, width = tokens.shape
    tall = gate_weight.shape[0]
    ff = gate_weight.shape[2]
    slots = sources * per_source

    def along(array, by):
        pairs = [
            (2 * z + c, 2 * ((z + by) % chips) + c) for z in range(chips) for c in range(2)
        ]
        return lax.ppermute(array, "dp", pairs)

    def other_core(array):
        return lax.ppermute(array, "dp", [(d, d ^ 1) for d in range(groups)])

    with jax.named_scope("gather_weights"):
        own = jnp.concatenate([gate_weight[:, 0], up_weight[:, 0], down_weight[:, 0]], axis=1)
        full = lax.all_gather(own, "dp", axis=0, tiled=True)

    with jax.named_scope("routing"):
        usable = jnp.arange(per_source, dtype=jnp.int32)[None, :] < live_count[:, None]
        flat_index = local_index.reshape(slots)
        live = usable.reshape(slots)
        weight = jnp.where(live, route_gate[0, :, 0, :].reshape(slots), 0.0)
        names = flat_index[:, None] == jnp.arange(held, dtype=jnp.int32)[None, :]
        pick = (names & live[:, None]).astype(BF16)
        same = flat_index[:, None] == flat_index[None, :]
        high = lax.reduce_precision(weight, 8, 7)
        low = weight - high
        mix_high = jnp.where(same, high[None, :], 0.0).astype(BF16)
        mix_low = jnp.where(same, low[None, :], 0.0).astype(BF16)

    with jax.named_scope("rows_out"):
        rows = dot(pick, tokens, ROW_BY_ROW).astype(BF16)
        expert_rows = exchange(rows.reshape(sources, per_source, width)).reshape(slots, width)
        other_rows = other_core(expert_rows)
        wanted = dot(pick, target, ROW_BY_ROW)

    with jax.named_scope("forward"):
        gate_pre, up_pre, hidden = project_in(expert_rows, full, ff)
        expert_out = project_out(hidden, full, ff)
        other_hidden = other_core(hidden)

    with jax.named_scope("combine"):
        returned = exchange(expert_out.reshape(sources, per_source, width)).reshape(slots, width)
        combined = dot(mix_high, returned, ROW_BY_ROW) + dot(mix_low, returned, ROW_BY_ROW)
        slot_grad = (weight[:, None] * (combined - wanted)).astype(BF16)
        owner_grad = exchange(slot_grad.reshape(sources, per_source, width)).reshape(slots, width)
        other_grad = other_core(owner_grad)

    with jax.named_scope("backward"):
        gate_grad, up_grad = back_in(owner_grad, full, gate_pre, up_pre, ff)
        other_gate, other_up = other_core(gate_grad), other_core(up_grad)

    with jax.named_scope("weight_gradients"):
        place = lax.axis_index("dp")
        z, core = place // 2, place % 2
        mine = (expert_rows, gate_grad, up_grad, owner_grad, hidden)
        theirs = (other_rows, other_gate, other_up, other_grad, other_hidden)

        def terms(steps, dtype=F32):
            blocks = jnp.stack([((z + s) % chips) * 2 + core for s in steps]).astype(jnp.int32)
            return chip_gradient(blocks, mine, theirs, dtype)

        half = tall // 2
        far = chips // 2
        farthest = terms([far], BF16)[0]
        ahead, behind = along(farthest[:half], 1), along(farthest[half:], -1)
        for step in range(far - 1, 0, -1):
            both = terms([step, chips - step])
            if step == far - 1:
                first = jnp.concatenate([both[0, :half] + ahead.astype(F32), both[0, half:]], axis=0)
                second = jnp.concatenate([both[1, :half], both[1, half:] + behind.astype(F32)], axis=0)
            else:
                first, second = both[0] + ahead.astype(F32), both[1] + behind.astype(F32)
            ahead, behind = along(first.astype(BF16), 1), along(second.astype(BF16), -1)
        factor = (groups * sources * per_source) ** (-0.5)
        gradients = last_sum(ahead, behind, terms([0])[0], ff, factor)

    with jax.named_scope("token_gradient"):
        row_grad = back_out(gate_grad, up_grad, full, ff)
        came_back = exchange(row_grad.reshape(sources, per_source, width)).reshape(slots, width)
        token_grad = dot(names.astype(BF16), came_back, OVER_FIRST).astype(BF16)

    return (token_grad, *(g[:, None, :] for g in gradients))


def solution(mesh):
    return jax.shard_map(
        on_device,
        mesh=mesh,
        in_specs=(
            P(("dp", "expert"), None),
            P(("dp", "expert"), None),
            P("dp", None, "expert", None),
            P("dp", None, "expert"),
            P("dp", None, "expert", None),
            P("dp", "expert", None),
            P("dp", "expert", None),
            P("dp", "expert", None),
        ),
        out_specs=(
            P(("dp", "expert"), None),
            P("dp", "expert", None),
            P("dp", "expert", None),
            P("dp", "expert", None),
        ),
        check_vma=False,
    )
```

time: 247 us -> 241 us (0.976)
  blocking collectives: 63.4 us -> 23.2 us
  Pallas kernels: 0 us -> 27.7 us
  starting transfers between devices: 7.35 us -> 32.2 us
  matrix products: 25.2 us -> 10.8 us
  waiting for transfers between devices: 94.9 us -> 88.6 us
  local copies, waits for them, and re-layouts: 23.8 us -> 30.1 us
  other arithmetic: 17.8 us -> 13.4 us
    unnamed x3 -> x1, waiting for transfers between devices: 42 us -> 0.02 us
    all_to_all x3 -> x1, blocking collectives: 63.4 us -> 23.2 us  [exchange(): lax.all_to_all(block, 'expert', split_axis=0, concat_axis=0, tiled=True)]
    pallas_call x0 -> x10, Pallas kernels: none -> 27.7 us  [the longest x5 14 us: chip_gradient(): call(body, (count,), [column, whole, whole, column, whole] * 2, pl.BlockS...]
    ppermute x0 -> x13, waiting for transfers between devices: none -> 18.2 us  [the longest x8 16.2 us: along(): return lax.ppermute(array, 'dp', pairs)]
    all_to_all x1 -> x3, waiting for transfers between devices: 14.9 us -> 32.4 us  [exchange(): lax.all_to_all(block, 'expert', split_axis=0, concat_axis=0, tiled=True)]
    dot_general x11 -> x5, matrix products: 25.2 us -> 10.8 us  [dot(): return lax.dot_general(a, b, (dims, ((), ())), preferred_element_type=F32)]
    ppermute x0 -> x13, starting transfers between devices: none -> 13.3 us  [the longest x8 12.3 us: along(): return lax.ppermute(array, 'dp', pairs)]
    all_to_all x1 -> x3, starting transfers between devices: 7.27 us -> 18.9 us  [exchange(): lax.all_to_all(block, 'expert', split_axis=0, concat_axis=0, tiled=True)]
  transfers between devices with their start and end apart: 3 -> 17, of which waited for: 3 -> 11; matrix products, arithmetic and copies ran while one was open for 5% -> 6% of each run, Pallas kernels for 0% -> 8%
where the time goes in v1:
time: 241 us; the launch traced here: 240 us
  waiting for transfers between devices  88.6 us (37%)
  starting transfers between devices  32.2 us (13%)
  local copies, waits for them, and re-layouts  30.1 us (12%)
  Pallas kernels  27.7 us (11%)
  blocking collectives  23.2 us (10%)
  between operations  14.3 us (6%)
  other arithmetic  13.4 us (6%)
  matrix products  10.8 us (4%)
    all_gather x1, waiting for transfers between devices, on_device(): full = lax.all_gather(own, 'dp', axis=0, tiled=True)  37.9 us
    all_to_all x3, waiting for transfers between devices, exchange(): lax.all_to_all(block, 'expert', split_axis=0, concat_axis=0, tiled=True)  32.4 us
    unnamed x45, local copies, waits for them, and re-layouts  29.2 us
    all_to_all x1, blocking collectives, exchange(): lax.all_to_all(block, 'expert', split_axis=0, concat_axis=0, tiled=True)  23.2 us
    all_to_all x3, starting transfers between devices, exchange(): lax.all_to_all(block, 'expert', split_axis=0, concat_axis=0, tiled=True)  18.9 us
    ppermute x8, waiting for transfers between devices, along(): return lax.ppermute(array, 'dp', pairs)  16.2 us
    pallas_call x5, Pallas kernels, chip_gradient(): call(body, (count,), [column, whole, whole, column, whole] * 2, pl.BlockS...  14 us
    ppermute x8, starting transfers between devices, along(): return lax.ppermute(array, 'dp', pairs)  12.3 us
  transfers between devices with their start and end apart: 17, of which 11 were waited for; matrix products, arithmetic and copies ran while one was open for 6% of the time, Pallas kernels for 8%

profile of v1, /device:TPU:2, one launch (start us, length us, event | category | flops | bytes accessed | tf_op | source)
XLA Modules:
  0.0 240.2 jit_solution(3059797407079527595)
XLA Ops:
  7.2 2.1 pad_maximum_fusion
  13.2 23.2 %all_to_all.20 = bf16[16,16,2048]{2,1,0:T(8,128)(2,1)} all-to-all(bf16[16,16,2048]{2,1,0:T(8,128)(2,1)S(1)} %bitcast.87), channel_id=1, replica_groups=mesh['dp'=16,'expert'=16] {'expert'}, dimensions={0} | all-to-all | bytes 2097152 | tf_op jit(solution)/shard_map/rows_out/all_to_all | solution.py:17
  36.4 37.9 %all-gather.2.cloned.1.call-done.wg.wu.wd = bf16[2048,2304]{1,0:T(8,128)(2,1)} async-done(((bf16[128,2304]{1,0:T(8,128)(2,1)}), bf16[2048,2304]{1,0:T(8,128)(2,1)}) %all-gather.2.cloned.1.call-update) | async-done | bytes 9437200 | tf_op jit(solution)/shard_map/gather_weights/all_gather | solution.py:212
  74.3 3.7 %copy-done.1 = bf16[2048,2304]{1,0:T(8,128)(2,1)S(1)} copy-done((bf16[2048,2304]{1,0:T(8,128)(2,1)S(1)}, bf16[2048,2304]{1,0:T(8,128)(2,1)}, u32[]{:S(2)}) %copy-start.1) | copy-done | bytes 9437208
  79.2 2.7 %forward.2 = (f32[256,768]{1,0:T(8,128)S(1)}, f32[256,768]{1,0:T(8,128)S(1)}, bf16[256,768]{1,0:T(8,128)(2,1)S(1)}) custom-call(bf16[256,2048]{1,0:T(8,128)(2,1)S(1)} %bitcast.74, bf16[2048,2304]{1,0:T(8,128)(2,1)S(1)} %copy-done.1, bf16[2048,2304]{1,0:T(8,128)(2,1)S(1)} %copy-done.1), custom_call_target="tpu_custom_call" | custom-call | flops 1610612736 | bytes 9306112 | tf_op jit(solution)/shard_map/forward/pallas_call | solution.py:53
  81.9 4.2 %copy-done.2 = bf16[2048,2304]{1,0:T(8,128)(2,1)S(1)} copy-done((bf16[2048,2304]{1,0:T(8,128)(2,1)S(1)}, bf16[2048,2304]{1,0:T(8,128)(2,1)}, u32[]{:S(2)}) %copy-start.2) | copy-done | bytes 9437208
  89.1 7.3 %all-to-all-start.1 = ((bf16[16,16,2048]{2,1,0:T(8,128)(2,1)}), bf16[16,16,2048]{2,1,0:T(8,128)(2,1)}, u32[]{:S(2)}, u32[]{:S(2)}) async-start(bf16[16,16,2048]{2,1,0:T(8,128)(2,1)} %bitcast.82), calls=%async_computation.1 | async-start | bytes 2097152 | tf_op jit(solution)/shard_map/combine/all_to_all | solution.py:17
  99.6 13.1 %all-to-all-done.1 = bf16[16,16,2048]{2,1,0:T(8,128)(2,1)} async-done(((bf16[16,16,2048]{2,1,0:T(8,128)(2,1)}), bf16[16,16,2048]{2,1,0:T(8,128)(2,1)}, u32[]{:S(2)}, u32[]{:S(2)}) %all-to-all-start.1) | async-done | bytes 1048608 | tf_op jit(solution)/shard_map/combine/all_to_all | solution.py:17
  116.6 2.1 fusion.1
  118.7 5.8 %all-to-all-start.2 = ((bf16[16,16,2048]{2,1,0:T(8,128)(2,1)}), bf16[16,16,2048]{2,1,0:T(8,128)(2,1)}, u32[]{:S(2)}, u32[]{:S(2)}) async-start(bf16[16,16,2048]{2,1,0:T(8,128)(2,1)} %bitcast.86), calls=%async_computation.2 | async-start | bytes 2097152 | tf_op jit(solution)/shard_map/combine/all_to_all | solution.py:17
  124.5 15.2 %all-to-all-done.2 = bf16[16,16,2048]{2,1,0:T(8,128)(2,1)} async-done(((bf16[16,16,2048]{2,1,0:T(8,128)(2,1)}), bf16[16,16,2048]{2,1,0:T(8,128)(2,1)}, u32[]{:S(2)}, u32[]{:S(2)}) %all-to-all-start.2) | async-done | bytes 1048608 | tf_op jit(solution)/shard_map/combine/all_to_all | solution.py:17
  140.3 3.7 %copy-done.3 = bf16[2048,2304]{1,0:T(8,128)(2,1)S(1)} copy-done((bf16[2048,2304]{1,0:T(8,128)(2,1)S(1)}, bf16[2048,2304]{1,0:T(8,128)(2,1)}, u32[]{:S(2)}) %copy-start.3) | copy-done | bytes 9437208
  146.2 3.7 %backward.1 = (bf16[256,768]{1,0:T(8,128)(2,1)}, bf16[256,768]{1,0:T(8,128)(2,1)}) custom-call(bf16[256,2048]{1,0:T(8,128)(2,1)} %bitcast.9.x.oa, bf16[2048,2304]{1,0:T(8,128)(2,1)S(1)} %copy-done.3, f32[256,768]{1,0:T(8,128)S(1)} %copy-done.14, f32[256,768]{1,0:T(8,128)S(1)} %copy-done.16), custom_call_target="tpu_custom_call" | custom-call | flops 805306368 | bytes 6553600 | tf_op jit(solution)/shard_map/backward/pallas_call | solution.py:102
  153.7 2.1 weight_gradients.9
  158.0 3.3 %weight_gradients.8 = f32[2,128,2304]{2,1,0:T(8,128)S(1)} custom-call(s32[2]{0:T(128)S(1)} %pad_add_fusion.2.names, bf16[256,2048]{1,0:T(8,128)(2,1)S(1)} %bitcast.76, bf16[256,768]{1,0:T(8,128)(2,1)} %get-tuple-element.15.g.ga, bf16[256,768]{1,0:T(8,128)(2,1)} %get-tuple-element.16.u.ua, bf16[256,2048]{1,0:T(8,128)(2,1)} %bitcast.9.x.oa, ...), custom_call_target="tpu_custom_call" | custom-call | flops 603979776 | bytes 5242880 | tf_op jit(solution)/shard_map/weight_gradients/pallas_call | solution.py:159
  161.5 3.5 %collective-permute-done.9 = bf16[64,2304]{1,0:T(8,128)(2,1)S(1)} collective-permute-done((bf16[64,2304]{1,0:T(8,128)(2,1)S(1)}, bf16[64,2304]{1,0:T(8,128)(2,1)S(1)}, u32[]{:S(2)}, u32[]{:S(2)}) %collective-permute-start.9) | collective-permute-done | bytes 294944 | tf_op jit(solution)/shard_map/weight_gradients/ppermute | solution.py:205
  165.1 2.3 collective-permute-done.5
  169.2 3.2 %collective-permute-start.10 = (bf16[128,2304]{1,0:T(8,128)(2,1)}, bf16[128,2304]{1,0:T(8,128)(2,1)}, u32[]{:S(2)}, u32[]{:S(2)}) collective-permute-start(bf16[128,2304]{1,0:T(8,128)(2,1)} %pad_maximum_fusion.2), channel_id=1, source_target_pairs={{0,224},{16,240},{32,0},{48,16},{64,32},{80,48},{96,64},{112,80},{... | collective-permute-start | bytes 1769480 | tf_op jit(solution)/shard_map/weight_gradients/ppermute | solution.py:205
  173.7 3.3 %weight_gradients.7 = f32[2,128,2304]{2,1,0:T(8,128)S(1)} custom-call(s32[2]{0:T(128)S(1)} %pad_add_fusion.1.names, bf16[256,2048]{1,0:T(8,128)(2,1)S(1)} %bitcast.77, bf16[256,768]{1,0:T(8,128)(2,1)} %get-tuple-element.15.g.ga, bf16[256,768]{1,0:T(8,128)(2,1)} %get-tuple-element.16.u.ua, bf16[256,2048]{1,0:T(8,128)(2,1)} %bitcast.9.x.oa, ...), custom_call_target="tpu_custom_call" | custom-call | flops 603979776 | bytes 5242880 | tf_op jit(solution)/shard_map/weight_gradients/pallas_call | solution.py:159
  177.0 7.0 %collective-permute-done.6 = bf16[128,2304]{1,0:T(8,128)(2,1)} collective-permute-done((bf16[128,2304]{1,0:T(8,128)(2,1)}, bf16[128,2304]{1,0:T(8,128)(2,1)}, u32[]{:S(2)}, u32[]{:S(2)}) %collective-permute-start.6) | collective-permute-done | bytes 589856 | tf_op jit(solution)/shard_map/weight_gradients/ppermute | solution.py:205
  184.2 2.5 %fusion.3 = (bf16[128,2304]{1,0:T(8,128)(2,1)}, bf16[128,2304]{1,0:T(8,128)(2,1)}) fusion(f32[2,128,2304]{2,1,0:T(8,128)S(1)} %weight_gradients.7, bf16[128,2304]{1,0:T(8,128)(2,1)} %collective-permute-done.10, bf16[128,2304]{1,0:T(8,128)(2,1)} %collective-permute-done.6), kind=kLoop, calls=%fused_computation.8 | loop fusion | flops 1769472 | bytes 4718592 | tf_op jit(solution)/shard_map/weight_gradients/convert_element_type | solution.py:270
  186.6 3.7 %collective-permute-start.11 = (bf16[128,2304]{1,0:T(8,128)(2,1)}, bf16[128,2304]{1,0:T(8,128)(2,1)}, u32[]{:S(2)}, u32[]{:S(2)}) collective-permute-start(bf16[128,2304]{1,0:T(8,128)(2,1)} %get-tuple-element.28), channel_id=1, source_target_pairs={{0,224},{16,240},{32,0},{48,16},{64,32},{80,48},{96,64},{112,80},{... | collective-permute-start | bytes 1769480 | tf_op jit(solution)/shard_map/weight_gradients/ppermute | solution.py:205
  190.4 3.7 %copy-done.4 = bf16[2048,2304]{1,0:T(8,128)(2,1)S(1)} copy-done((bf16[2048,2304]{1,0:T(8,128)(2,1)S(1)}, bf16[2048,2304]{1,0:T(8,128)(2,1)}, u32[]{:S(2)}) %copy-start.4) | copy-done | bytes 9437208
  194.1 3.9 %token_gradient.1 = bf16[256,2048]{1,0:T(8,128)(2,1)S(1)} custom-call(bf16[256,768]{1,0:T(8,128)(2,1)} %get-tuple-element.15.g.ga, bf16[256,768]{1,0:T(8,128)(2,1)} %get-tuple-element.16.u.ua, bf16[2048,2304]{1,0:T(8,128)(2,1)S(1)} %copy-done.4, bf16[2048,2304]{1,0:T(8,128)(2,1)S(1)} %copy-done.4), custom_call_target="tpu_custom_call" | custom-call | flops 1610612736 | bytes 8126464 | tf_op jit(solution)/shard_map/token_gradient/pallas_call | solution.py:127
  199.0 5.8 %all-to-all-start.3 = ((bf16[16,16,2048]{2,1,0:T(8,128)(2,1)}), bf16[16,16,2048]{2,1,0:T(8,128)(2,1)}, u32[]{:S(2)}, u32[]{:S(2)}) async-start(bf16[16,16,2048]{2,1,0:T(8,128)(2,1)} %bitcast.81), calls=%async_computation.3 | async-start | bytes 2097152 | tf_op jit(solution)/shard_map/token_gradient/all_to_all | solution.py:17
  206.0 3.3 %weight_gradients.6 = f32[2,128,2304]{2,1,0:T(8,128)S(1)} custom-call(s32[2]{0:T(128)S(1)} %pad_add_fusion.names, bf16[256,2048]{1,0:T(8,128)(2,1)S(1)} %bitcast.78, bf16[256,768]{1,0:T(8,128)(2,1)} %get-tuple-element.15.g.ga, bf16[256,768]{1,0:T(8,128)(2,1)} %get-tuple-element.16.u.ua, bf16[256,2048]{1,0:T(8,128)(2,1)} %bitcast.9.x.oa, ...), custom_call_target="tpu_custom_call" | custom-call | flops 603979776 | bytes 5242880 | tf_op jit(solution)/shard_map/weight_gradients/pallas_call | solution.py:159
  209.3 2.5 %fusion.5 = (bf16[128,2304]{1,0:T(8,128)(2,1)}, bf16[128,2304]{1,0:T(8,128)(2,1)}) fusion(f32[2,128,2304]{2,1,0:T(8,128)S(1)} %weight_gradients.6, bf16[128,2304]{1,0:T(8,128)(2,1)} %collective-permute-done.11, bf16[128,2304]{1,0:T(8,128)(2,1)} %collective-permute-done.7), kind=kLoop, calls=%fused_computation.11 | loop fusion | flops 1769472 | bytes 4718592 | tf_op jit(solution)/shard_map/weight_gradients/convert_element_type | solution.py:270
  211.8 3.2 %collective-permute-start.12 = (bf16[128,2304]{1,0:T(8,128)(2,1)}, bf16[128,2304]{1,0:T(8,128)(2,1)}, u32[]{:S(2)}, u32[]{:S(2)}) collective-permute-start(bf16[128,2304]{1,0:T(8,128)(2,1)} %get-tuple-element.26), channel_id=1, source_target_pairs={{0,224},{16,240},{32,0},{48,16},{64,32},{80,48},{96,64},{112,80},{... | collective-permute-start | bytes 1769480 | tf_op jit(solution)/shard_map/weight_gradients/ppermute | solution.py:205
  215.0 4.1 %all-to-all-done.3 = bf16[16,16,2048]{2,1,0:T(8,128)(2,1)} async-done(((bf16[16,16,2048]{2,1,0:T(8,128)(2,1)}), bf16[16,16,2048]{2,1,0:T(8,128)(2,1)}, u32[]{:S(2)}, u32[]{:S(2)}) %all-to-all-start.3) | async-done | bytes 1048608 | tf_op jit(solution)/shard_map/token_gradient/all_to_all | solution.py:17
  219.1 4.1 %convolution_convert_fusion = bf16[768,2048]{1,0:T(8,128)(2,1)} fusion(bf16[256,2048]{1,0:T(8,128)(2,1)} %bitcast.11, s32[256]{0:T(256)S(1)} %eq.38), kind=kOutput, calls=%fused_computation | convolution fusion | flops 807075840 | bytes 4195328 | tf_op jit(solution)/shard_map/token_gradient/dot_general | solution.py:21
  223.2 2.0 weight_gradients.10
  225.3 3.2 %collective-permute-done.8.a = bf16[128,2304]{1,0:T(8,128)(2,1)} collective-permute-done((bf16[128,2304]{1,0:T(8,128)(2,1)}, bf16[128,2304]{1,0:T(8,128)(2,1)}, u32[]{:S(2)}, u32[]{:S(2)}) %collective-permute-start.8) | collective-permute-done | bytes 589856 | tf_op jit(solution)/shard_map/weight_gradients/ppermute | solution.py:205
  (84 shorter events, 34.4 us)
Async XLA Ops:
  7.2 5.0 %copy-start = (bf16[768,2048]{1,0:T(8,128)(2,1)S(1)}, bf16[768,2048]{1,0:T(8,128)(2,1)}, u32[]{:S(2)}) copy-start(bf16[768,2048]{1,0:T(8,128)(2,1)} %param.8) | copy-start | bytes 9437188
  7.2 67.1 %all-gather.2.cloned.1.call-start = ((), (), s32[]{:S(2)}) async-start(), calls=%async_computation.4 | async-start | bytes 10027008 | tf_op jit(solution)/shard_map/gather_weights/all_gather | solution.py:212
  10.2 3.0 %copy-start.18 = (pred[256]{0:T(512)(128)(4,1)}, pred[256]{0:T(512)(128)(4,1)S(1)}, u32[]{:S(2)}) copy-start(pred[256]{0:T(512)(128)(4,1)S(1)} %lt.75) | copy-start | bytes 772
  74.2 3.7 %copy-start.1 = (bf16[2048,2304]{1,0:T(8,128)(2,1)S(1)}, bf16[2048,2304]{1,0:T(8,128)(2,1)}, u32[]{:S(2)}) copy-start(bf16[2048,2304]{1,0:T(8,128)(2,1)} %all-gather.2.cloned.1.call-done.wg.wu.wd) | copy-start | bytes 28311556
  77.9 1.2 copy-start.5
  81.9 6.2 %copy-start.13 = (f32[256,768]{1,0:T(8,128)}, f32[256,768]{1,0:T(8,128)S(1)}, u32[]{:S(2)}) copy-start(f32[256,768]{1,0:T(8,128)S(1)} %get-tuple-element.13.gate_ref) | copy-start | bytes 2359300
  81.9 6.2 %copy-start.15 = (f32[256,768]{1,0:T(8,128)}, f32[256,768]{1,0:T(8,128)S(1)}, u32[]{:S(2)}) copy-start(f32[256,768]{1,0:T(8,128)S(1)} %get-tuple-element.14.up_ref) | copy-start | bytes 2359300
  81.9 4.2 %copy-start.2 = (bf16[2048,2304]{1,0:T(8,128)(2,1)S(1)}, bf16[2048,2304]{1,0:T(8,128)(2,1)}, u32[]{:S(2)}) copy-start(bf16[2048,2304]{1,0:T(8,128)(2,1)} %all-gather.2.cloned.1.call-done.wg.wu.wd) | copy-start | bytes 28311556
  89.1 23.6 %all-to-all-start.1 = ((bf16[16,16,2048]{2,1,0:T(8,128)(2,1)}), bf16[16,16,2048]{2,1,0:T(8,128)(2,1)}, u32[]{:S(2)}, u32[]{:S(2)}) async-start(bf16[16,16,2048]{2,1,0:T(8,128)(2,1)} %bitcast.82), calls=%async_computation.1 | async-start | bytes 2097152 | tf_op jit(solution)/shard_map/combine/all_to_all | solution.py:17
  114.4 2.2 copy-start.17
  114.4 2.2 copy-start.19
  118.7 21.1 %all-to-all-start.2 = ((bf16[16,16,2048]{2,1,0:T(8,128)(2,1)}), bf16[16,16,2048]{2,1,0:T(8,128)(2,1)}, u32[]{:S(2)}, u32[]{:S(2)}) async-start(bf16[16,16,2048]{2,1,0:T(8,128)(2,1)} %bitcast.86), calls=%async_computation.2 | async-start | bytes 2097152 | tf_op jit(solution)/shard_map/combine/all_to_all | solution.py:17
  124.5 26.0 %collective-permute-start = (bf16[256,2048]{1,0:T(8,128)(2,1)}, bf16[256,2048]{1,0:T(8,128)(2,1)}, u32[]{:S(2)}, u32[]{:S(2)}) collective-permute-start(bf16[256,2048]{1,0:T(8,128)(2,1)} %bitcast.73), channel_id=1, source_target_pairs={{0,16},{16,0},{32,48},{48,32},{64,80},{80,64},{96,112},{112,96},{1... | collective-permute-start | bytes 3145736 | tf_op jit(solution)/shard_map/rows_out/ppermute | solution.py:208
  139.8 12.8 %collective-permute-start.3 = (bf16[256,2048]{1,0:T(8,128)(2,1)}, bf16[256,2048]{1,0:T(8,128)(2,1)}, u32[]{:S(2)}, u32[]{:S(2)}) collective-permute-start(bf16[256,2048]{1,0:T(8,128)(2,1)} %bitcast.9.x.oa), channel_id=1, source_target_pairs={{0,16},{16,0},{32,48},{48,32},{64,80},{80,64},{96,112},{112,96},{1... | collective-permute-start | bytes 3145736 | tf_op jit(solution)/shard_map/combine/ppermute | solution.py:208
  139.8 10.7 %collective-permute-start.4 = (bf16[256,768]{1,0:T(8,128)(2,1)S(1)}, bf16[256,768]{1,0:T(8,128)(2,1)}, u32[]{:S(2)}, u32[]{:S(2)}) collective-permute-start(bf16[256,768]{1,0:T(8,128)(2,1)S(1)} %get-tuple-element.12.h.ha), channel_id=1, source_target_pairs={{0,16},{16,0},{32,48},{48,32},{64,80},{80,64},{96,112},{112,96},{1... | collective-permute-start | bytes 1179656 | tf_op jit(solution)/shard_map/forward/ppermute | solution.py:208
  140.3 3.7 %copy-start.3 = (bf16[2048,2304]{1,0:T(8,128)(2,1)S(1)}, bf16[2048,2304]{1,0:T(8,128)(2,1)}, u32[]{:S(2)}) copy-start(bf16[2048,2304]{1,0:T(8,128)(2,1)} %all-gather.2.cloned.1.call-done.wg.wu.wd) | copy-start | bytes 28311556
  149.9 2.1 collective-permute-start.1
  149.9 2.6 %collective-permute-start.2 = (bf16[256,768]{1,0:T(8,128)(2,1)}, bf16[256,768]{1,0:T(8,128)(2,1)}, u32[]{:S(2)}, u32[]{:S(2)}) collective-permute-start(bf16[256,768]{1,0:T(8,128)(2,1)} %get-tuple-element.16.u.ua), channel_id=1, source_target_pairs={{0,16},{16,0},{32,48},{48,32},{64,80},{80,64},{96,112},{112,96},{1... | collective-permute-start | bytes 1179656 | tf_op jit(solution)/shard_map/backward/ppermute | solution.py:208
  152.5 1.2 copy-start.6
  153.7 4.3 %copy-start.7 = (bf16[16,16,2048]{2,1,0:T(8,128)(2,1)S(1)}, bf16[16,16,2048]{2,1,0:T(8,128)(2,1)}, u32[]{:S(2)}) copy-start(bf16[16,16,2048]{2,1,0:T(8,128)(2,1)} %all_to_all.20) | copy-start | bytes 3145732
  155.9 9.1 %collective-permute-start.9 = (bf16[64,2304]{1,0:T(8,128)(2,1)S(1)}, bf16[64,2304]{1,0:T(8,128)(2,1)S(1)}, u32[]{:S(2)}, u32[]{:S(2)}) collective-permute-start(bf16[64,2304]{1,0:T(8,128)(2,1)S(1)} %get-tuple-element.34), channel_id=1, source_target_pairs={{0,224},{16,240},{32,0},{48,16},{64,32},{80,48},{96,64},{112,80},{... | collective-permute-start | bytes 884744 | tf_op jit(solution)/shard_map/weight_gradients/ppermute | solution.py:205
  157.4 10.0 %collective-permute-start.5 = (bf16[64,2304]{1,0:T(8,128)(2,1)S(1)}, bf16[64,2304]{1,0:T(8,128)(2,1)S(1)}, u32[]{:S(2)}, u32[]{:S(2)}) collective-permute-start(bf16[64,2304]{1,0:T(8,128)(2,1)S(1)} %get-tuple-element.35), channel_id=1, source_target_pairs={{0,32},{16,48},{32,64},{48,80},{64,96},{80,112},{96,128},{112,144}... | collective-permute-start | bytes 884744 | tf_op jit(solution)/shard_map/weight_gradients/ppermute | solution.py:205
  168.3 15.7 %collective-permute-start.6 = (bf16[128,2304]{1,0:T(8,128)(2,1)}, bf16[128,2304]{1,0:T(8,128)(2,1)}, u32[]{:S(2)}, u32[]{:S(2)}) collective-permute-start(bf16[128,2304]{1,0:T(8,128)(2,1)} %pad_maximum_fusion.1), channel_id=1, source_target_pairs={{0,32},{16,48},{32,64},{48,80},{64,96},{80,112},{96,128},{112,144}... | collective-permute-start | bytes 1769480 | tf_op jit(solution)/shard_map/weight_gradients/ppermute | solution.py:205
  169.2 15.0 %collective-permute-start.10 = (bf16[128,2304]{1,0:T(8,128)(2,1)}, bf16[128,2304]{1,0:T(8,128)(2,1)}, u32[]{:S(2)}, u32[]{:S(2)}) collective-permute-start(bf16[128,2304]{1,0:T(8,128)(2,1)} %pad_maximum_fusion.2), channel_id=1, source_target_pairs={{0,224},{16,240},{32,0},{48,16},{64,32},{80,48},{96,64},{112,80},{... | collective-permute-start | bytes 1769480 | tf_op jit(solution)/shard_map/weight_gradients/ppermute | solution.py:205
  172.5 1.2 copy-start.8
  186.6 22.7 %collective-permute-start.11 = (bf16[128,2304]{1,0:T(8,128)(2,1)}, bf16[128,2304]{1,0:T(8,128)(2,1)}, u32[]{:S(2)}, u32[]{:S(2)}) collective-permute-start(bf16[128,2304]{1,0:T(8,128)(2,1)} %get-tuple-element.28), channel_id=1, source_target_pairs={{0,224},{16,240},{32,0},{48,16},{64,32},{80,48},{96,64},{112,80},{... | collective-permute-start | bytes 1769480 | tf_op jit(solution)/shard_map/weight_gradients/ppermute | solution.py:205
  190.3 19.0 %collective-permute-start.7 = (bf16[128,2304]{1,0:T(8,128)(2,1)}, bf16[128,2304]{1,0:T(8,128)(2,1)}, u32[]{:S(2)}, u32[]{:S(2)}) collective-permute-start(bf16[128,2304]{1,0:T(8,128)(2,1)} %get-tuple-element.29), channel_id=1, source_target_pairs={{0,32},{16,48},{32,64},{48,80},{64,96},{80,112},{96,128},{112,144}... | collective-permute-start | bytes 1769480 | tf_op jit(solution)/shard_map/weight_gradients/ppermute | solution.py:205
  190.4 3.7 %copy-start.4 = (bf16[2048,2304]{1,0:T(8,128)(2,1)S(1)}, bf16[2048,2304]{1,0:T(8,128)(2,1)}, u32[]{:S(2)}) copy-start(bf16[2048,2304]{1,0:T(8,128)(2,1)} %all-gather.2.cloned.1.call-done.wg.wu.wd) | copy-start | bytes 28311556
  199.0 20.1 %all-to-all-start.3 = ((bf16[16,16,2048]{2,1,0:T(8,128)(2,1)}), bf16[16,16,2048]{2,1,0:T(8,128)(2,1)}, u32[]{:S(2)}, u32[]{:S(2)}) async-start(bf16[16,16,2048]{2,1,0:T(8,128)(2,1)} %bitcast.81), calls=%async_computation.3 | async-start | bytes 2097152 | tf_op jit(solution)/shard_map/token_gradient/all_to_all | solution.py:17
  211.8 13.5 %collective-permute-start.12 = (bf16[128,2304]{1,0:T(8,128)(2,1)}, bf16[128,2304]{1,0:T(8,128)(2,1)}, u32[]{:S(2)}, u32[]{:S(2)}) collective-permute-start(bf16[128,2304]{1,0:T(8,128)(2,1)} %get-tuple-element.26), channel_id=1, source_target_pairs={{0,224},{16,240},{32,0},{48,16},{64,32},{80,48},{96,64},{112,80},{... | collective-permute-start | bytes 1769480 | tf_op jit(solution)/shard_map/weight_gradients/ppermute | solution.py:205
  215.0 13.4 %collective-permute-start.8 = (bf16[128,2304]{1,0:T(8,128)(2,1)}, bf16[128,2304]{1,0:T(8,128)(2,1)}, u32[]{:S(2)}, u32[]{:S(2)}) collective-permute-start(bf16[128,2304]{1,0:T(8,128)(2,1)} %get-tuple-element.27), channel_id=1, source_target_pairs={{0,32},{16,48},{32,64},{48,80},{64,96},{80,112},{96,128},{112,144}... | collective-permute-start | bytes 1769480 | tf_op jit(solution)/shard_map/weight_gradients/ppermute | solution.py:205
  219.1 4.1 %copy-start.10 = (bf16[16,16,2048]{2,1,0:T(8,128)(2,1)S(1)}, bf16[16,16,2048]{2,1,0:T(8,128)(2,1)}, u32[]{:S(2)}) copy-start(bf16[16,16,2048]{2,1,0:T(8,128)(2,1)} %all_to_all.20) | copy-start | bytes 3145732
  (5 other events, 5.4 us)
Sparse Core Ops, SparseCore 0:
  10.4 63.7 all-gather.1

commit v2 on v1

v2 whole, which is shorter than its diff:
```python
import jax
import jax.numpy as jnp
from jax import lax
from jax.experimental import pallas as pl
from jax.experimental.pallas import tpu as pltpu
from jax.sharding import PartitionSpec as P

F32 = jnp.float32
BF16 = jnp.bfloat16
ROW_BY_ROW = ((1,), (0,))
OVER_LAST = ((1,), (1,))
OVER_FIRST = ((0,), (0,))
MIB = 1024 * 1024
VMEM_LIMIT = 24 * MIB


def exchange(block):
    return lax.all_to_all(block, "expert", split_axis=0, concat_axis=0, tiled=True)


def dot(a, b, dims):
    return lax.dot_general(a, b, (dims, ((), ())), preferred_element_type=F32)


def in_hbm(array):
    return pltpu.with_memory_space_constraint(array, pltpu.HBM)


def call(body, grid, in_specs, out_specs, out_shape, flops, moved, prefetch=0, limit=VMEM_LIMIT):
    return pl.pallas_call(
        body,
        grid_spec=pltpu.PrefetchScalarGridSpec(
            num_scalar_prefetch=prefetch, grid=grid, in_specs=in_specs, out_specs=out_specs
        ),
        out_shape=out_shape,
        compiler_params=pltpu.CompilerParams(vmem_limit_bytes=limit),
        cost_estimate=pl.CostEstimate(flops=flops, bytes_accessed=moved, transcendentals=0),
    )


def side_by_side(gate_weight, up_weight, down_weight):
    tall, ff = gate_weight.shape

    def body(g, u, d, out):
        out[:, :ff] = g[...]
        out[:, ff : 2 * ff] = u[...]
        out[:, 2 * ff :] = d[...]

    part = pl.BlockSpec((tall, ff), lambda i: (0, 0))
    return call(
        body,
        (1,),
        [part] * 3,
        pl.BlockSpec((tall, 3 * ff), lambda i: (0, 0)),
        shape(tall, 3 * ff, BF16),
        0,
        12 * tall * ff,
    )(gate_weight, up_weight, down_weight)


def shape(rows, columns, dtype):
    return jax.ShapeDtypeStruct((rows, columns), dtype)


def project_in(rows, full, ff):
    slots, width = rows.shape
    wide = 256
    steps = ff // wide

    def body(x, wg, wu, gate_pre, up_pre, hidden):
        g = dot(x[...], wg[...], ROW_BY_ROW)
        u = dot(x[...], wu[...], ROW_BY_ROW)
        gate_pre[...] = g
        up_pre[...] = u
        hidden[...] = (g * jax.nn.sigmoid(g) * u).astype(BF16)

    part = pl.BlockSpec((slots, wide), lambda j: (0, j))
    return call(
        body,
        (steps,),
        [
            pl.BlockSpec((slots, width), lambda j: (0, 0)),
            pl.BlockSpec((width, wide), lambda j: (0, j)),
            pl.BlockSpec((width, wide), lambda j: (0, steps + j)),
        ],
        [part, part, part],
        [shape(slots, ff, F32), shape(slots, ff, F32), shape(slots, ff, BF16)],
        4 * slots * width * ff,
        4 * width * ff + 2 * slots * width + 10 * slots * ff,
    )(rows, in_hbm(full), in_hbm(full))


def project_out(hidden, full, ff):
    slots, width = hidden.shape[0], full.shape[0]
    tall = 512

    def body(h, wd, out):
        out[...] = dot(h[...], wd[...], OVER_LAST).astype(BF16)

    return call(
        body,
        (width // tall,),
        [
            pl.BlockSpec((slots, ff), lambda j: (0, 0)),
            pl.BlockSpec((tall, ff), lambda j: (j, 2)),
        ],
        pl.BlockSpec((slots, tall), lambda j: (0, j)),
        shape(slots, width, BF16),
        2 * slots * width * ff,
        2 * width * ff + 2 * slots * (width + ff),
    )(hidden, in_hbm(full))


def combine(mix_high, mix_low, weight, returned, wanted):
    slots, width = returned.shape
    wide = 512

    def body(high, low, w, back, goal, out):
        x = back[...]
        total = dot(high[...], x, ROW_BY_ROW) + dot(low[...], x, ROW_BY_ROW)
        out[...] = (w[...] * (total - goal[...].astype(F32))).astype(BF16)

    mix = pl.BlockSpec((slots, slots), lambda j: (0, 0))
    part = pl.BlockSpec((slots, wide), lambda j: (0, j))
    return call(
        body,
        (width // wide,),
        [mix, mix, pl.BlockSpec((slots, 1), lambda j: (0, 0)), part, part],
        part,
        shape(slots, width, BF16),
        4 * slots * slots * width,
        6 * slots * width,
    )(mix_high, mix_low, weight, returned, wanted)


def back_in(owner_grad, full, gate_pre, up_pre, ff):
    slots, width = owner_grad.shape
    wide = 256
    steps = ff // wide

    def body(x, wd, gate_ref, up_ref, out):
        h = dot(x[...], wd[...], ROW_BY_ROW)
        g = gate_ref[...]
        sig = jax.nn.sigmoid(g)
        out[0] = (h * up_ref[...] * sig * (1.0 + g * (1.0 - sig))).astype(BF16)
        out[1] = (h * (g * sig)).astype(BF16)

    part = pl.BlockSpec((slots, wide), lambda j: (0, j))
    return call(
        body,
        (steps,),
        [
            pl.BlockSpec((slots, width), lambda j: (0, 0)),
            pl.BlockSpec((width, wide), lambda j: (0, 2 * steps + j)),
            part,
            part,
        ],
        pl.BlockSpec((2, slots, wide), lambda j: (0, 0, j)),
        jax.ShapeDtypeStruct((2, slots, ff), BF16),
        2 * slots * width * ff,
        2 * width * ff + 2 * slots * width + 12 * slots * ff,
    )(owner_grad, in_hbm(full), gate_pre, up_pre)


def back_out(pre_grad, full, ff):
    slots, width = pre_grad.shape[1], full.shape[0]
    tall = 512

    def body(x, wg, wu, out):
        out[...] = (
            dot(x[0], wg[...], OVER_LAST) + dot(x[1], wu[...], OVER_LAST)
        ).astype(BF16)

    return call(
        body,
        (width // tall,),
        [
            pl.BlockSpec((2, slots, ff), lambda j: (0, 0, 0)),
            pl.BlockSpec((tall, ff), lambda j: (j, 0)),
            pl.BlockSpec((tall, ff), lambda j: (j, 1)),
        ],
        pl.BlockSpec((slots, tall), lambda j: (0, j)),
        shape(slots, width, BF16),
        4 * slots * width * ff,
        4 * width * ff + 2 * slots * (width + 2 * ff),
    )(pre_grad, in_hbm(full), in_hbm(full))


def chip_terms(blocks, own, other, halves):
    count = blocks.shape[0]
    slots, ff = own[3].shape
    tall = 128

    def body(names, xa, pa, oa, ha, xb, pb, ob, hb, *outs):
        xa, xb, oa, ob = xa[...], xb[...], oa[...], ob[...]
        gate = dot(xa, pa[0], OVER_FIRST) + dot(xb, pb[0], OVER_FIRST)
        up = dot(xa, pa[1], OVER_FIRST) + dot(xb, pb[1], OVER_FIRST)
        down = dot(oa, ha[...], OVER_FIRST) + dot(ob, hb[...], OVER_FIRST)
        for at, part in ((0, gate), (ff, up), (2 * ff, down)):
            if halves:
                outs[0][:, at : at + ff] = part[: tall // 2].astype(BF16)
                outs[1][:, at : at + ff] = part[tall // 2 :].astype(BF16)
            else:
                outs[0][0, :, at : at + ff] = part

    column = pl.BlockSpec((slots, tall), lambda i, names: (0, names[i]))
    pair = pl.BlockSpec((2, slots, ff), lambda i, names: (0, 0, 0))
    whole = pl.BlockSpec((slots, ff), lambda i, names: (0, 0))
    if halves:
        out_specs = [pl.BlockSpec((tall // 2, 3 * ff), lambda i, names: (0, 0))] * 2
        out_shape = [shape(tall // 2, 3 * ff, BF16)] * 2
    else:
        out_specs = pl.BlockSpec((1, tall, 3 * ff), lambda i, names: (i, 0, 0))
        out_shape = jax.ShapeDtypeStruct((count, tall, 3 * ff), F32)
    return call(
        body,
        (count,),
        [column, pair, column, whole] * 2,
        out_specs,
        out_shape,
        12 * count * slots * tall * ff,
        12 * slots * ff + count * (8 * slots * tall + 12 * tall * ff),
        prefetch=1,
    )(blocks, *own, *other)


def add_terms(ahead, behind, terms, at):
    tall, width = terms.shape[1:]
    part = ahead.shape[0]

    def body(a, b, first, second, out_a, out_b):
        if part == tall:
            out_a[...] = (first[0] + a[...].astype(F32)).astype(BF16)
            out_b[...] = (second[0] + b[...].astype(F32)).astype(BF16)
        else:
            out_a[:part] = (first[0, :part] + a[...].astype(F32)).astype(BF16)
            out_a[part:] = first[0, part:].astype(BF16)
            out_b[:part] = second[0, :part].astype(BF16)
            out_b[part:] = (second[0, part:] + b[...].astype(F32)).astype(BF16)

    came = pl.BlockSpec((part, width), lambda i: (0, 0))
    sent = pl.BlockSpec((tall, width), lambda i: (0, 0))
    return call(
        body,
        (1,),
        [
            came,
            came,
            pl.BlockSpec((1, tall, width), lambda i: (at, 0, 0)),
            pl.BlockSpec((1, tall, width), lambda i: (at + 1, 0, 0)),
        ],
        [sent, sent],
        [shape(tall, width, BF16)] * 2,
        2 * tall * width,
        16 * tall * width,
    )(ahead, behind, terms, terms)


def last_sum(ahead, behind, terms, at, ff, factor):
    tall = ahead.shape[0]

    def body(a, b, mine, gate, up, down):
        total = (a[...].astype(F32) + b[...].astype(F32) + mine[0]) * factor
        gate[:, 0, :] = total[:, :ff]
        up[:, 0, :] = total[:, ff : 2 * ff]
        down[:, 0, :] = total[:, 2 * ff :]

    came = pl.BlockSpec((tall, 3 * ff), lambda i: (0, 0))
    part = pl.BlockSpec((tall, 1, ff), lambda i: (0, 0, 0))
    return call(
        body,
        (1,),
        [came, came, pl.BlockSpec((1, tall, 3 * ff), lambda i: (at, 0, 0))],
        [part] * 3,
        [jax.ShapeDtypeStruct((tall, 1, ff), F32)] * 3,
        12 * tall * ff,
        36 * tall * ff,
    )(ahead, behind, terms)


def to_tokens(names, came_back):
    held, slots = names.shape
    width = came_back.shape[1]
    wide = 512

    def body(which, back, out):
        out[...] = dot(which[...], back[...], ROW_BY_ROW).astype(BF16)

    return call(
        body,
        (width // wide,),
        [
            pl.BlockSpec((held, slots), lambda j: (0, 0)),
            pl.BlockSpec((slots, wide), lambda j: (0, j)),
        ],
        pl.BlockSpec((held, wide), lambda j: (0, j)),
        shape(held, width, BF16),
        2 * held * slots * width,
        2 * (held + slots) * width,
    )(names, came_back)


def on_device(
    tokens, target, route_index, route_count, route_gate, gate_weight, up_weight, down_weight
):
    groups = lax.axis_size("dp")
    sources = lax.axis_size("expert")
    chips = groups // 2
    local_index = route_index[0, :, 0, :]
    live_count = route_count[0, :, 0]
    per_source = local_index.shape[1]
    held, width = tokens.shape
    tall = gate_weight.shape[0]
    ff = gate_weight.shape[2]
    slots = sources * per_source

    def along(array, by):
        pairs = [
            (2 * z + c, 2 * ((z + by) % chips) + c) for z in range(chips) for c in range(2)
        ]
        return lax.ppermute(array, "dp", pairs)

    def other_core(array):
        return lax.ppermute(array, "dp", [(d, d ^ 1) for d in range(groups)])

    with jax.named_scope("gather_weights"):
        own = side_by_side(gate_weight[:, 0], up_weight[:, 0], down_weight[:, 0])
        full = lax.all_gather(own, "dp", axis=0, tiled=True)

    with jax.named_scope("routing"):
        usable = jnp.arange(per_source, dtype=jnp.int32)[None, :] < live_count[:, None]
        flat_index = local_index.reshape(slots)
        live = usable.reshape(slots)
        weight = jnp.where(live, route_gate[0, :, 0, :].reshape(slots), 0.0)
        names = flat_index[:, None] == jnp.arange(held, dtype=jnp.int32)[None, :]
        pick = (names & live[:, None]).astype(BF16)
        same = flat_index[:, None] == flat_index[None, :]
        high = lax.reduce_precision(weight, 8, 7)
        low = weight - high
        mix_high = jnp.where(same, high[None, :], 0.0).astype(BF16)
        mix_low = jnp.where(same, low[None, :], 0.0).astype(BF16)

    with jax.named_scope("rows_out"):
        rows = dot(pick, tokens, ROW_BY_ROW).astype(BF16)
        expert_rows = exchange(rows.reshape(sources, per_source, width)).reshape(slots, width)
        other_rows = other_core(expert_rows)
        wanted = dot(pick, target, ROW_BY_ROW).astype(BF16)

    with jax.named_scope("forward"):
        gate_pre, up_pre, hidden = project_in(expert_rows, full, ff)
        expert_out = project_out(hidden, full, ff)
        other_hidden = other_core(hidden)

    with jax.named_scope("combine"):
        returned = exchange(expert_out.reshape(sources, per_source, width)).reshape(slots, width)
        slot_grad = combine(mix_high, mix_low, weight[:, None], returned, wanted)
        owner_grad = exchange(slot_grad.reshape(sources, per_source, width)).reshape(slots, width)
        other_grad = other_core(owner_grad)

    with jax.named_scope("backward"):
        pre_grad = back_in(owner_grad, full, gate_pre, up_pre, ff)
        other_pre = other_core(pre_grad)

    with jax.named_scope("weight_gradients"):
        place = lax.axis_index("dp")
        z, core = place // 2, place % 2
        mine = (expert_rows, pre_grad, owner_grad, hidden)
        theirs = (other_rows, other_pre, other_grad, other_hidden)
        far = chips // 2
        steps = [s for near in range(far - 1, 0, -1) for s in (near, chips - near)] + [0]
        blocks = ((z + jnp.array([far] + steps, jnp.int32)) & (chips - 1)) * 2 + core
        ahead, behind = chip_terms(blocks[:1], mine, theirs, True)
        ahead, behind = along(ahead, 1), along(behind, -1)
        terms = chip_terms(blocks[1:], mine, theirs, False)
        for at in range(0, len(steps) - 1, 2):
            ahead, behind = add_terms(ahead, behind, terms, at)
            ahead, behind = along(ahead, 1), along(behind, -1)
        factor = (groups * sources * per_source) ** (-0.5)
        gradients = last_sum(ahead, behind, terms, len(steps) - 1, ff, factor)

    with jax.named_scope("token_gradient"):
        row_grad = back_out(pre_grad, full, ff)
        came_back = exchange(row_grad.reshape(sources, per_source, width)).reshape(slots, width)
        token_grad = to_tokens(names.T.astype(BF16), came_back)

    return (token_grad, *gradients)


def solution(mesh):
    return jax.shard_map(
        on_device,
        mesh=mesh,
        in_specs=(
            P(("dp", "expert"), None),
            P(("dp", "expert"), None),
            P("dp", None, "expert", None),
            P("dp", None, "expert"),
            P("dp", None, "expert", None),
            P("dp", "expert", None),
            P("dp", "expert", None),
            P("dp", "expert", None),
        ),
        out_specs=(
            P(("dp", "expert"), None),
            P("dp", "expert", None),
            P("dp", "expert", None),
            P("dp", "expert", None),
        ),
        check_vma=False,
    )
```

time: 241 us -> 229 us (0.950)
  blocking collectives: 23.2 us -> 0 us
  Pallas kernels: 27.7 us -> 41.8 us
  waiting for transfers between devices: 88.6 us -> 97.7 us
  other arithmetic: 13.4 us -> 5.32 us
  starting transfers between devices: 32.2 us -> 40 us
  local copies, waits for them, and re-layouts: 30.1 us -> 22.4 us
  matrix products: 10.8 us -> 5.94 us
    all_to_all x1 -> x0, blocking collectives: 23.2 us -> none  [exchange(): lax.all_to_all(block, 'expert', split_axis=0, concat_axis=0, tiled=True)]
    all_to_all x3 -> x4, waiting for transfers between devices: 32.4 us -> 43.7 us  [exchange(): lax.all_to_all(block, 'expert', split_axis=0, concat_axis=0, tiled=True)]
    unnamed x45 -> x44, local copies, waits for them, and re-layouts: 29.2 us -> 20.6 us
    pallas_call x7 -> x10, Pallas kernels: 19.4 us -> 27.8 us  [the longest x2 9.22 us: chip_terms(): call(body, (count,), [column, pair, column, whole] * 2, out_specs, out_sh...]
    all_to_all x3 -> x4, starting transfers between devices: 18.9 us -> 26.3 us  [exchange(): lax.all_to_all(block, 'expert', split_axis=0, concat_axis=0, tiled=True)]
    dot_general x5 -> x2, matrix products: 10.8 us -> 5.94 us  [dot(): return lax.dot_general(a, b, (dims, ((), ())), preferred_element_type=F32)]
    convert_element_type x2, other arithmetic: 4.92 us -> 0.94 us  [the longest x1 0.8 us: on_device(): mix_low = jnp.where(same, low[None, :], 0.0).astype(BF16)]
    concatenate x3 -> x0, other arithmetic: 3.83 us -> none  [the longest x1 2.12 us: on_device(): jnp.concatenate([gate_weight[:, 0], up_weight[:, 0], down_weight[:, 0]],...]
  transfers between devices with their start and end apart: 17 -> 17, of which waited for: 11 -> 10; matrix products, arithmetic and copies ran while one was open for 6% -> 6% of each run, Pallas kernels for 8% -> 10%
where the time goes in v2:
time: 229 us; the launch traced here: 227 us
  waiting for transfers between devices  97.7 us (43%)
  Pallas kernels  41.8 us (18%)
  starting transfers between devices  40 us (17%)
  local copies, waits for them, and re-layouts  22.4 us (10%)
  between operations  14.2 us (6%)
  matrix products  5.94 us (3%)
  other arithmetic  5.32 us (2%)
    all_to_all x4, waiting for transfers between devices, exchange(): lax.all_to_all(block, 'expert', split_axis=0, concat_axis=0, tiled=True)  43.7 us
    all_gather x1, waiting for transfers between devices, on_device(): full = lax.all_gather(own, 'dp', axis=0, tiled=True)  35.8 us
    all_to_all x4, starting transfers between devices, exchange(): lax.all_to_all(block, 'expert', split_axis=0, concat_axis=0, tiled=True)  26.3 us
    unnamed x44, local copies, waits for them, and re-layouts  20.6 us
    ppermute x8, waiting for transfers between devices, along(): return lax.ppermute(array, 'dp', pairs)  15.4 us
    ppermute x8, starting transfers between devices, along(): return lax.ppermute(array, 'dp', pairs)  13.1 us
    pallas_call x2, Pallas kernels, chip_terms(): call(body, (count,), [column, pair, column, whole] * 2, out_specs, out_sh...  9.22 us
    dot_general x2, matrix products, dot(): return lax.dot_general(a, b, (dims, ((), ())), preferred_element_type=F32)  5.94 us
  transfers between devices with their start and end apart: 17, of which 10 were waited for; matrix products, arithmetic and copies ran while one was open for 6% of the time, Pallas kernels for 10%

profile of v2, /device:TPU:2, one launch (start us, length us, event | category | flops | bytes accessed | tf_op | source)
XLA Modules:
  0.0 227.4 jit_solution(14999748670155973294)
XLA Ops:
  12.4 1.4 reduce.8
  13.8 2.0 convolution_convert_fusion.1
  15.8 7.5 %all-to-all-start = ((bf16[16,16,2048]{2,1,0:T(8,128)(2,1)}), bf16[16,16,2048]{2,1,0:T(8,128)(2,1)}, u32[]{:S(2)}, u32[]{:S(2)}) async-start(bf16[16,16,2048]{2,1,0:T(8,128)(2,1)} %bitcast.23), calls=%async_computation | async-start | bytes 2097152 | tf_op jit(solution)/shard_map/rows_out/all_to_all | solution.py:18
  26.1 13.1 %all-to-all-done = bf16[16,16,2048]{2,1,0:T(8,128)(2,1)} async-done(((bf16[16,16,2048]{2,1,0:T(8,128)(2,1)}), bf16[16,16,2048]{2,1,0:T(8,128)(2,1)}, u32[]{:S(2)}, u32[]{:S(2)}) %all-to-all-start) | async-done | bytes 1048608 | tf_op jit(solution)/shard_map/rows_out/all_to_all | solution.py:18
  39.2 35.8 %all-gather.2.cloned.1.call-done.wg.wu.wd = bf16[2048,2304]{1,0:T(8,128)(2,1)} async-done(((bf16[128,2304]{1,0:T(8,128)(2,1)}), bf16[2048,2304]{1,0:T(8,128)(2,1)}) %all-gather.2.cloned.1.call-update) | async-done | bytes 9437200 | tf_op jit(solution)/shard_map/gather_weights/all_gather | solution.py:328
  75.0 5.3 %forward.2 = (f32[256,768]{1,0:T(8,128)S(1)}, f32[256,768]{1,0:T(8,128)S(1)}, bf16[256,768]{1,0:T(8,128)(2,1)S(1)}) custom-call(bf16[256,2048]{1,0:T(8,128)(2,1)} %bitcast.2.x.xa, bf16[2048,2304]{1,0:T(8,128)(2,1)} %all-gather.2.cloned.1.call-done.wg.wu.wd, bf16[2048,2304]{1,0:T(8,128)(2,1)} %all-gather.2.cloned.1.call-done.wg.wu.wd), custom_call_target="tpu_custom_call" | custom-call | flops 1610612736 | bytes 9306112 | tf_op jit(solution)/shard_map/forward/pallas_call | solution.py:78
  80.4 4.2 %forward.3 = bf16[256,2048]{1,0:T(8,128)(2,1)S(1)} custom-call(bf16[256,768]{1,0:T(8,128)(2,1)S(1)} %get-tuple-element.18.h.ha, bf16[2048,2304]{1,0:T(8,128)(2,1)} %all-gather.2.cloned.1.call-done.wg.wu.wd), custom_call_target="tpu_custom_call" | custom-call | flops 805306368 | bytes 4587520 | tf_op jit(solution)/shard_map/forward/pallas_call | solution.py:100
  85.5 7.3 %all-to-all-start.1 = ((bf16[16,16,2048]{2,1,0:T(8,128)(2,1)}), bf16[16,16,2048]{2,1,0:T(8,128)(2,1)}, u32[]{:S(2)}, u32[]{:S(2)}) async-start(bf16[16,16,2048]{2,1,0:T(8,128)(2,1)} %bitcast.18), calls=%async_computation.1 | async-start | bytes 2097152 | tf_op jit(solution)/shard_map/combine/all_to_all | solution.py:18
  93.6 1.6 broadcast_select_fusion.w
  95.2 3.9 %convolution_convert_fusion.goal = bf16[256,2048]{1,0:T(8,128)(2,1)} fusion(bf16[768,2048]{1,0:T(8,128)(2,1)} %param.10, s32[256]{0:T(256)S(1)} %eq.37, pred[256]{0:T(512)(128)(4,1)S(1)} %lt.49), kind=kOutput, calls=%fused_computation | convolution fusion | flops 806223872 | bytes 4195584 | tf_op jit(solution)/shard_map/rows_out/dot_general | solution.py:22
  99.1 10.0 %all-to-all-done.1 = bf16[16,16,2048]{2,1,0:T(8,128)(2,1)} async-done(((bf16[16,16,2048]{2,1,0:T(8,128)(2,1)}), bf16[16,16,2048]{2,1,0:T(8,128)(2,1)}, u32[]{:S(2)}, u32[]{:S(2)}) %all-to-all-start.1) | async-done | bytes 1048608 | tf_op jit(solution)/shard_map/combine/all_to_all | solution.py:18
  113.0 2.9 %combine.1 = bf16[256,2048]{1,0:T(8,128)(2,1)S(1)} custom-call(bf16[256,256]{1,0:T(8,128)(2,1)S(1)} %copy-done.14, bf16[256,256]{1,0:T(8,128)(2,1)S(1)} %copy-done.13, f32[256,1]{1,0:T(8,128)S(1)} %copy-done.15, bf16[256,2048]{1,0:T(8,128)(2,1)} %bitcast.7.back, bf16[256,2048]{1,0:T(8,128)(2,1)S(1)} %copy-done.8), custom_call_target="tpu_custom_call" | custom-call | flops 536870912 | bytes 3145728 | tf_op jit(solution)/shard_map/combine/pallas_call | solution.py:125
  117.0 5.8 %all-to-all-start.2 = ((bf16[16,16,2048]{2,1,0:T(8,128)(2,1)}), bf16[16,16,2048]{2,1,0:T(8,128)(2,1)}, u32[]{:S(2)}, u32[]{:S(2)}) async-start(bf16[16,16,2048]{2,1,0:T(8,128)(2,1)} %bitcast.17), calls=%async_computation.2 | async-start | bytes 2097152 | tf_op jit(solution)/shard_map/combine/all_to_all | solution.py:18
  122.8 15.2 %all-to-all-done.2 = bf16[16,16,2048]{2,1,0:T(8,128)(2,1)} async-done(((bf16[16,16,2048]{2,1,0:T(8,128)(2,1)}), bf16[16,16,2048]{2,1,0:T(8,128)(2,1)}, u32[]{:S(2)}, u32[]{:S(2)}) %all-to-all-start.2) | async-done | bytes 1048608 | tf_op jit(solution)/shard_map/combine/all_to_all | solution.py:18
  140.3 4.5 %backward.1.x.pa = bf16[2,256,768]{2,1,0:T(8,128)(2,1)} custom-call(bf16[256,2048]{1,0:T(8,128)(2,1)} %bitcast.9.x.oa, bf16[2048,2304]{1,0:T(8,128)(2,1)} %all-gather.2.cloned.1.call-done.wg.wu.wd, f32[256,768]{1,0:T(8,128)S(1)} %copy-done.10, f32[256,768]{1,0:T(8,128)S(1)} %copy-done.12), custom_call_target="tpu_custom_call" | custom-call | flops 805306368 | bytes 6553600 | tf_op jit(solution)/shard_map/backward/pallas_call | solution.py:149
  145.4 2.4 %collective-permute-done.3.hb = bf16[256,768]{1,0:T(8,128)(2,1)} collective-permute-done((bf16[256,768]{1,0:T(8,128)(2,1)S(1)}, bf16[256,768]{1,0:T(8,128)(2,1)}, u32[]{:S(2)}, u32[]{:S(2)}) %collective-permute-start.3) | collective-permute-done | bytes 393248 | tf_op jit(solution)/shard_map/forward/ppermute | solution.py:324
  148.2 2.1 weight_gradients.6
  150.4 3.2 %collective-permute-start.5 = (bf16[64,2304]{1,0:T(8,128)(2,1)S(1)}, bf16[64,2304]{1,0:T(8,128)(2,1)S(1)}, u32[]{:S(2)}, u32[]{:S(2)}) collective-permute-start(bf16[64,2304]{1,0:T(8,128)(2,1)S(1)} %get-tuple-element.22), channel_id=1, source_target_pairs={{0,224},{16,240},{32,0},{48,16},{64,32},{80,48},{96,64},{112,80},{... | collective-permute-start | bytes 884744 | tf_op jit(solution)/shard_map/weight_gradients/ppermute | solution.py:321
  153.7 7.1 %weight_gradients.7.first.second.mine = f32[7,128,2304]{2,1,0:T(8,128)S(1)} custom-call(s32[7]{0:T(128)S(1)} %slice.7.names, bf16[256,2048]{1,0:T(8,128)(2,1)} %bitcast.2.x.xa, bf16[2,256,768]{2,1,0:T(8,128)(2,1)} %backward.1.x.pa, bf16[256,2048]{1,0:T(8,128)(2,1)} %bitcast.9.x.oa, bf16[256,768]{1,0:T(8,128)(2,1)S(1)} %get-tuple-element.18.h.ha, ...), custom_call_target="tpu_custom_call" | custom-call | flops 2113929216 | bytes 12451840 | tf_op jit(solution)/shard_map/weight_gradients/pallas_call | solution.py:215
  161.9 2.5 %collective-permute-start.7 = (bf16[128,2304]{1,0:T(8,128)(2,1)S(1)}, bf16[128,2304]{1,0:T(8,128)(2,1)S(1)}, u32[]{:S(2)}, u32[]{:S(2)}) collective-permute-start(bf16[128,2304]{1,0:T(8,128)(2,1)S(1)} %get-tuple-element.24), channel_id=1, source_target_pairs={{0,224},{16,240},{32,0},{48,16},{64,32},{80,48},{96,64},{112,80},{... | collective-permute-start | bytes 1769480 | tf_op jit(solution)/shard_map/weight_gradients/ppermute | solution.py:321
  164.4 13.0 %collective-permute-done.6.a = bf16[128,2304]{1,0:T(8,128)(2,1)S(1)} collective-permute-done((bf16[128,2304]{1,0:T(8,128)(2,1)S(1)}, bf16[128,2304]{1,0:T(8,128)(2,1)S(1)}, u32[]{:S(2)}, u32[]{:S(2)}) %collective-permute-start.6) | collective-permute-done | bytes 589856 | tf_op jit(solution)/shard_map/weight_gradients/ppermute | solution.py:321
  179.1 2.7 %collective-permute-start.9 = (bf16[128,2304]{1,0:T(8,128)(2,1)}, bf16[128,2304]{1,0:T(8,128)(2,1)}, u32[]{:S(2)}, u32[]{:S(2)}) collective-permute-start(bf16[128,2304]{1,0:T(8,128)(2,1)} %get-tuple-element.26), channel_id=1, source_target_pairs={{0,224},{16,240},{32,0},{48,16},{64,32},{80,48},{96,64},{112,80},{... | collective-permute-start | bytes 1769480 | tf_op jit(solution)/shard_map/weight_gradients/ppermute | solution.py:321
  181.8 5.0 %token_gradient.2 = bf16[256,2048]{1,0:T(8,128)(2,1)S(1)} custom-call(bf16[2,256,768]{2,1,0:T(8,128)(2,1)} %backward.1.x.pa, bf16[2048,2304]{1,0:T(8,128)(2,1)} %all-gather.2.cloned.1.call-done.wg.wu.wd, bf16[2048,2304]{1,0:T(8,128)(2,1)} %all-gather.2.cloned.1.call-done.wg.wu.wd), custom_call_target="tpu_custom_call" | custom-call | flops 1610612736 | bytes 8126464 | tf_op jit(solution)/shard_map/token_gradient/pallas_call | solution.py:174
  187.8 5.8 %all-to-all-start.3 = ((bf16[16,16,2048]{2,1,0:T(8,128)(2,1)}), bf16[16,16,2048]{2,1,0:T(8,128)(2,1)}, u32[]{:S(2)}, u32[]{:S(2)}) async-start(bf16[16,16,2048]{2,1,0:T(8,128)(2,1)} %bitcast.16), calls=%async_computation.3 | async-start | bytes 2097152 | tf_op jit(solution)/shard_map/token_gradient/all_to_all | solution.py:18
  194.2 3.3 %copy-done.2 = f32[7,128,2304]{2,1,0:T(8,128)S(1)} copy-done((f32[7,128,2304]{2,1,0:T(8,128)S(1)}, f32[7,128,2304]{2,1,0:T(8,128)}, u32[]{:S(2)}) %copy-start.2) | copy-done | bytes 8257560
  197.6 2.4 %weight_gradients.10 = (bf16[128,2304]{1,0:T(8,128)(2,1)}, bf16[128,2304]{1,0:T(8,128)(2,1)}) custom-call(bf16[128,2304]{1,0:T(8,128)(2,1)} %collective-permute-done.8.a, bf16[128,2304]{1,0:T(8,128)(2,1)} %collective-permute-done.9.b, f32[7,128,2304]{2,1,0:T(8,128)S(1)} %copy-done.2, f32[7,128,2304]{2,1,0:T(8,128)S(1)} %copy-done.2), custom_call_target="tpu_custom_call" | custom-call | flops 589824 | bytes 4718592 | tf_op jit(solution)/shard_map/weight_gradients/pallas_call | solution.py:243
  200.8 2.5 %collective-permute-start.11 = (bf16[128,2304]{1,0:T(8,128)(2,1)}, bf16[128,2304]{1,0:T(8,128)(2,1)}, u32[]{:S(2)}, u32[]{:S(2)}) collective-permute-start(bf16[128,2304]{1,0:T(8,128)(2,1)} %get-tuple-element.28), channel_id=1, source_target_pairs={{0,224},{16,240},{32,0},{48,16},{64,32},{80,48},{96,64},{112,80},{... | collective-permute-start | bytes 1769480 | tf_op jit(solution)/shard_map/weight_gradients/ppermute | solution.py:321
  203.4 5.3 %all-to-all-done.3 = bf16[16,16,2048]{2,1,0:T(8,128)(2,1)} async-done(((bf16[16,16,2048]{2,1,0:T(8,128)(2,1)}), bf16[16,16,2048]{2,1,0:T(8,128)(2,1)}, u32[]{:S(2)}, u32[]{:S(2)}) %all-to-all-start.3) | async-done | bytes 1048608 | tf_op jit(solution)/shard_map/token_gradient/all_to_all | solution.py:18
  208.7 4.4 %token_gradient.3 = bf16[768,2048]{1,0:T(8,128)(2,1)} custom-call(bf16[768,256]{1,0:T(8,128)(2,1)S(1)} %fusion.which, bf16[256,2048]{1,0:T(8,128)(2,1)} %bitcast.11.back), custom_call_target="tpu_custom_call" | custom-call | flops 805306368 | bytes 4194304 | tf_op jit(solution)/shard_map/token_gradient/pallas_call | solution.py:289
  213.1 1.7 collective-permute-done.10.a
  214.8 3.3 %copy-done.3 = f32[7,128,2304]{2,1,0:T(8,128)S(1)} copy-done((f32[7,128,2304]{2,1,0:T(8,128)S(1)}, f32[7,128,2304]{2,1,0:T(8,128)}, u32[]{:S(2)}) %copy-start.3) | copy-done | bytes 8257560
  218.1 2.4 %weight_gradients.11 = (f32[128,1,768]{2,1,0:T(1,128)}, f32[128,1,768]{2,1,0:T(1,128)}, f32[128,1,768]{2,1,0:T(1,128)}) custom-call(bf16[128,2304]{1,0:T(8,128)(2,1)} %collective-permute-done.10.a, bf16[128,2304]{1,0:T(8,128)(2,1)} %collective-permute-done.11.b, f32[7,128,2304]{2,1,0:T(8,128)S(1)} %copy-done.3), custom_call_target="tpu_custom_call" | custom-call | flops 1179648 | bytes 3538944 | tf_op jit(solution)/shard_map/weight_gradients/pallas_call | solution.py:270
  (76 shorter events, 23.4 us)
Async XLA Ops:
  7.2 6.7 %copy-start = (bf16[768,2048]{1,0:T(8,128)(2,1)S(1)}, bf16[768,2048]{1,0:T(8,128)(2,1)}, u32[]{:S(2)}) copy-start(bf16[768,2048]{1,0:T(8,128)(2,1)} %param.9) | copy-start | bytes 9437188
  7.2 67.8 %all-gather.2.cloned.1.call-start = ((), (), s32[]{:S(2)}) async-start(), calls=%async_computation.4 | async-start | bytes 10027008 | tf_op jit(solution)/shard_map/gather_weights/all_gather | solution.py:328
  7.2 1.1 copy-start.16
  13.8 10.7 %copy-start.19 = (f32[1,16,1,16]{3,2,1,0:T(1,128)S(1)}, f32[1,16,1,16]{3,2,1,0:T(1,128)}, u32[]{:S(2)}) copy-start(f32[1,16,1,16]{3,2,1,0:T(1,128)} %param.13) | copy-start | bytes 3076
  15.8 23.4 %all-to-all-start = ((bf16[16,16,2048]{2,1,0:T(8,128)(2,1)}), bf16[16,16,2048]{2,1,0:T(8,128)(2,1)}, u32[]{:S(2)}, u32[]{:S(2)}) async-start(bf16[16,16,2048]{2,1,0:T(8,128)(2,1)} %bitcast.23), calls=%async_computation | async-start | bytes 2097152 | tf_op jit(solution)/shard_map/rows_out/all_to_all | solution.py:18
  80.3 4.2 %copy-start.9 = (f32[256,768]{1,0:T(8,128)}, f32[256,768]{1,0:T(8,128)S(1)}, u32[]{:S(2)}) copy-start(f32[256,768]{1,0:T(8,128)S(1)} %get-tuple-element.19.gate_ref) | copy-start | bytes 2359300
  80.4 4.2 %copy-start.11 = (f32[256,768]{1,0:T(8,128)}, f32[256,768]{1,0:T(8,128)S(1)}, u32[]{:S(2)}) copy-start(f32[256,768]{1,0:T(8,128)S(1)} %get-tuple-element.20.up_ref) | copy-start | bytes 2359300
  84.5 1.0 copy-start.6
  85.5 23.6 %all-to-all-start.1 = ((bf16[16,16,2048]{2,1,0:T(8,128)(2,1)}), bf16[16,16,2048]{2,1,0:T(8,128)(2,1)}, u32[]{:S(2)}, u32[]{:S(2)}) async-start(bf16[16,16,2048]{2,1,0:T(8,128)(2,1)} %bitcast.18), calls=%async_computation.1 | async-start | bytes 2097152 | tf_op jit(solution)/shard_map/combine/all_to_all | solution.py:18
  109.1 1.2 copy-start.8
  116.0 1.0 copy-start.5
  117.0 21.1 %all-to-all-start.2 = ((bf16[16,16,2048]{2,1,0:T(8,128)(2,1)}), bf16[16,16,2048]{2,1,0:T(8,128)(2,1)}, u32[]{:S(2)}, u32[]{:S(2)}) async-start(bf16[16,16,2048]{2,1,0:T(8,128)(2,1)} %bitcast.17), calls=%async_computation.2 | async-start | bytes 2097152 | tf_op jit(solution)/shard_map/combine/all_to_all | solution.py:18
  122.8 22.6 %collective-permute-start = (bf16[256,2048]{1,0:T(8,128)(2,1)}, bf16[256,2048]{1,0:T(8,128)(2,1)}, u32[]{:S(2)}, u32[]{:S(2)}) collective-permute-start(bf16[256,2048]{1,0:T(8,128)(2,1)} %bitcast.2.x.xa), channel_id=1, source_target_pairs={{0,16},{16,0},{32,48},{48,32},{64,80},{80,64},{96,112},{112,96},{1... | collective-permute-start | bytes 3145736 | tf_op jit(solution)/shard_map/rows_out/ppermute | solution.py:324
  138.0 10.1 %collective-permute-start.2 = (bf16[256,2048]{1,0:T(8,128)(2,1)}, bf16[256,2048]{1,0:T(8,128)(2,1)}, u32[]{:S(2)}, u32[]{:S(2)}) collective-permute-start(bf16[256,2048]{1,0:T(8,128)(2,1)} %bitcast.9.x.oa), channel_id=1, source_target_pairs={{0,16},{16,0},{32,48},{48,32},{64,80},{80,64},{96,112},{112,96},{1... | collective-permute-start | bytes 3145736 | tf_op jit(solution)/shard_map/combine/ppermute | solution.py:324
  138.0 1.1 copy-start.10
  139.2 1.1 copy-start.12
  140.3 5.1 %copy-start.20 = (s32[8]{0:T(128)S(1)}, s32[8]{0:T(128)}, u32[]{:S(2)}) copy-start(s32[8]{0:T(128)} %constant.36.clone) | copy-start | bytes 100
  144.8 3.3 %collective-permute-start.1 = (bf16[2,256,768]{2,1,0:T(8,128)(2,1)}, bf16[2,256,768]{2,1,0:T(8,128)(2,1)}, u32[]{:S(2)}, u32[]{:S(2)}) collective-permute-start(bf16[2,256,768]{2,1,0:T(8,128)(2,1)} %backward.1.x.pa), channel_id=1, source_target_pairs={{0,16},{16,0},{32,48},{48,32},{64,80},{80,64},{96,112},{112,96},{1... | collective-permute-start | bytes 2359304 | tf_op jit(solution)/shard_map/backward/ppermute | solution.py:324
  145.3 2.5 %collective-permute-start.3 = (bf16[256,768]{1,0:T(8,128)(2,1)S(1)}, bf16[256,768]{1,0:T(8,128)(2,1)}, u32[]{:S(2)}, u32[]{:S(2)}) collective-permute-start(bf16[256,768]{1,0:T(8,128)(2,1)S(1)} %get-tuple-element.18.h.ha), channel_id=1, source_target_pairs={{0,16},{16,0},{32,48},{48,32},{64,80},{80,64},{96,112},{112,96},{1... | collective-permute-start | bytes 1179656 | tf_op jit(solution)/shard_map/forward/ppermute | solution.py:324
  150.3 10.6 %collective-permute-start.4 = (bf16[64,2304]{1,0:T(8,128)(2,1)S(1)}, bf16[64,2304]{1,0:T(8,128)(2,1)S(1)}, u32[]{:S(2)}, u32[]{:S(2)}) collective-permute-start(bf16[64,2304]{1,0:T(8,128)(2,1)S(1)} %get-tuple-element.21), channel_id=1, source_target_pairs={{0,32},{16,48},{32,64},{48,80},{64,96},{80,112},{96,128},{112,144}... | collective-permute-start | bytes 884744 | tf_op jit(solution)/shard_map/weight_gradients/ppermute | solution.py:321
  150.4 10.5 %collective-permute-start.5 = (bf16[64,2304]{1,0:T(8,128)(2,1)S(1)}, bf16[64,2304]{1,0:T(8,128)(2,1)S(1)}, u32[]{:S(2)}, u32[]{:S(2)}) collective-permute-start(bf16[64,2304]{1,0:T(8,128)(2,1)S(1)} %get-tuple-element.22), channel_id=1, source_target_pairs={{0,224},{16,240},{32,0},{48,16},{64,32},{80,48},{96,64},{112,80},{... | collective-permute-start | bytes 884744 | tf_op jit(solution)/shard_map/weight_gradients/ppermute | solution.py:321
  160.8 16.6 %copy-start.1 = (f32[7,128,2304]{2,1,0:T(8,128)}, f32[7,128,2304]{2,1,0:T(8,128)S(1)}, u32[]{:S(2)}) copy-start(f32[7,128,2304]{2,1,0:T(8,128)S(1)} %weight_gradients.7.first.second.mine) | copy-start | bytes 24772612
  161.0 16.3 %collective-permute-start.6 = (bf16[128,2304]{1,0:T(8,128)(2,1)S(1)}, bf16[128,2304]{1,0:T(8,128)(2,1)S(1)}, u32[]{:S(2)}, u32[]{:S(2)}) collective-permute-start(bf16[128,2304]{1,0:T(8,128)(2,1)S(1)} %get-tuple-element.23), channel_id=1, source_target_pairs={{0,32},{16,48},{32,64},{48,80},{64,96},{80,112},{96,128},{112,144}... | collective-permute-start | bytes 1769480 | tf_op jit(solution)/shard_map/weight_gradients/ppermute | solution.py:321
  161.9 15.5 %collective-permute-start.7 = (bf16[128,2304]{1,0:T(8,128)(2,1)S(1)}, bf16[128,2304]{1,0:T(8,128)(2,1)S(1)}, u32[]{:S(2)}, u32[]{:S(2)}) collective-permute-start(bf16[128,2304]{1,0:T(8,128)(2,1)S(1)} %get-tuple-element.24), channel_id=1, source_target_pairs={{0,224},{16,240},{32,0},{48,16},{64,32},{80,48},{96,64},{112,80},{... | collective-permute-start | bytes 1769480 | tf_op jit(solution)/shard_map/weight_gradients/ppermute | solution.py:321
  178.5 15.7 %collective-permute-start.8 = (bf16[128,2304]{1,0:T(8,128)(2,1)}, bf16[128,2304]{1,0:T(8,128)(2,1)}, u32[]{:S(2)}, u32[]{:S(2)}) collective-permute-start(bf16[128,2304]{1,0:T(8,128)(2,1)} %get-tuple-element.25), channel_id=1, source_target_pairs={{0,32},{16,48},{32,64},{48,80},{64,96},{80,112},{96,128},{112,144}... | collective-permute-start | bytes 1769480 | tf_op jit(solution)/shard_map/weight_gradients/ppermute | solution.py:321
  179.1 15.1 %collective-permute-start.9 = (bf16[128,2304]{1,0:T(8,128)(2,1)}, bf16[128,2304]{1,0:T(8,128)(2,1)}, u32[]{:S(2)}, u32[]{:S(2)}) collective-permute-start(bf16[128,2304]{1,0:T(8,128)(2,1)} %get-tuple-element.26), channel_id=1, source_target_pairs={{0,224},{16,240},{32,0},{48,16},{64,32},{80,48},{96,64},{112,80},{... | collective-permute-start | bytes 1769480 | tf_op jit(solution)/shard_map/weight_gradients/ppermute | solution.py:321
  186.8 1.0 copy-start.4
  187.8 20.9 %all-to-all-start.3 = ((bf16[16,16,2048]{2,1,0:T(8,128)(2,1)}), bf16[16,16,2048]{2,1,0:T(8,128)(2,1)}, u32[]{:S(2)}, u32[]{:S(2)}) async-start(bf16[16,16,2048]{2,1,0:T(8,128)(2,1)} %bitcast.16), calls=%async_computation.3 | async-start | bytes 2097152 | tf_op jit(solution)/shard_map/token_gradient/all_to_all | solution.py:18
  194.2 3.3 %copy-start.2 = (f32[7,128,2304]{2,1,0:T(8,128)S(1)}, f32[7,128,2304]{2,1,0:T(8,128)}, u32[]{:S(2)}) copy-start(f32[7,128,2304]{2,1,0:T(8,128)} %copy-done.1) | copy-start | bytes 24772612
  200.0 14.8 %collective-permute-start.10 = (bf16[128,2304]{1,0:T(8,128)(2,1)}, bf16[128,2304]{1,0:T(8,128)(2,1)}, u32[]{:S(2)}, u32[]{:S(2)}) collective-permute-start(bf16[128,2304]{1,0:T(8,128)(2,1)} %get-tuple-element.27), channel_id=1, source_target_pairs={{0,32},{16,48},{32,64},{48,80},{64,96},{80,112},{96,128},{112,144}... | collective-permute-start | bytes 1769480 | tf_op jit(solution)/shard_map/weight_gradients/ppermute | solution.py:321
  200.8 14.0 %collective-permute-start.11 = (bf16[128,2304]{1,0:T(8,128)(2,1)}, bf16[128,2304]{1,0:T(8,128)(2,1)}, u32[]{:S(2)}, u32[]{:S(2)}) collective-permute-start(bf16[128,2304]{1,0:T(8,128)(2,1)} %get-tuple-element.28), channel_id=1, source_target_pairs={{0,224},{16,240},{32,0},{48,16},{64,32},{80,48},{96,64},{112,80},{... | collective-permute-start | bytes 1769480 | tf_op jit(solution)/shard_map/weight_gradients/ppermute | solution.py:321
  214.8 3.3 %copy-start.3 = (f32[7,128,2304]{2,1,0:T(8,128)S(1)}, f32[7,128,2304]{2,1,0:T(8,128)}, u32[]{:S(2)}) copy-start(f32[7,128,2304]{2,1,0:T(8,128)} %copy-done.1) | copy-start | bytes 24772612
  (6 other events, 5.4 us)
Sparse Core Ops, SparseCore 0:
  11.2 63.7 all-gather.1

commit v3 on v2

--- a/solution.py
+++ b/solution.py
@@ -26,6 +26,10 @@
     return pltpu.with_memory_space_constraint(array, pltpu.HBM)
 
 
+def held_in_hbm(dims, dtype):
+    return pltpu.HBM(dims, dtype)
+
+
 def call(body, grid, in_specs, out_specs, out_shape, flops, moved, prefetch=0, limit=VMEM_LIMIT):
     return pl.pallas_call(
         body,
@@ -52,10 +56,10 @@
         (1,),
         [part] * 3,
         pl.BlockSpec((tall, 3 * ff), lambda i: (0, 0)),
-        shape(tall, 3 * ff, BF16),
+        held_in_hbm((tall, 3 * ff), BF16),
         0,
         12 * tall * ff,
-    )(gate_weight, up_weight, down_weight)
+    )(in_hbm(gate_weight), in_hbm(up_weight), in_hbm(down_weight))
 
 
 def shape(rows, columns, dtype):
@@ -84,7 +88,7 @@
             pl.BlockSpec((width, wide), lambda j: (0, steps + j)),
         ],
         [part, part, part],
-        [shape(slots, ff, F32), shape(slots, ff, F32), shape(slots, ff, BF16)],
+        [held_in_hbm((slots, ff), F32), held_in_hbm((slots, ff), F32), shape(slots, ff, BF16)],
         4 * slots * width * ff,
         4 * width * ff + 2 * slots * width + 10 * slots * ff,
     )(rows, in_hbm(full), in_hbm(full))
@@ -105,7 +109,7 @@
             pl.BlockSpec((tall, ff), lambda j: (j, 2)),
         ],
         pl.BlockSpec((slots, tall), lambda j: (0, j)),
-        shape(slots, width, BF16),
+        held_in_hbm((slots, width), BF16),
         2 * slots * width * ff,
         2 * width * ff + 2 * slots * (width + ff),
     )(hidden, in_hbm(full))
@@ -127,10 +131,10 @@
         (width // wide,),
         [mix, mix, pl.BlockSpec((slots, 1), lambda j: (0, 0)), part, part],
         part,
-        shape(slots, width, BF16),
+        held_in_hbm((slots, width), BF16),
         4 * slots * slots * width,
         6 * slots * width,
-    )(mix_high, mix_low, weight, returned, wanted)
+    )(in_hbm(mix_high), in_hbm(mix_low), in_hbm(weight), in_hbm(returned), in_hbm(wanted))
 
 
 def back_in(owner_grad, full, gate_pre, up_pre, ff):
@@ -159,7 +163,7 @@
         jax.ShapeDtypeStruct((2, slots, ff), BF16),
         2 * slots * width * ff,
         2 * width * ff + 2 * slots * width + 12 * slots * ff,
-    )(owner_grad, in_hbm(full), gate_pre, up_pre)
+    )(in_hbm(owner_grad), in_hbm(full), in_hbm(gate_pre), in_hbm(up_pre))
 
 
 def back_out(pre_grad, full, ff):
@@ -180,7 +184,7 @@
             pl.BlockSpec((tall, ff), lambda j: (j, 1)),
         ],
         pl.BlockSpec((slots, tall), lambda j: (0, j)),
-        shape(slots, width, BF16),
+        held_in_hbm((slots, width), BF16),
         4 * slots * width * ff,
         4 * width * ff + 2 * slots * (width + 2 * ff),
     )(pre_grad, in_hbm(full), in_hbm(full))
@@ -211,7 +215,7 @@
         out_shape = [shape(tall // 2, 3 * ff, BF16)] * 2
     else:
         out_specs = pl.BlockSpec((1, tall, 3 * ff), lambda i, names: (i, 0, 0))
-        out_shape = jax.ShapeDtypeStruct((count, tall, 3 * ff), F32)
+        out_shape = held_in_hbm((count, tall, 3 * ff), F32)
     return call(
         body,
         (count,),
@@ -238,22 +242,23 @@
             out_b[:part] = second[0, :part].astype(BF16)
             out_b[part:] = (second[0, part:] + b[...].astype(F32)).astype(BF16)
 
-    came = pl.BlockSpec((part, width), lambda i: (0, 0))
-    sent = pl.BlockSpec((tall, width), lambda i: (0, 0))
-    return call(
-        body,
-        (1,),
+    wide = width // 3
+    came = pl.BlockSpec((part, wide), lambda i: (0, i))
+    sent = pl.BlockSpec((tall, wide), lambda i: (0, i))
+    return call(
+        body,
+        (3,),
         [
             came,
             came,
-            pl.BlockSpec((1, tall, width), lambda i: (at, 0, 0)),
-            pl.BlockSpec((1, tall, width), lambda i: (at + 1, 0, 0)),
+            pl.BlockSpec((1, tall, wide), lambda i: (at, 0, i)),
+            pl.BlockSpec((1, tall, wide), lambda i: (at + 1, 0, i)),
         ],
         [sent, sent],
         [shape(tall, width, BF16)] * 2,
         2 * tall * width,
         16 * tall * width,
-    )(ahead, behind, terms, terms)
+    )(ahead, behind, in_hbm(terms), in_hbm(terms))
 
 
 def last_sum(ahead, behind, terms, at, ff, factor):
@@ -275,7 +280,7 @@
         [jax.ShapeDtypeStruct((tall, 1, ff), F32)] * 3,
         12 * tall * ff,
         36 * tall * ff,
-    )(ahead, behind, terms)
+    )(ahead, behind, in_hbm(terms))
 
 
 def to_tokens(names, came_back):

time: 229 us -> 224 us (0.978)
  local copies, waits for them, and re-layouts: 22.4 us -> 2.85 us
  Pallas kernels: 41.8 us -> 56.3 us
    unnamed x44 -> x8, local copies, waits for them, and re-layouts: 20.6 us -> 1.04 us
    pallas_call x3, Pallas kernels: 3.76 us -> 9.75 us  [add_terms(): call(body, (3,), [came, came, pl.BlockSpec((1, tall, wide), lambda i: (at...]
  transfers between devices with their start and end apart: 17 -> 17, of which waited for: 10 -> 9; matrix products, arithmetic and copies ran while one was open for 6% -> 6% of each run, Pallas kernels for 10% -> 13%
where the time goes in v3:
time: 224 us; the launch traced here: 223 us
  waiting for transfers between devices  98.4 us (44%)
  Pallas kernels  56.3 us (25%)
  starting transfers between devices  40 us (18%)
  between operations  14.1 us (6%)
  matrix products  5.88 us (3%)
  other arithmetic  5.32 us (2%)
  local copies, waits for them, and re-layouts  2.85 us (1%)
    all_to_all x4, waiting for transfers between devices, exchange(): lax.all_to_all(block, 'expert', split_axis=0, concat_axis=0, tiled=True)  45.5 us
    all_gather x1, waiting for transfers between devices, on_device(): full = lax.all_gather(own, 'dp', axis=0, tiled=True)  36.1 us
    all_to_all x4, starting transfers between devices, exchange(): lax.all_to_all(block, 'expert', split_axis=0, concat_axis=0, tiled=True)  26.4 us
    ppermute x8, waiting for transfers between devices, along(): return lax.ppermute(array, 'dp', pairs)  13.9 us
    ppermute x8, starting transfers between devices, along(): return lax.ppermute(array, 'dp', pairs)  13.1 us
    pallas_call x2, Pallas kernels, chip_terms(): call(body, (count,), [column, pair, column, whole] * 2, out_specs, out_sh...  11.2 us
    pallas_call x3, Pallas kernels, add_terms(): call(body, (3,), [came, came, pl.BlockSpec((1, tall, wide), lambda i: (at...  9.75 us
    pallas_call x1, Pallas kernels, project_in(): call(body, (steps,), [pl.BlockSpec((slots, width), lambda j: (0, 0)), pl....  6.43 us
  transfers between devices with their start and end apart: 17, of which 9 were waited for; matrix products, arithmetic and copies ran while one was open for 6% of the time, Pallas kernels for 13%

profile of v3, /device:TPU:2, one launch (start us, length us, event | category | flops | bytes accessed | tf_op | source)
XLA Modules:
  0.0 222.9 jit_solution(12254456219373729829)
XLA Ops:
  7.2 2.1 gather_weights.1
  10.7 1.4 reduce.8
  12.2 2.0 convolution_convert_fusion.1
  14.2 7.5 %all-to-all-start = ((bf16[16,16,2048]{2,1,0:T(8,128)(2,1)}), bf16[16,16,2048]{2,1,0:T(8,128)(2,1)}, u32[]{:S(2)}, u32[]{:S(2)}) async-start(bf16[16,16,2048]{2,1,0:T(8,128)(2,1)} %bitcast.20), calls=%async_computation | async-start | bytes 2097152 | tf_op jit(solution)/shard_map/rows_out/all_to_all | solution.py:18
  24.4 13.1 %all-to-all-done = bf16[16,16,2048]{2,1,0:T(8,128)(2,1)} async-done(((bf16[16,16,2048]{2,1,0:T(8,128)(2,1)}), bf16[16,16,2048]{2,1,0:T(8,128)(2,1)}, u32[]{:S(2)}, u32[]{:S(2)}) %all-to-all-start) | async-done | bytes 1048608 | tf_op jit(solution)/shard_map/rows_out/all_to_all | solution.py:18
  37.5 36.1 %all-gather.2.cloned.1.call-done.wg.wu.wd = bf16[2048,2304]{1,0:T(8,128)(2,1)} async-done(((bf16[128,2304]{1,0:T(8,128)(2,1)}), bf16[2048,2304]{1,0:T(8,128)(2,1)}) %all-gather.2.cloned.1.call-update) | async-done | bytes 9437200 | tf_op jit(solution)/shard_map/gather_weights/all_gather | solution.py:333
  73.7 6.4 %forward.2 = (f32[256,768]{1,0:T(8,128)}, f32[256,768]{1,0:T(8,128)}, bf16[256,768]{1,0:T(8,128)(2,1)S(1)}) custom-call(bf16[256,2048]{1,0:T(8,128)(2,1)} %bitcast.2.x.xa, bf16[2048,2304]{1,0:T(8,128)(2,1)} %all-gather.2.cloned.1.call-done.wg.wu.wd, bf16[2048,2304]{1,0:T(8,128)(2,1)} %all-gather.2.cloned.1.call-done.wg.wu.wd), custom_call_target="tpu_custom_call" | custom-call | flops 1610612736 | bytes 9306112 | tf_op jit(solution)/shard_map/forward/pallas_call | solution.py:82
  80.1 4.5 %forward.3 = bf16[256,2048]{1,0:T(8,128)(2,1)} custom-call(bf16[256,768]{1,0:T(8,128)(2,1)S(1)} %get-tuple-element.18.h.ha, bf16[2048,2304]{1,0:T(8,128)(2,1)} %all-gather.2.cloned.1.call-done.wg.wu.wd), custom_call_target="tpu_custom_call" | custom-call | flops 805306368 | bytes 4587520 | tf_op jit(solution)/shard_map/forward/pallas_call | solution.py:104
  84.6 7.3 %all-to-all-start.1 = ((bf16[16,16,2048]{2,1,0:T(8,128)(2,1)}), bf16[16,16,2048]{2,1,0:T(8,128)(2,1)}, u32[]{:S(2)}, u32[]{:S(2)}) async-start(bf16[16,16,2048]{2,1,0:T(8,128)(2,1)} %bitcast.19), calls=%async_computation.1 | async-start | bytes 2097152 | tf_op jit(solution)/shard_map/combine/all_to_all | solution.py:18
  92.7 1.6 broadcast_select_fusion.w
  94.3 3.9 %convolution_convert_fusion.goal = bf16[256,2048]{1,0:T(8,128)(2,1)} fusion(bf16[768,2048]{1,0:T(8,128)(2,1)} %param.10, s32[256]{0:T(256)S(1)} %eq.37, pred[256]{0:T(512)(128)(4,1)S(1)} %lt.49), kind=kOutput, calls=%fused_computation | convolution fusion | flops 806223872 | bytes 4195584 | tf_op jit(solution)/shard_map/rows_out/dot_general | solution.py:22
  98.2 10.0 %all-to-all-done.1 = bf16[16,16,2048]{2,1,0:T(8,128)(2,1)} async-done(((bf16[16,16,2048]{2,1,0:T(8,128)(2,1)}), bf16[16,16,2048]{2,1,0:T(8,128)(2,1)}, u32[]{:S(2)}, u32[]{:S(2)}) %all-to-all-start.1) | async-done | bytes 1048608 | tf_op jit(solution)/shard_map/combine/all_to_all | solution.py:18
  108.2 4.2 %combine.1 = bf16[256,2048]{1,0:T(8,128)(2,1)} custom-call(bf16[256,256]{1,0:T(8,128)(2,1)} %get-tuple-element.35.high, bf16[256,256]{1,0:T(8,128)(2,1)} %get-tuple-element.34.low, f32[256,1]{1,0:T(8,128)} %broadcast_select_fusion.w, bf16[256,2048]{1,0:T(8,128)(2,1)} %bitcast.7.back, bf16[256,2048]{1,0:T(8,128)(2,1)} %convolution_convert_fusion.goal), custom_call_target="tpu_custom_call" | custom-call | flops 536870912 | bytes 3145728 | tf_op jit(solution)/shard_map/combine/pallas_call | solution.py:129
  112.5 5.8 %all-to-all-start.2 = ((bf16[16,16,2048]{2,1,0:T(8,128)(2,1)}), bf16[16,16,2048]{2,1,0:T(8,128)(2,1)}, u32[]{:S(2)}, u32[]{:S(2)}) async-start(bf16[16,16,2048]{2,1,0:T(8,128)(2,1)} %bitcast.18), calls=%async_computation.2 | async-start | bytes 2097152 | tf_op jit(solution)/shard_map/combine/all_to_all | solution.py:18
  118.3 15.2 %all-to-all-done.2 = bf16[16,16,2048]{2,1,0:T(8,128)(2,1)} async-done(((bf16[16,16,2048]{2,1,0:T(8,128)(2,1)}), bf16[16,16,2048]{2,1,0:T(8,128)(2,1)}, u32[]{:S(2)}, u32[]{:S(2)}) %all-to-all-start.2) | async-done | bytes 1048608 | tf_op jit(solution)/shard_map/combine/all_to_all | solution.py:18
  133.5 5.1 %backward.1.x.pa = bf16[2,256,768]{2,1,0:T(8,128)(2,1)} custom-call(bf16[256,2048]{1,0:T(8,128)(2,1)} %bitcast.9.x.oa, bf16[2048,2304]{1,0:T(8,128)(2,1)} %all-gather.2.cloned.1.call-done.wg.wu.wd, f32[256,768]{1,0:T(8,128)} %get-tuple-element.19.gate_ref, f32[256,768]{1,0:T(8,128)} %get-tuple-element.20.up_ref), custom_call_target="tpu_custom_call" | custom-call | flops 805306368 | bytes 6553600 | tf_op jit(solution)/shard_map/backward/pallas_call | solution.py:153
  139.1 2.5 %collective-permute-done.3.hb = bf16[256,768]{1,0:T(8,128)(2,1)} collective-permute-done((bf16[256,768]{1,0:T(8,128)(2,1)S(1)}, bf16[256,768]{1,0:T(8,128)(2,1)}, u32[]{:S(2)}, u32[]{:S(2)}) %collective-permute-start.3) | collective-permute-done | bytes 393248 | tf_op jit(solution)/shard_map/forward/ppermute | solution.py:329
  141.9 2.1 weight_gradients.6
  144.1 3.2 %collective-permute-start.5 = (bf16[64,2304]{1,0:T(8,128)(2,1)S(1)}, bf16[64,2304]{1,0:T(8,128)(2,1)S(1)}, u32[]{:S(2)}, u32[]{:S(2)}) collective-permute-start(bf16[64,2304]{1,0:T(8,128)(2,1)S(1)} %get-tuple-element.22), channel_id=1, source_target_pairs={{0,224},{16,240},{32,0},{48,16},{64,32},{80,48},{96,64},{112,80},{... | collective-permute-start | bytes 884744 | tf_op jit(solution)/shard_map/weight_gradients/ppermute | solution.py:326
  147.4 9.2 %weight_gradients.7.first.second.mine = f32[7,128,2304]{2,1,0:T(8,128)} custom-call(s32[7]{0:T(128)S(1)} %slice.7.names, bf16[256,2048]{1,0:T(8,128)(2,1)} %bitcast.2.x.xa, bf16[2,256,768]{2,1,0:T(8,128)(2,1)} %backward.1.x.pa, bf16[256,2048]{1,0:T(8,128)(2,1)} %bitcast.9.x.oa, bf16[256,768]{1,0:T(8,128)(2,1)S(1)} %get-tuple-element.18.h.ha, ...), custom_call_target="tpu_custom_call" | custom-call | flops 2113929216 | bytes 12451840 | tf_op jit(solution)/shard_map/weight_gradients/pallas_call | solution.py:219
  156.6 2.5 %weight_gradients.8 = (bf16[128,2304]{1,0:T(8,128)(2,1)S(1)}, bf16[128,2304]{1,0:T(8,128)(2,1)S(1)}) custom-call(bf16[64,2304]{1,0:T(8,128)(2,1)S(1)} %collective-permute-done.4.a, bf16[64,2304]{1,0:T(8,128)(2,1)S(1)} %collective-permute-done.5.b, f32[7,128,2304]{2,1,0:T(8,128)} %weight_gradients.7.first.second.mine, ...), custom_call_target="tpu_custom_call" | custom-call | flops 589824 | bytes 4718592 | tf_op jit(solution)/shard_map/weight_gradients/pallas_call | solution.py:248
  159.2 3.2 %collective-permute-start.7 = (bf16[128,2304]{1,0:T(8,128)(2,1)S(1)}, bf16[128,2304]{1,0:T(8,128)(2,1)S(1)}, u32[]{:S(2)}, u32[]{:S(2)}) collective-permute-start(bf16[128,2304]{1,0:T(8,128)(2,1)S(1)} %get-tuple-element.24), channel_id=1, source_target_pairs={{0,224},{16,240},{32,0},{48,16},{64,32},{80,48},{96,64},{112,80},{... | collective-permute-start | bytes 1769480 | tf_op jit(solution)/shard_map/weight_gradients/ppermute | solution.py:326
  162.4 13.0 %collective-permute-done.6.a = bf16[128,2304]{1,0:T(8,128)(2,1)S(1)} collective-permute-done((bf16[128,2304]{1,0:T(8,128)(2,1)S(1)}, bf16[128,2304]{1,0:T(8,128)(2,1)S(1)}, u32[]{:S(2)}, u32[]{:S(2)}) %collective-permute-start.6) | collective-permute-done | bytes 589856 | tf_op jit(solution)/shard_map/weight_gradients/ppermute | solution.py:326
  175.4 3.5 %weight_gradients.9 = (bf16[128,2304]{1,0:T(8,128)(2,1)}, bf16[128,2304]{1,0:T(8,128)(2,1)}) custom-call(bf16[128,2304]{1,0:T(8,128)(2,1)S(1)} %collective-permute-done.6.a, bf16[128,2304]{1,0:T(8,128)(2,1)S(1)} %collective-permute-done.7.b, f32[7,128,2304]{2,1,0:T(8,128)} %weight_gradients.7.first.second.mine, f32[7,128,2304]{2,1,0:T(8,128)} %weight_gradients.7.first.second.mine), custom_call_target="tpu_custom_call" | custom-call | flops 589824 | bytes 4718592 | tf_op jit(solution)/shard_map/weight_gradients/pallas_call | solution.py:248
  178.9 3.2 %collective-permute-start.9 = (bf16[128,2304]{1,0:T(8,128)(2,1)}, bf16[128,2304]{1,0:T(8,128)(2,1)}, u32[]{:S(2)}, u32[]{:S(2)}) collective-permute-start(bf16[128,2304]{1,0:T(8,128)(2,1)} %get-tuple-element.26), channel_id=1, source_target_pairs={{0,224},{16,240},{32,0},{48,16},{64,32},{80,48},{96,64},{112,80},{... | collective-permute-start | bytes 1769480 | tf_op jit(solution)/shard_map/weight_gradients/ppermute | solution.py:326
  182.1 5.8 %token_gradient.2 = bf16[256,2048]{1,0:T(8,128)(2,1)} custom-call(bf16[2,256,768]{2,1,0:T(8,128)(2,1)} %backward.1.x.pa, bf16[2048,2304]{1,0:T(8,128)(2,1)} %all-gather.2.cloned.1.call-done.wg.wu.wd, bf16[2048,2304]{1,0:T(8,128)(2,1)} %all-gather.2.cloned.1.call-done.wg.wu.wd), custom_call_target="tpu_custom_call" | custom-call | flops 1610612736 | bytes 8126464 | tf_op jit(solution)/shard_map/token_gradient/pallas_call | solution.py:178
  187.9 5.8 %all-to-all-start.3 = ((bf16[16,16,2048]{2,1,0:T(8,128)(2,1)}), bf16[16,16,2048]{2,1,0:T(8,128)(2,1)}, u32[]{:S(2)}, u32[]{:S(2)}) async-start(bf16[16,16,2048]{2,1,0:T(8,128)(2,1)} %bitcast.17), calls=%async_computation.3 | async-start | bytes 2097152 | tf_op jit(solution)/shard_map/token_gradient/all_to_all | solution.py:18
  194.6 3.8 %weight_gradients.10 = (bf16[128,2304]{1,0:T(8,128)(2,1)}, bf16[128,2304]{1,0:T(8,128)(2,1)}) custom-call(bf16[128,2304]{1,0:T(8,128)(2,1)} %collective-permute-done.8.a, bf16[128,2304]{1,0:T(8,128)(2,1)} %collective-permute-done.9.b, f32[7,128,2304]{2,1,0:T(8,128)} %weight_gradients.7.first.second.mine, f32[7,128,2304]{2,1,0:T(8,128)} %weight_gradients.7.first.second.mine), custom_call_target="tpu_custom_call" | custom-call | flops 589824 | bytes 4718592 | tf_op jit(solution)/shard_map/weight_gradients/pallas_call | solution.py:248
  199.1 2.4 %collective-permute-start.11 = (bf16[128,2304]{1,0:T(8,128)(2,1)}, bf16[128,2304]{1,0:T(8,128)(2,1)}, u32[]{:S(2)}, u32[]{:S(2)}) collective-permute-start(bf16[128,2304]{1,0:T(8,128)(2,1)} %get-tuple-element.28), channel_id=1, source_target_pairs={{0,224},{16,240},{32,0},{48,16},{64,32},{80,48},{96,64},{112,80},{... | collective-permute-start | bytes 1769480 | tf_op jit(solution)/shard_map/weight_gradients/ppermute | solution.py:326
  201.7 7.1 %all-to-all-done.3 = bf16[16,16,2048]{2,1,0:T(8,128)(2,1)} async-done(((bf16[16,16,2048]{2,1,0:T(8,128)(2,1)}), bf16[16,16,2048]{2,1,0:T(8,128)(2,1)}, u32[]{:S(2)}, u32[]{:S(2)}) %all-to-all-start.3) | async-done | bytes 1048608 | tf_op jit(solution)/shard_map/token_gradient/all_to_all | solution.py:18
  208.8 4.4 %token_gradient.3 = bf16[768,2048]{1,0:T(8,128)(2,1)} custom-call(bf16[768,256]{1,0:T(8,128)(2,1)S(1)} %fusion.which, bf16[256,2048]{1,0:T(8,128)(2,1)} %bitcast.11.back), custom_call_target="tpu_custom_call" | custom-call | flops 805306368 | bytes 4194304 | tf_op jit(solution)/shard_map/token_gradient/pallas_call | solution.py:294
  213.2 2.8 %weight_gradients.11 = (f32[128,1,768]{2,1,0:T(1,128)}, f32[128,1,768]{2,1,0:T(1,128)}, f32[128,1,768]{2,1,0:T(1,128)}) custom-call(bf16[128,2304]{1,0:T(8,128)(2,1)} %collective-permute-done.10.a, bf16[128,2304]{1,0:T(8,128)(2,1)} %collective-permute-done.11.b, f32[7,128,2304]{2,1,0:T(8,128)} %weight_gradients.7.first.second.mine), custom_call_target="tpu_custom_call" | custom-call | flops 1179648 | bytes 3538944 | tf_op jit(solution)/shard_map/weight_gradients/pallas_call | solution.py:275
  (40 shorter events, 8.0 us)
Async XLA Ops:
  7.2 5.0 %copy-start = (bf16[768,2048]{1,0:T(8,128)(2,1)S(1)}, bf16[768,2048]{1,0:T(8,128)(2,1)}, u32[]{:S(2)}) copy-start(bf16[768,2048]{1,0:T(8,128)(2,1)} %param.9) | copy-start | bytes 9437188
  7.2 66.5 %all-gather.2.cloned.1.call-start = ((), (), s32[]{:S(2)}) async-start(), calls=%async_computation.4 | async-start | bytes 10027008 | tf_op jit(solution)/shard_map/gather_weights/all_gather | solution.py:333
  12.1 10.7 %copy-start.1 = (f32[1,16,1,16]{3,2,1,0:T(1,128)S(1)}, f32[1,16,1,16]{3,2,1,0:T(1,128)}, u32[]{:S(2)}) copy-start(f32[1,16,1,16]{3,2,1,0:T(1,128)} %param.13) | copy-start | bytes 3076
  14.2 23.4 %all-to-all-start = ((bf16[16,16,2048]{2,1,0:T(8,128)(2,1)}), bf16[16,16,2048]{2,1,0:T(8,128)(2,1)}, u32[]{:S(2)}, u32[]{:S(2)}) async-start(bf16[16,16,2048]{2,1,0:T(8,128)(2,1)} %bitcast.20), calls=%async_computation | async-start | bytes 2097152 | tf_op jit(solution)/shard_map/rows_out/all_to_all | solution.py:18
  84.6 23.6 %all-to-all-start.1 = ((bf16[16,16,2048]{2,1,0:T(8,128)(2,1)}), bf16[16,16,2048]{2,1,0:T(8,128)(2,1)}, u32[]{:S(2)}, u32[]{:S(2)}) async-start(bf16[16,16,2048]{2,1,0:T(8,128)(2,1)} %bitcast.19), calls=%async_computation.1 | async-start | bytes 2097152 | tf_op jit(solution)/shard_map/combine/all_to_all | solution.py:18
  112.5 21.1 %all-to-all-start.2 = ((bf16[16,16,2048]{2,1,0:T(8,128)(2,1)}), bf16[16,16,2048]{2,1,0:T(8,128)(2,1)}, u32[]{:S(2)}, u32[]{:S(2)}) async-start(bf16[16,16,2048]{2,1,0:T(8,128)(2,1)} %bitcast.18), calls=%async_computation.2 | async-start | bytes 2097152 | tf_op jit(solution)/shard_map/combine/all_to_all | solution.py:18
  118.3 20.8 %collective-permute-start = (bf16[256,2048]{1,0:T(8,128)(2,1)}, bf16[256,2048]{1,0:T(8,128)(2,1)}, u32[]{:S(2)}, u32[]{:S(2)}) collective-permute-start(bf16[256,2048]{1,0:T(8,128)(2,1)} %bitcast.2.x.xa), channel_id=1, source_target_pairs={{0,16},{16,0},{32,48},{48,32},{64,80},{80,64},{96,112},{112,96},{1... | collective-permute-start | bytes 3145736 | tf_op jit(solution)/shard_map/rows_out/ppermute | solution.py:329
  133.5 8.4 %collective-permute-start.2 = (bf16[256,2048]{1,0:T(8,128)(2,1)}, bf16[256,2048]{1,0:T(8,128)(2,1)}, u32[]{:S(2)}, u32[]{:S(2)}) collective-permute-start(bf16[256,2048]{1,0:T(8,128)(2,1)} %bitcast.9.x.oa), channel_id=1, source_target_pairs={{0,16},{16,0},{32,48},{48,32},{64,80},{80,64},{96,112},{112,96},{1... | collective-permute-start | bytes 3145736 | tf_op jit(solution)/shard_map/combine/ppermute | solution.py:329
  133.5 5.6 %copy-start.2 = (s32[8]{0:T(128)S(1)}, s32[8]{0:T(128)}, u32[]{:S(2)}) copy-start(s32[8]{0:T(128)} %constant.36.clone) | copy-start | bytes 100
  138.6 3.3 %collective-permute-start.1 = (bf16[2,256,768]{2,1,0:T(8,128)(2,1)}, bf16[2,256,768]{2,1,0:T(8,128)(2,1)}, u32[]{:S(2)}, u32[]{:S(2)}) collective-permute-start(bf16[2,256,768]{2,1,0:T(8,128)(2,1)} %backward.1.x.pa), channel_id=1, source_target_pairs={{0,16},{16,0},{32,48},{48,32},{64,80},{80,64},{96,112},{112,96},{1... | collective-permute-start | bytes 2359304 | tf_op jit(solution)/shard_map/backward/ppermute | solution.py:329
  139.1 2.5 %collective-permute-start.3 = (bf16[256,768]{1,0:T(8,128)(2,1)S(1)}, bf16[256,768]{1,0:T(8,128)(2,1)}, u32[]{:S(2)}, u32[]{:S(2)}) collective-permute-start(bf16[256,768]{1,0:T(8,128)(2,1)S(1)} %get-tuple-element.18.h.ha), channel_id=1, source_target_pairs={{0,16},{16,0},{32,48},{48,32},{64,80},{80,64},{96,112},{112,96},{1... | collective-permute-start | bytes 1179656 | tf_op jit(solution)/shard_map/forward/ppermute | solution.py:329
  144.0 12.6 %collective-permute-start.4 = (bf16[64,2304]{1,0:T(8,128)(2,1)S(1)}, bf16[64,2304]{1,0:T(8,128)(2,1)S(1)}, u32[]{:S(2)}, u32[]{:S(2)}) collective-permute-start(bf16[64,2304]{1,0:T(8,128)(2,1)S(1)} %get-tuple-element.21), channel_id=1, source_target_pairs={{0,32},{16,48},{32,64},{48,80},{64,96},{80,112},{96,128},{112,144}... | collective-permute-start | bytes 884744 | tf_op jit(solution)/shard_map/weight_gradients/ppermute | solution.py:326
  144.1 12.5 %collective-permute-start.5 = (bf16[64,2304]{1,0:T(8,128)(2,1)S(1)}, bf16[64,2304]{1,0:T(8,128)(2,1)S(1)}, u32[]{:S(2)}, u32[]{:S(2)}) collective-permute-start(bf16[64,2304]{1,0:T(8,128)(2,1)S(1)} %get-tuple-element.22), channel_id=1, source_target_pairs={{0,224},{16,240},{32,0},{48,16},{64,32},{80,48},{96,64},{112,80},{... | collective-permute-start | bytes 884744 | tf_op jit(solution)/shard_map/weight_gradients/ppermute | solution.py:326
  159.1 16.3 %collective-permute-start.6 = (bf16[128,2304]{1,0:T(8,128)(2,1)S(1)}, bf16[128,2304]{1,0:T(8,128)(2,1)S(1)}, u32[]{:S(2)}, u32[]{:S(2)}) collective-permute-start(bf16[128,2304]{1,0:T(8,128)(2,1)S(1)} %get-tuple-element.23), channel_id=1, source_target_pairs={{0,32},{16,48},{32,64},{48,80},{64,96},{80,112},{96,128},{112,144}... | collective-permute-start | bytes 1769480 | tf_op jit(solution)/shard_map/weight_gradients/ppermute | solution.py:326
  159.2 16.2 %collective-permute-start.7 = (bf16[128,2304]{1,0:T(8,128)(2,1)S(1)}, bf16[128,2304]{1,0:T(8,128)(2,1)S(1)}, u32[]{:S(2)}, u32[]{:S(2)}) collective-permute-start(bf16[128,2304]{1,0:T(8,128)(2,1)S(1)} %get-tuple-element.24), channel_id=1, source_target_pairs={{0,224},{16,240},{32,0},{48,16},{64,32},{80,48},{96,64},{112,80},{... | collective-permute-start | bytes 1769480 | tf_op jit(solution)/shard_map/weight_gradients/ppermute | solution.py:326
  178.9 15.7 %collective-permute-start.8 = (bf16[128,2304]{1,0:T(8,128)(2,1)}, bf16[128,2304]{1,0:T(8,128)(2,1)}, u32[]{:S(2)}, u32[]{:S(2)}) collective-permute-start(bf16[128,2304]{1,0:T(8,128)(2,1)} %get-tuple-element.25), channel_id=1, source_target_pairs={{0,32},{16,48},{32,64},{48,80},{64,96},{80,112},{96,128},{112,144}... | collective-permute-start | bytes 1769480 | tf_op jit(solution)/shard_map/weight_gradients/ppermute | solution.py:326
  178.9 15.7 %collective-permute-start.9 = (bf16[128,2304]{1,0:T(8,128)(2,1)}, bf16[128,2304]{1,0:T(8,128)(2,1)}, u32[]{:S(2)}, u32[]{:S(2)}) collective-permute-start(bf16[128,2304]{1,0:T(8,128)(2,1)} %get-tuple-element.26), channel_id=1, source_target_pairs={{0,224},{16,240},{32,0},{48,16},{64,32},{80,48},{96,64},{112,80},{... | collective-permute-start | bytes 1769480 | tf_op jit(solution)/shard_map/weight_gradients/ppermute | solution.py:326
  187.9 20.9 %all-to-all-start.3 = ((bf16[16,16,2048]{2,1,0:T(8,128)(2,1)}), bf16[16,16,2048]{2,1,0:T(8,128)(2,1)}, u32[]{:S(2)}, u32[]{:S(2)}) async-start(bf16[16,16,2048]{2,1,0:T(8,128)(2,1)} %bitcast.17), calls=%async_computation.3 | async-start | bytes 2097152 | tf_op jit(solution)/shard_map/token_gradient/all_to_all | solution.py:18
  198.3 14.9 %collective-permute-start.10 = (bf16[128,2304]{1,0:T(8,128)(2,1)}, bf16[128,2304]{1,0:T(8,128)(2,1)}, u32[]{:S(2)}, u32[]{:S(2)}) collective-permute-start(bf16[128,2304]{1,0:T(8,128)(2,1)} %get-tuple-element.27), channel_id=1, source_target_pairs={{0,32},{16,48},{32,64},{48,80},{64,96},{80,112},{96,128},{112,144}... | collective-permute-start | bytes 1769480 | tf_op jit(solution)/shard_map/weight_gradients/ppermute | solution.py:326
  199.1 14.1 %collective-permute-start.11 = (bf16[128,2304]{1,0:T(8,128)(2,1)}, bf16[128,2304]{1,0:T(8,128)(2,1)}, u32[]{:S(2)}, u32[]{:S(2)}) collective-permute-start(bf16[128,2304]{1,0:T(8,128)(2,1)} %get-tuple-element.28), channel_id=1, source_target_pairs={{0,224},{16,240},{32,0},{48,16},{64,32},{80,48},{96,64},{112,80},{... | collective-permute-start | bytes 1769480 | tf_op jit(solution)/shard_map/weight_gradients/ppermute | solution.py:326
Sparse Core Ops, SparseCore 0:
  9.8 63.7 all-gather.1

commit v4 on v3

v4 whole, which is shorter than its diff:
```python
import jax
import jax.numpy as jnp
from jax import lax
from jax.experimental import pallas as pl
from jax.experimental.pallas import tpu as pltpu
from jax.sharding import PartitionSpec as P

F32 = jnp.float32
BF16 = jnp.bfloat16
ROW_BY_ROW = ((1,), (0,))
OVER_LAST = ((1,), (1,))
OVER_FIRST = ((0,), (0,))
MIB = 1024 * 1024
VMEM_LIMIT = 24 * MIB


def exchange(block):
    return lax.all_to_all(block, "expert", split_axis=0, concat_axis=0, tiled=True)


def dot(a, b, dims):
    return lax.dot_general(a, b, (dims, ((), ())), preferred_element_type=F32)


def in_hbm(array):
    return pltpu.with_memory_space_constraint(array, pltpu.HBM)


def held_in_hbm(dims, dtype):
    return pltpu.HBM(dims, dtype)


def call(body, grid, in_specs, out_specs, out_shape, flops, moved, prefetch=0, scratch=()):
    return pl.pallas_call(
        body,
        grid_spec=pltpu.PrefetchScalarGridSpec(
            num_scalar_prefetch=prefetch,
            grid=grid,
            in_specs=in_specs,
            out_specs=out_specs,
            scratch_shapes=list(scratch),
        ),
        out_shape=out_shape,
        compiler_params=pltpu.CompilerParams(vmem_limit_bytes=VMEM_LIMIT),
        cost_estimate=pl.CostEstimate(flops=flops, bytes_accessed=moved, transcendentals=0),
    )


def side_by_side(gate_weight, up_weight, down_weight):
    tall, ff = gate_weight.shape

    def body(g, u, d, out, done):
        copies = [
            pltpu.make_async_copy(part, out.at[:, pl.ds(i * ff, ff)], done.at[i])
            for i, part in enumerate((g, u, d))
        ]
        for copy in copies:
            copy.start()
        for copy in copies:
            copy.wait()

    place = pl.BlockSpec(memory_space=pltpu.HBM)
    return pl.pallas_call(
        body,
        in_specs=[place] * 3,
        out_specs=place,
        out_shape=shape(tall, 3 * ff, BF16),
        scratch_shapes=[pltpu.SemaphoreType.DMA((3,))],
        compiler_params=pltpu.CompilerParams(vmem_limit_bytes=VMEM_LIMIT),
        cost_estimate=pl.CostEstimate(flops=0, bytes_accessed=12 * tall * ff, transcendentals=0),
    )(gate_weight, up_weight, down_weight)


def shape(rows, columns, dtype):
    return jax.ShapeDtypeStruct((rows, columns), dtype)


def add_up(total, step, term):
    @pl.when(step == 0)
    def _():
        total[...] = term

    @pl.when(step > 0)
    def _():
        total[...] += term


def project_in(rows, full, ff):
    slots, width = rows.shape
    tall = 1024
    steps = width // tall

    def body(x, w, pre, hidden, total):
        step = pl.program_id(0)
        add_up(total, step, dot(x[...], w[...], ROW_BY_ROW))

        @pl.when(step == steps - 1)
        def _():
            g, u = total[:, :ff], total[:, ff:]
            pre[...] = total[...]
            hidden[...] = (g * jax.nn.sigmoid(g) * u).astype(BF16)

    return call(
        body,
        (steps,),
        [
            pl.BlockSpec((slots, tall), lambda j: (0, j)),
            pl.BlockSpec((tall, 2 * ff), lambda j: (j, 0)),
        ],
        [pl.BlockSpec((slots, 2 * ff), lambda j: (0, 0)), pl.BlockSpec((slots, ff), lambda j: (0, 0))],
        [shape(slots, 2 * ff, F32), shape(slots, ff, BF16)],
        4 * slots * width * ff,
        4 * width * ff + 2 * slots * width + 10 * slots * ff,
        scratch=[pltpu.VMEM((slots, 2 * ff), F32)],
    )(in_hbm(rows), in_hbm(full))


def project_out(hidden, full, ff):
    slots, width = hidden.shape[0], full.shape[0]
    tall = 1024

    def body(h, wd, out):
        out[...] = dot(h[...], wd[...], OVER_LAST).astype(BF16)

    return call(
        body,
        (width // tall,),
        [
            pl.BlockSpec((slots, ff), lambda j: (0, 0)),
            pl.BlockSpec((tall, ff), lambda j: (j, 2)),
        ],
        pl.BlockSpec((slots, tall), lambda j: (0, j)),
        held_in_hbm((slots, width), BF16),
        2 * slots * width * ff,
        2 * width * ff + 2 * slots * (width + ff),
    )(hidden, in_hbm(full))


def combine(mix_high, mix_low, weight, returned, wanted):
    slots, width = returned.shape
    wide = width

    def body(high, low, w, back, goal, out):
        x = back[...]
        total = dot(high[...], x, ROW_BY_ROW) + dot(low[...], x, ROW_BY_ROW)
        out[...] = (w[...] * (total - goal[...].astype(F32))).astype(BF16)

    mix = pl.BlockSpec((slots, slots), lambda j: (0, 0))
    part = pl.BlockSpec((slots, wide), lambda j: (0, j))
    return call(
        body,
        (width // wide,),
        [mix, mix, pl.BlockSpec((slots, 1), lambda j: (0, 0)), part, part],
        part,
        held_in_hbm((slots, width), BF16),
        4 * slots * slots * width,
        6 * slots * width,
    )(in_hbm(mix_high), in_hbm(mix_low), in_hbm(weight), in_hbm(returned), in_hbm(wanted))


def back_in(owner_grad, full, pre, ff):
    slots, width = owner_grad.shape
    tall = 1024
    steps = width // tall

    def body(x, w, pre_ref, out, total):
        step = pl.program_id(0)
        add_up(total, step, dot(x[...], w[...], ROW_BY_ROW))

        @pl.when(step == steps - 1)
        def _():
            h, g = total[...], pre_ref[:, :ff]
            sig = jax.nn.sigmoid(g)
            out[0] = (h * pre_ref[:, ff:] * sig * (1.0 + g * (1.0 - sig))).astype(BF16)
            out[1] = (h * (g * sig)).astype(BF16)

    return call(
        body,
        (steps,),
        [
            pl.BlockSpec((slots, tall), lambda j: (0, j)),
            pl.BlockSpec((tall, ff), lambda j: (j, 2)),
            pl.BlockSpec((slots, 2 * ff), lambda j: (0, 0)),
        ],
        pl.BlockSpec((2, slots, ff), lambda j: (0, 0, 0)),
        jax.ShapeDtypeStruct((2, slots, ff), BF16),
        2 * slots * width * ff,
        2 * width * ff + 2 * slots * width + 12 * slots * ff,
        scratch=[pltpu.VMEM((slots, ff), F32)],
    )(in_hbm(owner_grad), in_hbm(full), in_hbm(pre))


def back_out(pre_grad, full, ff):
    slots, width = pre_grad.shape[1], full.shape[0]
    tall = 1024

    def body(x, wg, wu, out):
        out[...] = (
            dot(x[0], wg[...], OVER_LAST) + dot(x[1], wu[...], OVER_LAST)
        ).astype(BF16)

    return call(
        body,
        (width // tall,),
        [
            pl.BlockSpec((2, slots, ff), lambda j: (0, 0, 0)),
            pl.BlockSpec((tall, ff), lambda j: (j, 0)),
            pl.BlockSpec((tall, ff), lambda j: (j, 1)),
        ],
        pl.BlockSpec((slots, tall), lambda j: (0, j)),
        held_in_hbm((slots, width), BF16),
        4 * slots * width * ff,
        4 * width * ff + 2 * slots * (width + 2 * ff),
    )(pre_grad, in_hbm(full), in_hbm(full))


def chip_terms(blocks, own, other, halves):
    count = blocks.shape[0]
    slots, ff = own[3].shape
    tall = 128
    rows = tall // 2 if halves else tall
    dtype = BF16 if halves else F32

    def body(names, *refs):
        columns, outs = refs[: 4 * count], refs[4 * count + 4 :]
        pre_own, hidden_own, pre_other, hidden_other = refs[4 * count : 4 * count + 4]
        xa, oa, xb, ob = (
            jnp.concatenate([r[...] for r in columns[i * count : (i + 1) * count]], axis=1)
            for i in range(4)
        )
        gate = dot(xa, pre_own[0], OVER_FIRST) + dot(xb, pre_other[0], OVER_FIRST)
        up = dot(xa, pre_own[1], OVER_FIRST) + dot(xb, pre_other[1], OVER_FIRST)
        down = dot(oa, hidden_own[...], OVER_FIRST) + dot(ob, hidden_other[...], OVER_FIRST)
        for at, part in ((0, gate), (ff, up), (2 * ff, down)):
            for i, out in enumerate(outs):
                out[:, at : at + ff] = part[i * rows : (i + 1) * rows].astype(dtype)

    columns = [pl.BlockSpec((slots, tall), lambda i, names, k=k: (0, names[k])) for k in range(count)]
    pair = pl.BlockSpec((2, slots, ff), lambda i, names: (0, 0, 0))
    whole = pl.BlockSpec((slots, ff), lambda i, names: (0, 0))
    number = 2 if halves else count
    sums = pl.BlockSpec((rows, 3 * ff), lambda i, names: (0, 0))
    return call(
        body,
        (1,),
        columns * 4 + [pair, whole] * 2,
        [sums] * number,
        [shape(rows, 3 * ff, dtype)] * number,
        12 * count * slots * tall * ff,
        12 * slots * ff + count * (8 * slots * tall + 12 * tall * ff),
        prefetch=1,
    )(
        blocks,
        *[array for side in (own, other) for array in (side[0], side[2]) for _ in range(count)],
        *(own[1], own[3], other[1], other[3]),
    )


def add_term(came, term, last_rows=False):
    tall, width = term.shape
    part = came.shape[0]
    first = tall - part if last_rows else 0

    def body(a, mine, out):
        if part < tall:
            out[...] = mine[...].astype(BF16)
        out[first : first + part] = (mine[first : first + part] + a[...].astype(F32)).astype(BF16)

    return call(
        body,
        (1,),
        [
            pl.BlockSpec((part, width), lambda i: (0, 0)),
            pl.BlockSpec((tall, width), lambda i: (0, 0)),
        ],
        pl.BlockSpec((tall, width), lambda i: (0, 0)),
        shape(tall, width, BF16),
        tall * width,
        8 * tall * width,
    )(came, term)


def last_sum(ahead, behind, term, ff, factor):
    tall = ahead.shape[0]

    def body(a, b, mine, gate, up, down):
        total = (a[...].astype(F32) + b[...].astype(F32) + mine[...]) * factor
        gate[:, 0, :] = total[:, :ff]
        up[:, 0, :] = total[:, ff : 2 * ff]
        down[:, 0, :] = total[:, 2 * ff :]

    came = pl.BlockSpec((tall, 3 * ff), lambda i: (0, 0))
    part = pl.BlockSpec((tall, 1, ff), lambda i: (0, 0, 0))
    return call(
        body,
        (1,),
        [came] * 3,
        [part] * 3,
        [jax.ShapeDtypeStruct((tall, 1, ff), F32)] * 3,
        12 * tall * ff,
        36 * tall * ff,
    )(ahead, behind, term)


def to_tokens(names, came_back):
    held, slots = names.shape
    width = came_back.shape[1]
    wide = 1024

    def body(which, back, out):
        out[...] = dot(which[...], back[...], ROW_BY_ROW).astype(BF16)

    return call(
        body,
        (width // wide,),
        [
            pl.BlockSpec((held, slots), lambda j: (0, 0)),
            pl.BlockSpec((slots, wide), lambda j: (0, j)),
        ],
        pl.BlockSpec((held, wide), lambda j: (0, j)),
        shape(held, width, BF16),
        2 * held * slots * width,
        2 * (held + slots) * width,
    )(names, came_back)


def on_device(
    tokens, target, route_index, route_count, route_gate, gate_weight, up_weight, down_weight
):
    groups = lax.axis_size("dp")
    sources = lax.axis_size("expert")
    chips = groups // 2
    local_index = route_index[0, :, 0, :]
    live_count = route_count[0, :, 0]
    per_source = local_index.shape[1]
    held, width = tokens.shape
    tall = gate_weight.shape[0]
    ff = gate_weight.shape[2]
    slots = sources * per_source

    def along(array, by):
        pairs = [
            (2 * z + c, 2 * ((z + by) % chips) + c) for z in range(chips) for c in range(2)
        ]
        return lax.ppermute(array, "dp", pairs)

    def other_core(array):
        return lax.ppermute(array, "dp", [(d, d ^ 1) for d in range(groups)])

    with jax.named_scope("gather_weights"):
        own = side_by_side(gate_weight[:, 0], up_weight[:, 0], down_weight[:, 0])
        full = lax.all_gather(own, "dp", axis=0, tiled=True)

    with jax.named_scope("routing"):
        usable = jnp.arange(per_source, dtype=jnp.int32)[None, :] < live_count[:, None]
        flat_index = local_index.reshape(slots)
        live = usable.reshape(slots)
        weight = jnp.where(live, route_gate[0, :, 0, :].reshape(slots), 0.0)
        names = flat_index[:, None] == jnp.arange(held, dtype=jnp.int32)[None, :]
        pick = (names & live[:, None]).astype(BF16)
        same = flat_index[:, None] == flat_index[None, :]
        high = lax.reduce_precision(weight, 8, 7)
        low = weight - high
        mix_high = jnp.where(same, high[None, :], 0.0).astype(BF16)
        mix_low = jnp.where(same, low[None, :], 0.0).astype(BF16)

    with jax.named_scope("rows_out"):
        rows = dot(pick, tokens, ROW_BY_ROW).astype(BF16)
        expert_rows = exchange(rows.reshape(sources, per_source, width)).reshape(slots, width)
        other_rows = other_core(expert_rows)
        wanted = dot(pick, target, ROW_BY_ROW).astype(BF16)

    with jax.named_scope("forward"):
        pre, hidden = project_in(expert_rows, full, ff)
        expert_out = project_out(hidden, full, ff)
        other_hidden = other_core(hidden)

    with jax.named_scope("combine"):
        returned = exchange(expert_out.reshape(sources, per_source, width)).reshape(slots, width)
        slot_grad = combine(mix_high, mix_low, weight[:, None], returned, wanted)
        owner_grad = exchange(slot_grad.reshape(sources, per_source, width)).reshape(slots, width)
        other_grad = other_core(owner_grad)

    with jax.named_scope("backward"):
        pre_grad = back_in(owner_grad, full, pre, ff)
        other_pre = other_core(pre_grad)

    with jax.named_scope("weight_gradients"):
        place = lax.axis_index("dp")
        z, core = place // 2, place % 2
        mine = (expert_rows, pre_grad, owner_grad, hidden)
        theirs = (other_rows, other_pre, other_grad, other_hidden)
        far = chips // 2
        place_of = lambda steps: (((z + jnp.array(steps, jnp.int32)) & (chips - 1)) * 2 + core)
        ahead, behind = chip_terms(place_of([far]), mine, theirs, True)
        ahead, behind = along(ahead, 1), along(behind, -1)
        for near in range(far - 1, 0, -1):
            first, second = chip_terms(place_of([near, chips - near]), mine, theirs, False)
            ahead, behind = add_term(ahead, first), add_term(behind, second, True)
            ahead, behind = along(ahead, 1), along(behind, -1)
        factor = (groups * sources * per_source) ** (-0.5)
        (term,) = chip_terms(place_of([0]), mine, theirs, False)
        gradients = last_sum(ahead, behind, term, ff, factor)

    with jax.named_scope("token_gradient"):
        row_grad = back_out(pre_grad, full, ff)
        came_back = exchange(row_grad.reshape(sources, per_source, width)).reshape(slots, width)
        token_grad = to_tokens(names.T.astype(BF16), came_back)

    return (token_grad, *gradients)


def solution(mesh):
    return jax.shard_map(
        on_device,
        mesh=mesh,
        in_specs=(
            P(("dp", "expert"), None),
            P(("dp", "expert"), None),
            P("dp", None, "expert", None),
            P("dp", None, "expert"),
            P("dp", None, "expert", None),
            P("dp", "expert", None),
            P("dp", "expert", None),
            P("dp", "expert", None),
        ),
        out_specs=(
            P(("dp", "expert"), None),
            P("dp", "expert", None),
            P("dp", "expert", None),
            P("dp", "expert", None),
        ),
        check_vma=False,
    )
```

time: 224 us -> 217 us (0.969)
  Pallas kernels: 56.3 us -> 47.1 us
  local copies, waits for them, and re-layouts: 2.85 us -> 7.52 us
  waiting for transfers between devices: 98.4 us -> 94.5 us
    pallas_call x9 -> x15, Pallas kernels: 37.4 us -> 30.9 us  [the longest x5 13.3 us: chip_terms(): call(body, (1,), columns * 4 + [pair, whole] * 2, [sums] * number, [shape...]
    unnamed x8 -> x24, local copies, waits for them, and re-layouts: 1.04 us -> 5.8 us
    all_to_all x4, waiting for transfers between devices: 45.5 us -> 42.2 us  [exchange(): lax.all_to_all(block, 'expert', split_axis=0, concat_axis=0, tiled=True)]
  transfers between devices with their start and end apart: 17 -> 17, of which waited for: 9 -> 9; matrix products, arithmetic and copies ran while one was open for 6% -> 7% of each run, Pallas kernels for 13% -> 14%
where the time goes in v4:
time: 217 us; the launch traced here: 216 us
  waiting for transfers between devices  94.5 us (44%)
  Pallas kernels  47.1 us (22%)
  starting transfers between devices  40.3 us (19%)
  between operations  14.2 us (7%)
  local copies, waits for them, and re-layouts  7.52 us (3%)
  other arithmetic  6.07 us (3%)
  matrix products  5.9 us (3%)
    all_to_all x4, waiting for transfers between devices, exchange(): lax.all_to_all(block, 'expert', split_axis=0, concat_axis=0, tiled=True)  42.2 us
    all_gather x1, waiting for transfers between devices, on_device(): full = lax.all_gather(own, 'dp', axis=0, tiled=True)  35.8 us
    all_to_all x4, starting transfers between devices, exchange(): lax.all_to_all(block, 'expert', split_axis=0, concat_axis=0, tiled=True)  26.4 us
    ppermute x8, waiting for transfers between devices, along(): return lax.ppermute(array, 'dp', pairs)  13.7 us
    ppermute x8, starting transfers between devices, along(): return lax.ppermute(array, 'dp', pairs)  13.3 us
    pallas_call x5, Pallas kernels, chip_terms(): call(body, (1,), columns * 4 + [pair, whole] * 2, [sums] * number, [shape...  13.3 us
    pallas_call x6, Pallas kernels, add_term(): call(body, (1,), [pl.BlockSpec((part, width), lambda i: (0, 0)), pl.Block...  5.96 us
    dot_general x2, matrix products, dot(): return lax.dot_general(a, b, (dims, ((), ())), preferred_element_type=F32)  5.9 us
  transfers between devices with their start and end apart: 17, of which 9 were waited for; matrix products, arithmetic and copies ran while one was open for 7% of the time, Pallas kernels for 14%

profile of v4, /device:TPU:2, one launch (start us, length us, event | category | flops | bytes accessed | tf_op | source)
XLA Modules:
  0.0 215.6 jit_solution(15592547370447923580)
XLA Ops:
  13.9 2.0 convolution_convert_fusion.1
  15.9 7.5 %all-to-all-start = ((bf16[16,16,2048]{2,1,0:T(8,128)(2,1)}), bf16[16,16,2048]{2,1,0:T(8,128)(2,1)}, u32[]{:S(2)}, u32[]{:S(2)}) async-start(bf16[16,16,2048]{2,1,0:T(8,128)(2,1)} %bitcast.23), calls=%async_computation | async-start | bytes 2097152 | tf_op jit(solution)/shard_map/rows_out/all_to_all | solution.py:18
  26.1 13.1 %all-to-all-done = bf16[16,16,2048]{2,1,0:T(8,128)(2,1)} async-done(((bf16[16,16,2048]{2,1,0:T(8,128)(2,1)}), bf16[16,16,2048]{2,1,0:T(8,128)(2,1)}, u32[]{:S(2)}, u32[]{:S(2)}) %all-to-all-start) | async-done | bytes 1048608 | tf_op jit(solution)/shard_map/rows_out/all_to_all | solution.py:18
  39.3 35.8 %all-gather.2.cloned.1.call-done.w.wd.wg.wu = bf16[2048,2304]{1,0:T(8,128)(2,1)} async-done(((bf16[128,2304]{1,0:T(8,128)(2,1)}), bf16[2048,2304]{1,0:T(8,128)(2,1)}) %all-gather.2.cloned.1.call-update) | async-done | bytes 9437200 | tf_op jit(solution)/shard_map/gather_weights/all_gather | solution.py:352
  75.0 4.6 %forward.2 = (f32[256,1536]{1,0:T(8,128)S(1)}, bf16[256,768]{1,0:T(8,128)(2,1)S(1)}) custom-call(bf16[256,2048]{1,0:T(8,128)(2,1)} %bitcast.2.x.refs_0_.refs_1_, bf16[2048,2304]{1,0:T(8,128)(2,1)} %all-gather.2.cloned.1.call-done.w.wd.wg.wu), custom_call_target="tpu_custom_call" | custom-call | flops 1610612736 | bytes 9306112 | tf_op jit(solution)/shard_map/forward/pallas_call | solution.py:103
  79.6 4.0 %forward.3 = bf16[256,2048]{1,0:T(8,128)(2,1)} custom-call(bf16[256,768]{1,0:T(8,128)(2,1)S(1)} %get-tuple-element.17.h.refs_5_.refs_9_, bf16[2048,2304]{1,0:T(8,128)(2,1)} %all-gather.2.cloned.1.call-done.w.wd.wg.wu), custom_call_target="tpu_custom_call" | custom-call | flops 805306368 | bytes 4587520 | tf_op jit(solution)/shard_map/forward/pallas_call | solution.py:125
  83.7 7.3 %all-to-all-start.1 = ((bf16[16,16,2048]{2,1,0:T(8,128)(2,1)}), bf16[16,16,2048]{2,1,0:T(8,128)(2,1)}, u32[]{:S(2)}, u32[]{:S(2)}) async-start(bf16[16,16,2048]{2,1,0:T(8,128)(2,1)} %bitcast.22), calls=%async_computation.1 | async-start | bytes 2097152 | tf_op jit(solution)/shard_map/combine/all_to_all | solution.py:18
  93.4 3.9 %convolution_convert_fusion.goal = bf16[256,2048]{1,0:T(8,128)(2,1)} fusion(bf16[768,2048]{1,0:T(8,128)(2,1)} %param.14, s32[256]{0:T(256)S(1)} %eq.37, pred[256]{0:T(512)(128)(4,1)S(1)} %lt.49), kind=kOutput, calls=%fused_computation | convolution fusion | flops 806223872 | bytes 4195584 | tf_op jit(solution)/shard_map/rows_out/dot_general | solution.py:22
  97.3 10.0 %all-to-all-done.1 = bf16[16,16,2048]{2,1,0:T(8,128)(2,1)} async-done(((bf16[16,16,2048]{2,1,0:T(8,128)(2,1)}), bf16[16,16,2048]{2,1,0:T(8,128)(2,1)}, u32[]{:S(2)}, u32[]{:S(2)}) %all-to-all-start.1) | async-done | bytes 1048608 | tf_op jit(solution)/shard_map/combine/all_to_all | solution.py:18
  107.3 3.4 %combine.1 = bf16[256,2048]{1,0:T(8,128)(2,1)} custom-call(bf16[256,256]{1,0:T(8,128)(2,1)} %get-tuple-element.33.high, bf16[256,256]{1,0:T(8,128)(2,1)} %get-tuple-element.32.low, f32[256,1]{1,0:T(8,128)} %broadcast_select_fusion.w, bf16[256,2048]{1,0:T(8,128)(2,1)} %bitcast.7.back, bf16[256,2048]{1,0:T(8,128)(2,1)} %convolution_convert_fusion.goal), custom_call_target="tpu_custom_call" | custom-call | flops 536870912 | bytes 3145728 | tf_op jit(solution)/shard_map/combine/pallas_call | solution.py:150
  110.7 5.8 %all-to-all-start.2 = ((bf16[16,16,2048]{2,1,0:T(8,128)(2,1)}), bf16[16,16,2048]{2,1,0:T(8,128)(2,1)}, u32[]{:S(2)}, u32[]{:S(2)}) async-start(bf16[16,16,2048]{2,1,0:T(8,128)(2,1)} %bitcast.21), calls=%async_computation.2 | async-start | bytes 2097152 | tf_op jit(solution)/shard_map/combine/all_to_all | solution.py:18
  116.5 15.2 %all-to-all-done.2 = bf16[16,16,2048]{2,1,0:T(8,128)(2,1)} async-done(((bf16[16,16,2048]{2,1,0:T(8,128)(2,1)}), bf16[16,16,2048]{2,1,0:T(8,128)(2,1)}, u32[]{:S(2)}, u32[]{:S(2)}) %all-to-all-start.2) | async-done | bytes 1048608 | tf_op jit(solution)/shard_map/combine/all_to_all | solution.py:18
  131.7 4.6 %backward.1.x.refs_4_.refs_8_ = bf16[2,256,768]{2,1,0:T(8,128)(2,1)} custom-call(bf16[256,2048]{1,0:T(8,128)(2,1)} %bitcast.9.x.refs_1_.refs_2_.refs_3_, bf16[2048,2304]{1,0:T(8,128)(2,1)} %all-gather.2.cloned.1.call-done.w.wd.wg.wu, f32[256,1536]{1,0:T(8,128)} %copy-done.2), custom_call_target="tpu_custom_call" | custom-call | flops 805306368 | bytes 6553600 | tf_op jit(solution)/shard_map/backward/pallas_call | solution.py:177
  136.8 2.5 %collective-permute-done.3.refs_7_.refs_11_ = bf16[256,768]{1,0:T(8,128)(2,1)} collective-permute-done((bf16[256,768]{1,0:T(8,128)(2,1)S(1)}, bf16[256,768]{1,0:T(8,128)(2,1)}, u32[]{:S(2)}, u32[]{:S(2)}) %collective-permute-start.3) | collective-permute-done | bytes 393248 | tf_op jit(solution)/shard_map/forward/ppermute | solution.py:348
  139.6 2.1 weight_gradients.12
  141.8 3.2 %collective-permute-start.8 = (bf16[64,2304]{1,0:T(8,128)(2,1)S(1)}, bf16[64,2304]{1,0:T(8,128)(2,1)S(1)}, u32[]{:S(2)}, u32[]{:S(2)}) collective-permute-start(bf16[64,2304]{1,0:T(8,128)(2,1)S(1)} %get-tuple-element.23), channel_id=1, source_target_pairs={{0,224},{16,240},{32,0},{48,16},{64,32},{80,48},{96,64},{112,80},{... | collective-permute-start | bytes 884744 | tf_op jit(solution)/shard_map/weight_gradients/ppermute | solution.py:345
  145.1 3.0 %weight_gradients.13 = (f32[128,2304]{1,0:T(8,128)S(1)}, f32[128,2304]{1,0:T(8,128)S(1)}) custom-call(s32[2]{0:T(128)S(1)} %multiply_add_fusion.2.names, bf16[256,2048]{1,0:T(8,128)(2,1)} %bitcast.2.x.refs_0_.refs_1_, bf16[256,2048]{1,0:T(8,128)(2,1)} %bitcast.2.x.refs_0_.refs_1_, bf16[256,2048]{1,0:T(8,128)(2,1)} %bitcast.9.x.refs_1_.refs_2_.refs_3_, ...), custom_call_target="tpu_custom_call" | custom-call | flops 603979776 | bytes 5242880 | tf_op jit(solution)/shard_map/weight_gradients/pallas_call | solution.py:243
  148.2 4.2 %collective-permute-done.4.a = bf16[64,2304]{1,0:T(8,128)(2,1)S(1)} collective-permute-done((bf16[64,2304]{1,0:T(8,128)(2,1)S(1)}, bf16[64,2304]{1,0:T(8,128)(2,1)S(1)}, u32[]{:S(2)}, u32[]{:S(2)}) %collective-permute-start.4) | collective-permute-done | bytes 294944 | tf_op jit(solution)/shard_map/weight_gradients/ppermute | solution.py:345
  152.8 3.3 %collective-permute-start.9 = (bf16[128,2304]{1,0:T(8,128)(2,1)S(1)}, bf16[128,2304]{1,0:T(8,128)(2,1)S(1)}, u32[]{:S(2)}, u32[]{:S(2)}) collective-permute-start(bf16[128,2304]{1,0:T(8,128)(2,1)S(1)} %weight_gradients.19), channel_id=1, source_target_pairs={{0,224},{16,240},{32,0},{48,16},{64,32},{80,48},{96,64},{112,80},{... | collective-permute-start | bytes 1769480 | tf_op jit(solution)/shard_map/weight_gradients/ppermute | solution.py:345
  156.1 3.1 %weight_gradients.15 = (f32[128,2304]{1,0:T(8,128)S(1)}, f32[128,2304]{1,0:T(8,128)S(1)}) custom-call(s32[2]{0:T(128)S(1)} %get-tuple-element.35.names, bf16[256,2048]{1,0:T(8,128)(2,1)} %bitcast.2.x.refs_0_.refs_1_, bf16[256,2048]{1,0:T(8,128)(2,1)} %bitcast.2.x.refs_0_.refs_1_, bf16[256,2048]{1,0:T(8,128)(2,1)} %bitcast.9.x.refs_1_.refs_2_.refs_3_, ...), custom_call_target="tpu_custom_call" | custom-call | flops 603979776 | bytes 5242880 | tf_op jit(solution)/shard_map/weight_gradients/pallas_call | solution.py:243
  159.2 9.5 %collective-permute-done.5.a = bf16[128,2304]{1,0:T(8,128)(2,1)S(1)} collective-permute-done((bf16[128,2304]{1,0:T(8,128)(2,1)S(1)}, bf16[128,2304]{1,0:T(8,128)(2,1)S(1)}, u32[]{:S(2)}, u32[]{:S(2)}) %collective-permute-start.5) | collective-permute-done | bytes 589856 | tf_op jit(solution)/shard_map/weight_gradients/ppermute | solution.py:345
  170.5 3.2 %collective-permute-start.10 = (bf16[128,2304]{1,0:T(8,128)(2,1)}, bf16[128,2304]{1,0:T(8,128)(2,1)}, u32[]{:S(2)}, u32[]{:S(2)}) collective-permute-start(bf16[128,2304]{1,0:T(8,128)(2,1)} %weight_gradients.20), channel_id=1, source_target_pairs={{0,224},{16,240},{32,0},{48,16},{64,32},{80,48},{96,64},{112,80},{... | collective-permute-start | bytes 1769480 | tf_op jit(solution)/shard_map/weight_gradients/ppermute | solution.py:345
  173.8 5.4 %token_gradient.2 = bf16[256,2048]{1,0:T(8,128)(2,1)} custom-call(bf16[2,256,768]{2,1,0:T(8,128)(2,1)} %backward.1.x.refs_4_.refs_8_, bf16[2048,2304]{1,0:T(8,128)(2,1)} %all-gather.2.cloned.1.call-done.w.wd.wg.wu, bf16[2048,2304]{1,0:T(8,128)(2,1)} %all-gather.2.cloned.1.call-done.w.wd.wg.wu), custom_call_target="tpu_custom_call" | custom-call | flops 1610612736 | bytes 8126464 | tf_op jit(solution)/shard_map/token_gradient/pallas_call | solution.py:202
  179.2 5.8 %all-to-all-start.3 = ((bf16[16,16,2048]{2,1,0:T(8,128)(2,1)}), bf16[16,16,2048]{2,1,0:T(8,128)(2,1)}, u32[]{:S(2)}, u32[]{:S(2)}) async-start(bf16[16,16,2048]{2,1,0:T(8,128)(2,1)} %bitcast.20), calls=%async_computation.3 | async-start | bytes 2097152 | tf_op jit(solution)/shard_map/token_gradient/all_to_all | solution.py:18
  184.9 3.0 %weight_gradients.17 = (f32[128,2304]{1,0:T(8,128)S(1)}, f32[128,2304]{1,0:T(8,128)S(1)}) custom-call(s32[2]{0:T(128)S(1)} %get-tuple-element.34.names, bf16[256,2048]{1,0:T(8,128)(2,1)} %bitcast.2.x.refs_0_.refs_1_, bf16[256,2048]{1,0:T(8,128)(2,1)} %bitcast.2.x.refs_0_.refs_1_, bf16[256,2048]{1,0:T(8,128)(2,1)} %bitcast.9.x.refs_1_.refs_2_.refs_3_, ...), custom_call_target="tpu_custom_call" | custom-call | flops 603979776 | bytes 5242880 | tf_op jit(solution)/shard_map/weight_gradients/pallas_call | solution.py:243
  188.0 2.0 weight_gradients.18
  190.0 2.0 weight_gradients.21
  192.0 3.2 %collective-permute-start.11 = (bf16[128,2304]{1,0:T(8,128)(2,1)}, bf16[128,2304]{1,0:T(8,128)(2,1)}, u32[]{:S(2)}, u32[]{:S(2)}) collective-permute-start(bf16[128,2304]{1,0:T(8,128)(2,1)} %weight_gradients.21), channel_id=1, source_target_pairs={{0,224},{16,240},{32,0},{48,16},{64,32},{80,48},{96,64},{112,80},{... | collective-permute-start | bytes 1769480 | tf_op jit(solution)/shard_map/weight_gradients/ppermute | solution.py:345
  196.1 3.8 %all-to-all-done.3 = bf16[16,16,2048]{2,1,0:T(8,128)(2,1)} async-done(((bf16[16,16,2048]{2,1,0:T(8,128)(2,1)}), bf16[16,16,2048]{2,1,0:T(8,128)(2,1)}, u32[]{:S(2)}, u32[]{:S(2)}) %all-to-all-start.3) | async-done | bytes 1048608 | tf_op jit(solution)/shard_map/token_gradient/all_to_all | solution.py:18
  200.9 3.4 %token_gradient.3 = bf16[768,2048]{1,0:T(8,128)(2,1)} custom-call(bf16[768,256]{1,0:T(8,128)(2,1)S(1)} %copy-done.3, bf16[256,2048]{1,0:T(8,128)(2,1)} %bitcast.11.back), custom_call_target="tpu_custom_call" | custom-call | flops 805306368 | bytes 4194304 | tf_op jit(solution)/shard_map/token_gradient/pallas_call | solution.py:313
  204.2 2.1 weight_gradients.22.mine
  206.3 2.4 %weight_gradients.23 = (f32[128,1,768]{2,1,0:T(1,128)}, f32[128,1,768]{2,1,0:T(1,128)}, f32[128,1,768]{2,1,0:T(1,128)}) custom-call(bf16[128,2304]{1,0:T(8,128)(2,1)} %collective-permute-done.7.a, bf16[128,2304]{1,0:T(8,128)(2,1)} %collective-permute-done.11.b, f32[128,2304]{1,0:T(8,128)S(1)} %weight_gradients.22.mine), custom_call_target="tpu_custom_call" | custom-call | flops 1179648 | bytes 3538944 | tf_op jit(solution)/shard_map/weight_gradients/pallas_call | solution.py:294
  (62 shorter events, 16.9 us)
Async XLA Ops:
  7.2 6.7 %copy-start = (bf16[768,2048]{1,0:T(8,128)(2,1)S(1)}, bf16[768,2048]{1,0:T(8,128)(2,1)}, u32[]{:S(2)}) copy-start(bf16[768,2048]{1,0:T(8,128)(2,1)} %param.13) | copy-start | bytes 9437188
  7.2 67.9 %all-gather.2.cloned.1.call-start = ((), (), s32[]{:S(2)}) async-start(), calls=%async_computation.4 | async-start | bytes 10027008 | tf_op jit(solution)/shard_map/gather_weights/all_gather | solution.py:352
  7.2 1.1 copy-start.4
  8.3 0.9 copy-start.5
  9.2 0.9 copy-start.6
  10.2 0.8 copy-start.1
  13.9 10.7 %copy-start.7 = (f32[1,16,1,16]{3,2,1,0:T(1,128)S(1)}, f32[1,16,1,16]{3,2,1,0:T(1,128)}, u32[]{:S(2)}) copy-start(f32[1,16,1,16]{3,2,1,0:T(1,128)} %param.17) | copy-start | bytes 3076
  15.9 23.4 %all-to-all-start = ((bf16[16,16,2048]{2,1,0:T(8,128)(2,1)}), bf16[16,16,2048]{2,1,0:T(8,128)(2,1)}, u32[]{:S(2)}, u32[]{:S(2)}) async-start(bf16[16,16,2048]{2,1,0:T(8,128)(2,1)} %bitcast.23), calls=%async_computation | async-start | bytes 2097152 | tf_op jit(solution)/shard_map/rows_out/all_to_all | solution.py:18
  79.6 4.1 %copy-start.2 = (f32[256,1536]{1,0:T(8,128)}, f32[256,1536]{1,0:T(8,128)S(1)}, u32[]{:S(2)}) copy-start(f32[256,1536]{1,0:T(8,128)S(1)} %get-tuple-element.18.pre_ref) | copy-start | bytes 4718596
  83.7 23.6 %all-to-all-start.1 = ((bf16[16,16,2048]{2,1,0:T(8,128)(2,1)}), bf16[16,16,2048]{2,1,0:T(8,128)(2,1)}, u32[]{:S(2)}, u32[]{:S(2)}) async-start(bf16[16,16,2048]{2,1,0:T(8,128)(2,1)} %bitcast.22), calls=%async_computation.1 | async-start | bytes 2097152 | tf_op jit(solution)/shard_map/combine/all_to_all | solution.py:18
  110.7 21.1 %all-to-all-start.2 = ((bf16[16,16,2048]{2,1,0:T(8,128)(2,1)}), bf16[16,16,2048]{2,1,0:T(8,128)(2,1)}, u32[]{:S(2)}, u32[]{:S(2)}) async-start(bf16[16,16,2048]{2,1,0:T(8,128)(2,1)} %bitcast.21), calls=%async_computation.2 | async-start | bytes 2097152 | tf_op jit(solution)/shard_map/combine/all_to_all | solution.py:18
  116.5 20.3 %collective-permute-start = (bf16[256,2048]{1,0:T(8,128)(2,1)}, bf16[256,2048]{1,0:T(8,128)(2,1)}, u32[]{:S(2)}, u32[]{:S(2)}) collective-permute-start(bf16[256,2048]{1,0:T(8,128)(2,1)} %bitcast.2.x.refs_0_.refs_1_), channel_id=1, source_target_pairs={{0,16},{16,0},{32,48},{48,32},{64,80},{80,64},{96,112},{112,96},{1... | collective-permute-start | bytes 3145736 | tf_op jit(solution)/shard_map/rows_out/ppermute | solution.py:348
  131.7 7.9 %collective-permute-start.1 = (bf16[256,2048]{1,0:T(8,128)(2,1)}, bf16[256,2048]{1,0:T(8,128)(2,1)}, u32[]{:S(2)}, u32[]{:S(2)}) collective-permute-start(bf16[256,2048]{1,0:T(8,128)(2,1)} %bitcast.9.x.refs_1_.refs_2_.refs_3_), channel_id=1, source_target_pairs={{0,16},{16,0},{32,48},{48,32},{64,80},{80,64},{96,112},{112,96},{1... | collective-permute-start | bytes 3145736 | tf_op jit(solution)/shard_map/combine/ppermute | solution.py:348
  136.3 3.3 %collective-permute-start.2 = (bf16[2,256,768]{2,1,0:T(8,128)(2,1)}, bf16[2,256,768]{2,1,0:T(8,128)(2,1)}, u32[]{:S(2)}, u32[]{:S(2)}) collective-permute-start(bf16[2,256,768]{2,1,0:T(8,128)(2,1)} %backward.1.x.refs_4_.refs_8_), channel_id=1, source_target_pairs={{0,16},{16,0},{32,48},{48,32},{64,80},{80,64},{96,112},{112,96},{1... | collective-permute-start | bytes 2359304 | tf_op jit(solution)/shard_map/backward/ppermute | solution.py:348
  136.8 2.5 %collective-permute-start.3 = (bf16[256,768]{1,0:T(8,128)(2,1)S(1)}, bf16[256,768]{1,0:T(8,128)(2,1)}, u32[]{:S(2)}, u32[]{:S(2)}) collective-permute-start(bf16[256,768]{1,0:T(8,128)(2,1)S(1)} %get-tuple-element.17.h.refs_5_.refs_9_), channel_id=1, source_target_pairs={{0,16},{16,0},{32,48},{48,32},{64,80},{80,64},{96,112},{112,96},{1... | collective-permute-start | bytes 1179656 | tf_op jit(solution)/shard_map/forward/ppermute | solution.py:348
  139.6 5.4 %copy-start.10 = (s32[2]{0:T(128)S(1)}, s32[2]{0:T(128)}, u32[]{:S(2)}) copy-start(s32[2]{0:T(128)} %constant.49.clone) | copy-start | bytes 28
  141.8 10.6 %collective-permute-start.4 = (bf16[64,2304]{1,0:T(8,128)(2,1)S(1)}, bf16[64,2304]{1,0:T(8,128)(2,1)S(1)}, u32[]{:S(2)}, u32[]{:S(2)}) collective-permute-start(bf16[64,2304]{1,0:T(8,128)(2,1)S(1)} %get-tuple-element.19), channel_id=1, source_target_pairs={{0,32},{16,48},{32,64},{48,80},{64,96},{80,112},{96,128},{112,144}... | collective-permute-start | bytes 884744 | tf_op jit(solution)/shard_map/weight_gradients/ppermute | solution.py:345
  141.8 10.8 %collective-permute-start.8 = (bf16[64,2304]{1,0:T(8,128)(2,1)S(1)}, bf16[64,2304]{1,0:T(8,128)(2,1)S(1)}, u32[]{:S(2)}, u32[]{:S(2)}) collective-permute-start(bf16[64,2304]{1,0:T(8,128)(2,1)S(1)} %get-tuple-element.23), channel_id=1, source_target_pairs={{0,224},{16,240},{32,0},{48,16},{64,32},{80,48},{96,64},{112,80},{... | collective-permute-start | bytes 884744 | tf_op jit(solution)/shard_map/weight_gradients/ppermute | solution.py:345
  148.1 7.9 %copy-start.8 = (s32[2]{0:T(128)S(1)}, s32[2]{0:T(128)}, u32[]{:S(2)}) copy-start(s32[2]{0:T(128)} %constant.51.clone) | copy-start | bytes 28
  148.2 7.9 %copy-start.9 = (s32[2]{0:T(128)S(1)}, s32[2]{0:T(128)}, u32[]{:S(2)}) copy-start(s32[2]{0:T(128)} %constant.50.clone) | copy-start | bytes 28
  152.4 16.3 %collective-permute-start.5 = (bf16[128,2304]{1,0:T(8,128)(2,1)S(1)}, bf16[128,2304]{1,0:T(8,128)(2,1)S(1)}, u32[]{:S(2)}, u32[]{:S(2)}) collective-permute-start(bf16[128,2304]{1,0:T(8,128)(2,1)S(1)} %weight_gradients.14), channel_id=1, source_target_pairs={{0,32},{16,48},{32,64},{48,80},{64,96},{80,112},{96,128},{112,144}... | collective-permute-start | bytes 1769480 | tf_op jit(solution)/shard_map/weight_gradients/ppermute | solution.py:345
  152.8 16.8 %collective-permute-start.9 = (bf16[128,2304]{1,0:T(8,128)(2,1)S(1)}, bf16[128,2304]{1,0:T(8,128)(2,1)S(1)}, u32[]{:S(2)}, u32[]{:S(2)}) collective-permute-start(bf16[128,2304]{1,0:T(8,128)(2,1)S(1)} %weight_gradients.19), channel_id=1, source_target_pairs={{0,224},{16,240},{32,0},{48,16},{64,32},{80,48},{96,64},{112,80},{... | collective-permute-start | bytes 1769480 | tf_op jit(solution)/shard_map/weight_gradients/ppermute | solution.py:345
  169.6 18.4 %collective-permute-start.6 = (bf16[128,2304]{1,0:T(8,128)(2,1)}, bf16[128,2304]{1,0:T(8,128)(2,1)}, u32[]{:S(2)}, u32[]{:S(2)}) collective-permute-start(bf16[128,2304]{1,0:T(8,128)(2,1)} %weight_gradients.16), channel_id=1, source_target_pairs={{0,32},{16,48},{32,64},{48,80},{64,96},{80,112},{96,128},{112,144}... | collective-permute-start | bytes 1769480 | tf_op jit(solution)/shard_map/weight_gradients/ppermute | solution.py:345
  170.5 19.5 %collective-permute-start.10 = (bf16[128,2304]{1,0:T(8,128)(2,1)}, bf16[128,2304]{1,0:T(8,128)(2,1)}, u32[]{:S(2)}, u32[]{:S(2)}) collective-permute-start(bf16[128,2304]{1,0:T(8,128)(2,1)} %weight_gradients.20), channel_id=1, source_target_pairs={{0,224},{16,240},{32,0},{48,16},{64,32},{80,48},{96,64},{112,80},{... | collective-permute-start | bytes 1769480 | tf_op jit(solution)/shard_map/weight_gradients/ppermute | solution.py:345
  179.2 20.7 %all-to-all-start.3 = ((bf16[16,16,2048]{2,1,0:T(8,128)(2,1)}), bf16[16,16,2048]{2,1,0:T(8,128)(2,1)}, u32[]{:S(2)}, u32[]{:S(2)}) async-start(bf16[16,16,2048]{2,1,0:T(8,128)(2,1)} %bitcast.20), calls=%async_computation.3 | async-start | bytes 2097152 | tf_op jit(solution)/shard_map/token_gradient/all_to_all | solution.py:18
  190.0 16.3 %collective-permute-start.7 = (bf16[128,2304]{1,0:T(8,128)(2,1)}, bf16[128,2304]{1,0:T(8,128)(2,1)}, u32[]{:S(2)}, u32[]{:S(2)}) collective-permute-start(bf16[128,2304]{1,0:T(8,128)(2,1)} %weight_gradients.18), channel_id=1, source_target_pairs={{0,32},{16,48},{32,64},{48,80},{64,96},{80,112},{96,128},{112,144}... | collective-permute-start | bytes 1769480 | tf_op jit(solution)/shard_map/weight_gradients/ppermute | solution.py:345
  192.0 14.3 %collective-permute-start.11 = (bf16[128,2304]{1,0:T(8,128)(2,1)}, bf16[128,2304]{1,0:T(8,128)(2,1)}, u32[]{:S(2)}, u32[]{:S(2)}) collective-permute-start(bf16[128,2304]{1,0:T(8,128)(2,1)} %weight_gradients.21), channel_id=1, source_target_pairs={{0,224},{16,240},{32,0},{48,16},{64,32},{80,48},{96,64},{112,80},{... | collective-permute-start | bytes 1769480 | tf_op jit(solution)/shard_map/weight_gradients/ppermute | solution.py:345
  199.9 1.0 copy-start.3
Sparse Core Ops, SparseCore 0:
  11.2 63.7 all-gather.1

commit v5 on v4

--- a/solution.py
+++ b/solution.py
@@ -24,6 +24,9 @@
 
 def in_hbm(array):
     return pltpu.with_memory_space_constraint(array, pltpu.HBM)
+
+
+UNREAD = pl.BlockSpec(memory_space=pltpu.HBM)
 
 
 def held_in_hbm(dims, dtype):
@@ -49,26 +52,21 @@
 def side_by_side(gate_weight, up_weight, down_weight):
     tall, ff = gate_weight.shape
 
-    def body(g, u, d, out, done):
-        copies = [
-            pltpu.make_async_copy(part, out.at[:, pl.ds(i * ff, ff)], done.at[i])
-            for i, part in enumerate((g, u, d))
-        ]
-        for copy in copies:
-            copy.start()
-        for copy in copies:
-            copy.wait()
-
-    place = pl.BlockSpec(memory_space=pltpu.HBM)
-    return pl.pallas_call(
-        body,
-        in_specs=[place] * 3,
-        out_specs=place,
-        out_shape=shape(tall, 3 * ff, BF16),
-        scratch_shapes=[pltpu.SemaphoreType.DMA((3,))],
-        compiler_params=pltpu.CompilerParams(vmem_limit_bytes=VMEM_LIMIT),
-        cost_estimate=pl.CostEstimate(flops=0, bytes_accessed=12 * tall * ff, transcendentals=0),
-    )(gate_weight, up_weight, down_weight)
+    def body(g, u, d, out):
+        out[:, :ff] = g[...]
+        out[:, ff : 2 * ff] = u[...]
+        out[:, 2 * ff :] = d[...]
+
+    part = pl.BlockSpec((tall, ff), lambda i: (0, 0))
+    return call(
+        body,
+        (1,),
+        [part] * 3,
+        pl.BlockSpec((tall, 3 * ff), lambda i: (0, 0)),
+        held_in_hbm((tall, 3 * ff), BF16),
+        0,
+        12 * tall * ff,
+    )(in_hbm(gate_weight), in_hbm(up_weight), in_hbm(down_weight))
 
 
 def shape(rows, columns, dtype):
@@ -85,12 +83,12 @@
         total[...] += term
 
 
-def project_in(rows, full, ff):
+def project_in(rows, full, ff, after):
     slots, width = rows.shape
     tall = 1024
     steps = width // tall
 
-    def body(x, w, pre, hidden, total):
+    def body(x, w, _, pre, hidden, total):
         step = pl.program_id(0)
         add_up(total, step, dot(x[...], w[...], ROW_BY_ROW))
 
@@ -106,13 +104,14 @@
         [
             pl.BlockSpec((slots, tall), lambda j: (0, j)),
             pl.BlockSpec((tall, 2 * ff), lambda j: (j, 0)),
+            UNREAD,
         ],
         [pl.BlockSpec((slots, 2 * ff), lambda j: (0, 0)), pl.BlockSpec((slots, ff), lambda j: (0, 0))],
         [shape(slots, 2 * ff, F32), shape(slots, ff, BF16)],
         4 * slots * width * ff,
         4 * width * ff + 2 * slots * width + 10 * slots * ff,
         scratch=[pltpu.VMEM((slots, 2 * ff), F32)],
-    )(in_hbm(rows), in_hbm(full))
+    )(in_hbm(rows), in_hbm(full), in_hbm(after))
 
 
 def project_out(hidden, full, ff):
@@ -136,11 +135,11 @@
     )(hidden, in_hbm(full))
 
 
-def combine(mix_high, mix_low, weight, returned, wanted):
+def combine(mix_high, mix_low, weight, returned, wanted, after):
     slots, width = returned.shape
     wide = width
 
-    def body(high, low, w, back, goal, out):
+    def body(high, low, w, back, goal, _, out):
         x = back[...]
         total = dot(high[...], x, ROW_BY_ROW) + dot(low[...], x, ROW_BY_ROW)
         out[...] = (w[...] * (total - goal[...].astype(F32))).astype(BF16)
@@ -150,12 +149,12 @@
     return call(
         body,
         (width // wide,),
-        [mix, mix, pl.BlockSpec((slots, 1), lambda j: (0, 0)), part, part],
+        [mix, mix, pl.BlockSpec((slots, 1), lambda j: (0, 0)), part, part, UNREAD],
         part,
         held_in_hbm((slots, width), BF16),
         4 * slots * slots * width,
         6 * slots * width,
-    )(in_hbm(mix_high), in_hbm(mix_low), in_hbm(weight), in_hbm(returned), in_hbm(wanted))
+    )(in_hbm(mix_high), in_hbm(mix_low), in_hbm(weight), in_hbm(returned), in_hbm(wanted), in_hbm(after))
 
 
 def back_in(owner_grad, full, pre, ff):
@@ -256,12 +255,13 @@
     )
 
 
-def add_term(came, term, last_rows=False):
+def add_term(came, term, last_rows=False, after=()):
     tall, width = term.shape
     part = came.shape[0]
     first = tall - part if last_rows else 0
 
-    def body(a, mine, out):
+    def body(a, mine, *refs):
+        out = refs[-1]
         if part < tall:
             out[...] = mine[...].astype(BF16)
         out[first : first + part] = (mine[first : first + part] + a[...].astype(F32)).astype(BF16)
@@ -272,12 +272,13 @@
         [
             pl.BlockSpec((part, width), lambda i: (0, 0)),
             pl.BlockSpec((tall, width), lambda i: (0, 0)),
-        ],
+        ]
+        + [UNREAD] * len(after),
         pl.BlockSpec((tall, width), lambda i: (0, 0)),
         shape(tall, width, BF16),
         tall * width,
         8 * tall * width,
-    )(came, term)
+    )(came, term, *map(in_hbm, after))
 
 
 def last_sum(ahead, behind, term, ff, factor):
@@ -371,19 +372,22 @@
         wanted = dot(pick, target, ROW_BY_ROW).astype(BF16)
 
     with jax.named_scope("forward"):
-        pre, hidden = project_in(expert_rows, full, ff)
+        pre, hidden = project_in(expert_rows, full, ff, other_rows)
         expert_out = project_out(hidden, full, ff)
         other_hidden = other_core(hidden)
 
     with jax.named_scope("combine"):
         returned = exchange(expert_out.reshape(sources, per_source, width)).reshape(slots, width)
-        slot_grad = combine(mix_high, mix_low, weight[:, None], returned, wanted)
+        slot_grad = combine(
+            mix_high, mix_low, weight[:, None], returned, wanted, other_hidden
+        )
         owner_grad = exchange(slot_grad.reshape(sources, per_source, width)).reshape(slots, width)
         other_grad = other_core(owner_grad)
 
     with jax.named_scope("backward"):
         pre_grad = back_in(owner_grad, full, pre, ff)
         other_pre = other_core(pre_grad)
+        row_grad = back_out(pre_grad, full, ff)
 
     with jax.named_scope("weight_gradients"):
         place = lax.axis_index("dp")
@@ -396,14 +400,14 @@
         ahead, behind = along(ahead, 1), along(behind, -1)
         for near in range(far - 1, 0, -1):
             first, second = chip_terms(place_of([near, chips - near]), mine, theirs, False)
-            ahead, behind = add_term(ahead, first), add_term(behind, second, True)
+            after = (row_grad,) if near == far - 2 else ()
+            ahead, behind = add_term(ahead, first, False, after), add_term(behind, second, True, after)
             ahead, behind = along(ahead, 1), along(behind, -1)
         factor = (groups * sources * per_source) ** (-0.5)
         (term,) = chip_terms(place_of([0]), mine, theirs, False)
         gradients = last_sum(ahead, behind, term, ff, factor)
 
     with jax.named_scope("token_gradient"):
-        row_grad = back_out(pre_grad, full, ff)
         came_back = exchange(row_grad.reshape(sources, per_source, width)).reshape(slots, width)
         token_grad = to_tokens(names.T.astype(BF16), came_back)
 

time: 217 us -> 212 us (0.977)
  blocking collectives: 0 us -> 44.3 us
  waiting for transfers between devices: 94.5 us -> 61.3 us
  starting transfers between devices: 40.3 us -> 26.7 us
  local copies, waits for them, and re-layouts: 7.52 us -> 3.8 us
    all_to_all x0 -> x2, blocking collectives: none -> 44.3 us  [exchange(): lax.all_to_all(block, 'expert', split_axis=0, concat_axis=0, tiled=True)]
    all_to_all x4 -> x2, waiting for transfers between devices: 42.2 us -> 11.1 us  [exchange(): lax.all_to_all(block, 'expert', split_axis=0, concat_axis=0, tiled=True)]
    all_to_all x4 -> x2, starting transfers between devices: 26.4 us -> 12.8 us  [exchange(): lax.all_to_all(block, 'expert', split_axis=0, concat_axis=0, tiled=True)]
    unnamed x24 -> x16, local copies, waits for them, and re-layouts: 5.8 us -> 2.06 us
  transfers between devices with their start and end apart: 17 -> 15, of which waited for: 9 -> 10; matrix products, arithmetic and copies ran while one was open for 7% -> 7% of each run, Pallas kernels for 14% -> 15%
where the time goes in v5:
time: 212 us; the launch traced here: 210 us
  waiting for transfers between devices  61.3 us (29%)
  Pallas kernels  49.2 us (23%)
  blocking collectives  44.3 us (21%)
  starting transfers between devices  26.7 us (13%)
  between operations  14.2 us (7%)
  other arithmetic  6.07 us (3%)
  matrix products  4.91 us (2%)
  local copies, waits for them, and re-layouts  3.8 us (2%)
    all_to_all x2, blocking collectives, exchange(): lax.all_to_all(block, 'expert', split_axis=0, concat_axis=0, tiled=True)  44.3 us
    all_gather x1, waiting for transfers between devices, on_device(): full = lax.all_gather(own, 'dp', axis=0, tiled=True)  34.9 us
    ppermute x8, starting transfers between devices, along(): return lax.ppermute(array, 'dp', pairs)  13.3 us
    pallas_call x5, Pallas kernels, chip_terms(): call(body, (1,), columns * 4 + [pair, whole] * 2, [sums] * number, [shape...  13.3 us
    ppermute x8, waiting for transfers between devices, along(): return lax.ppermute(array, 'dp', pairs)  12.8 us
    all_to_all x2, starting transfers between devices, exchange(): lax.all_to_all(block, 'expert', split_axis=0, concat_axis=0, tiled=True)  12.8 us
    all_to_all x2, waiting for transfers between devices, exchange(): lax.all_to_all(block, 'expert', split_axis=0, concat_axis=0, tiled=True)  11.1 us
    pallas_call x6, Pallas kernels, add_term(): call(body, (1,), [pl.BlockSpec((part, width), lambda i: (0, 0)), pl.Block...  5.97 us
  transfers between devices with their start and end apart: 15, of which 10 were waited for; matrix products, arithmetic and copies ran while one was open for 7% of the time, Pallas kernels for 15%

profile of v5, /device:TPU:2, one launch (start us, length us, event | category | flops | bytes accessed | tf_op | source)
XLA Modules:
  0.0 210.5 jit_solution(888999240238054147)
XLA Ops:
  7.2 2.1 %gather_weights.1 = bf16[128,2304]{1,0:T(8,128)(2,1)} custom-call(bf16[128,768]{1,0:T(8,128)(2,1)} %bitcast.21, bf16[128,768]{1,0:T(8,128)(2,1)} %bitcast.22, bf16[128,768]{1,0:T(8,128)(2,1)} %bitcast.23), custom_call_target="tpu_custom_call" | custom-call | bytes 1179648 | tf_op jit(solution)/shard_map/gather_weights/pallas_call | solution.py:61
  9.9 1.4 reduce.8
  13.2 23.2 %all_to_all.20 = bf16[16,16,2048]{2,1,0:T(8,128)(2,1)} all-to-all(bf16[16,16,2048]{2,1,0:T(8,128)(2,1)S(1)} %bitcast.20), channel_id=1, replica_groups=mesh['dp'=16,'expert'=16] {'expert'}, dimensions={0} | all-to-all | bytes 2097152 | tf_op jit(solution)/shard_map/rows_out/all_to_all | solution.py:18
  39.4 34.9 %all-gather.2.cloned.1.call-done.w.wd.wg.wu = bf16[2048,2304]{1,0:T(8,128)(2,1)} async-done(((bf16[128,2304]{1,0:T(8,128)(2,1)}), bf16[2048,2304]{1,0:T(8,128)(2,1)}) %all-gather.2.cloned.1.call-update) | async-done | bytes 9437200 | tf_op jit(solution)/shard_map/gather_weights/all_gather | solution.py:353
  74.2 4.6 %forward.2 = (f32[256,1536]{1,0:T(8,128)S(1)}, bf16[256,768]{1,0:T(8,128)(2,1)S(1)}) custom-call(bf16[256,2048]{1,0:T(8,128)(2,1)} %bitcast.2.x.refs_0_.refs_1_, bf16[2048,2304]{1,0:T(8,128)(2,1)} %all-gather.2.cloned.1.call-done.w.wd.wg.wu, bf16[256,2048]{1,0:T(8,128)(2,1)} %collective-permute-done._.refs_2_.refs_4_.refs_5_), custom_call_target="tpu_custom_call" | custom-call | flops 1610612736 | bytes 9306112 | tf_op jit(solution)/shard_map/forward/pallas_call | solution.py:101
  78.8 4.0 %forward.3 = bf16[256,2048]{1,0:T(8,128)(2,1)} custom-call(bf16[256,768]{1,0:T(8,128)(2,1)S(1)} %get-tuple-element.17.h.refs_5_.refs_9_, bf16[2048,2304]{1,0:T(8,128)(2,1)} %all-gather.2.cloned.1.call-done.w.wd.wg.wu), custom_call_target="tpu_custom_call" | custom-call | flops 805306368 | bytes 4587520 | tf_op jit(solution)/shard_map/forward/pallas_call | solution.py:124
  82.9 7.3 %all-to-all-start.1 = ((bf16[16,16,2048]{2,1,0:T(8,128)(2,1)}), bf16[16,16,2048]{2,1,0:T(8,128)(2,1)}, u32[]{:S(2)}, u32[]{:S(2)}) async-start(bf16[16,16,2048]{2,1,0:T(8,128)(2,1)} %bitcast.19), calls=%async_computation.1 | async-start | bytes 2097152 | tf_op jit(solution)/shard_map/combine/all_to_all | solution.py:18
  90.2 1.6 broadcast_select_fusion.w
  92.6 3.9 %convolution_convert_fusion.goal = bf16[256,2048]{1,0:T(8,128)(2,1)} fusion(bf16[768,2048]{1,0:T(8,128)(2,1)} %param.14, s32[256]{0:T(256)S(1)} %eq.37, pred[256]{0:T(512)(128)(4,1)S(1)} %lt.49), kind=kOutput, calls=%fused_computation | convolution fusion | flops 806223872 | bytes 4195584 | tf_op jit(solution)/shard_map/rows_out/dot_general | solution.py:22
  96.5 10.0 %all-to-all-done.1 = bf16[16,16,2048]{2,1,0:T(8,128)(2,1)} async-done(((bf16[16,16,2048]{2,1,0:T(8,128)(2,1)}), bf16[16,16,2048]{2,1,0:T(8,128)(2,1)}, u32[]{:S(2)}, u32[]{:S(2)}) %all-to-all-start.1) | async-done | bytes 1048608 | tf_op jit(solution)/shard_map/combine/all_to_all | solution.py:18
  106.5 3.4 %combine.1 = bf16[256,2048]{1,0:T(8,128)(2,1)} custom-call(bf16[256,256]{1,0:T(8,128)(2,1)} %get-tuple-element.33.high, bf16[256,256]{1,0:T(8,128)(2,1)} %get-tuple-element.32.low, f32[256,1]{1,0:T(8,128)} %broadcast_select_fusion.w, bf16[256,2048]{1,0:T(8,128)(2,1)} %bitcast.7.back, bf16[256,2048]{1,0:T(8,128)(2,1)} %convolution_convert_fusion.goal, ...), custom_call_target="tpu_custom_call" | custom-call | flops 536870912 | bytes 3145728 | tf_op jit(solution)/shard_map/combine/pallas_call | solution.py:149
  109.9 21.1 %all_to_all.21 = bf16[16,16,2048]{2,1,0:T(8,128)(2,1)} all-to-all(bf16[16,16,2048]{2,1,0:T(8,128)(2,1)} %bitcast.18), channel_id=1, replica_groups=mesh['dp'=16,'expert'=16] {'expert'}, dimensions={0} | all-to-all | bytes 2097152 | tf_op jit(solution)/shard_map/combine/all_to_all | solution.py:18
  131.0 4.5 %backward.2.x.refs_4_.refs_8_ = bf16[2,256,768]{2,1,0:T(8,128)(2,1)} custom-call(bf16[256,2048]{1,0:T(8,128)(2,1)} %bitcast.9.x.refs_1_.refs_2_.refs_3_, bf16[2048,2304]{1,0:T(8,128)(2,1)} %all-gather.2.cloned.1.call-done.w.wd.wg.wu, f32[256,1536]{1,0:T(8,128)} %copy-done.1), custom_call_target="tpu_custom_call" | custom-call | flops 805306368 | bytes 6553600 | tf_op jit(solution)/shard_map/backward/pallas_call | solution.py:176
  136.1 2.3 %collective-permute-done.3.refs_6_.refs_10_ = bf16[2,256,768]{2,1,0:T(8,128)(2,1)} collective-permute-done((bf16[2,256,768]{2,1,0:T(8,128)(2,1)}, bf16[2,256,768]{2,1,0:T(8,128)(2,1)}, u32[]{:S(2)}, u32[]{:S(2)}) %collective-permute-start.3) | collective-permute-done | bytes 786464 | tf_op jit(solution)/shard_map/backward/ppermute | solution.py:349
  138.3 2.1 weight_gradients.12
  140.6 3.2 %collective-permute-start.8 = (bf16[64,2304]{1,0:T(8,128)(2,1)S(1)}, bf16[64,2304]{1,0:T(8,128)(2,1)S(1)}, u32[]{:S(2)}, u32[]{:S(2)}) collective-permute-start(bf16[64,2304]{1,0:T(8,128)(2,1)S(1)} %get-tuple-element.23), channel_id=1, source_target_pairs={{0,224},{16,240},{32,0},{48,16},{64,32},{80,48},{96,64},{112,80},{... | collective-permute-start | bytes 884744 | tf_op jit(solution)/shard_map/weight_gradients/ppermute | solution.py:346
  143.8 3.0 %weight_gradients.13 = (f32[128,2304]{1,0:T(8,128)S(1)}, f32[128,2304]{1,0:T(8,128)S(1)}) custom-call(s32[2]{0:T(128)S(1)} %multiply_add_fusion.2.names, bf16[256,2048]{1,0:T(8,128)(2,1)} %bitcast.2.x.refs_0_.refs_1_, bf16[256,2048]{1,0:T(8,128)(2,1)} %bitcast.2.x.refs_0_.refs_1_, bf16[256,2048]{1,0:T(8,128)(2,1)} %bitcast.9.x.refs_1_.refs_2_.refs_3_, ...), custom_call_target="tpu_custom_call" | custom-call | flops 603979776 | bytes 5242880 | tf_op jit(solution)/shard_map/weight_gradients/pallas_call | solution.py:242
  146.9 4.2 %collective-permute-done.4.a = bf16[64,2304]{1,0:T(8,128)(2,1)S(1)} collective-permute-done((bf16[64,2304]{1,0:T(8,128)(2,1)S(1)}, bf16[64,2304]{1,0:T(8,128)(2,1)S(1)}, u32[]{:S(2)}, u32[]{:S(2)}) %collective-permute-start.4) | collective-permute-done | bytes 294944 | tf_op jit(solution)/shard_map/weight_gradients/ppermute | solution.py:346
  151.3 3.5 %collective-permute-start.9 = (bf16[128,2304]{1,0:T(8,128)(2,1)S(1)}, bf16[128,2304]{1,0:T(8,128)(2,1)S(1)}, u32[]{:S(2)}, u32[]{:S(2)}) collective-permute-start(bf16[128,2304]{1,0:T(8,128)(2,1)S(1)} %weight_gradients.19), channel_id=1, source_target_pairs={{0,224},{16,240},{32,0},{48,16},{64,32},{80,48},{96,64},{112,80},{... | collective-permute-start | bytes 1769480 | tf_op jit(solution)/shard_map/weight_gradients/ppermute | solution.py:346
  154.8 5.4 %backward.3.refs_0_ = bf16[256,2048]{1,0:T(8,128)(2,1)} custom-call(bf16[2,256,768]{2,1,0:T(8,128)(2,1)} %backward.2.x.refs_4_.refs_8_, bf16[2048,2304]{1,0:T(8,128)(2,1)} %all-gather.2.cloned.1.call-done.w.wd.wg.wu, bf16[2048,2304]{1,0:T(8,128)(2,1)} %all-gather.2.cloned.1.call-done.w.wd.wg.wu), custom_call_target="tpu_custom_call" | custom-call | flops 1610612736 | bytes 8126464 | tf_op jit(solution)/shard_map/backward/pallas_call | solution.py:201
  160.2 3.0 %weight_gradients.15 = (f32[128,2304]{1,0:T(8,128)S(1)}, f32[128,2304]{1,0:T(8,128)S(1)}) custom-call(s32[2]{0:T(128)S(1)} %get-tuple-element.35.names, bf16[256,2048]{1,0:T(8,128)(2,1)} %bitcast.2.x.refs_0_.refs_1_, bf16[256,2048]{1,0:T(8,128)(2,1)} %bitcast.2.x.refs_0_.refs_1_, bf16[256,2048]{1,0:T(8,128)(2,1)} %bitcast.9.x.refs_1_.refs_2_.refs_3_, ...), custom_call_target="tpu_custom_call" | custom-call | flops 603979776 | bytes 5242880 | tf_op jit(solution)/shard_map/weight_gradients/pallas_call | solution.py:242
  163.3 3.9 %collective-permute-done.5.a = bf16[128,2304]{1,0:T(8,128)(2,1)S(1)} collective-permute-done((bf16[128,2304]{1,0:T(8,128)(2,1)S(1)}, bf16[128,2304]{1,0:T(8,128)(2,1)S(1)}, u32[]{:S(2)}, u32[]{:S(2)}) %collective-permute-start.5) | collective-permute-done | bytes 589856 | tf_op jit(solution)/shard_map/weight_gradients/ppermute | solution.py:346
  169.0 3.2 %collective-permute-start.10 = (bf16[128,2304]{1,0:T(8,128)(2,1)}, bf16[128,2304]{1,0:T(8,128)(2,1)}, u32[]{:S(2)}, u32[]{:S(2)}) collective-permute-start(bf16[128,2304]{1,0:T(8,128)(2,1)} %weight_gradients.20), channel_id=1, source_target_pairs={{0,224},{16,240},{32,0},{48,16},{64,32},{80,48},{96,64},{112,80},{... | collective-permute-start | bytes 1769480 | tf_op jit(solution)/shard_map/weight_gradients/ppermute | solution.py:346
  172.3 5.5 %all-to-all-start.3 = ((bf16[16,16,2048]{2,1,0:T(8,128)(2,1)}), bf16[16,16,2048]{2,1,0:T(8,128)(2,1)}, u32[]{:S(2)}, u32[]{:S(2)}) async-start(bf16[16,16,2048]{2,1,0:T(8,128)(2,1)} %bitcast.17), calls=%async_computation.3 | async-start | bytes 2097152 | tf_op jit(solution)/shard_map/token_gradient/all_to_all | solution.py:18
  177.8 3.0 %weight_gradients.17 = (f32[128,2304]{1,0:T(8,128)S(1)}, f32[128,2304]{1,0:T(8,128)S(1)}) custom-call(s32[2]{0:T(128)S(1)} %get-tuple-element.34.names, bf16[256,2048]{1,0:T(8,128)(2,1)} %bitcast.2.x.refs_0_.refs_1_, bf16[256,2048]{1,0:T(8,128)(2,1)} %bitcast.2.x.refs_0_.refs_1_, bf16[256,2048]{1,0:T(8,128)(2,1)} %bitcast.9.x.refs_1_.refs_2_.refs_3_, ...), custom_call_target="tpu_custom_call" | custom-call | flops 603979776 | bytes 5242880 | tf_op jit(solution)/shard_map/weight_gradients/pallas_call | solution.py:242
  180.9 2.7 %collective-permute-done.6.a = bf16[128,2304]{1,0:T(8,128)(2,1)} collective-permute-done((bf16[128,2304]{1,0:T(8,128)(2,1)}, bf16[128,2304]{1,0:T(8,128)(2,1)}, u32[]{:S(2)}, u32[]{:S(2)}) %collective-permute-start.6) | collective-permute-done | bytes 589856 | tf_op jit(solution)/shard_map/weight_gradients/ppermute | solution.py:346
  183.5 2.0 weight_gradients.18
  185.5 2.0 weight_gradients.21
  187.5 3.2 %collective-permute-start.11 = (bf16[128,2304]{1,0:T(8,128)(2,1)}, bf16[128,2304]{1,0:T(8,128)(2,1)}, u32[]{:S(2)}, u32[]{:S(2)}) collective-permute-start(bf16[128,2304]{1,0:T(8,128)(2,1)} %weight_gradients.21), channel_id=1, source_target_pairs={{0,224},{16,240},{32,0},{48,16},{64,32},{80,48},{96,64},{112,80},{... | collective-permute-start | bytes 1769480 | tf_op jit(solution)/shard_map/weight_gradients/ppermute | solution.py:346
  193.7 3.3 %token_gradient.1 = bf16[768,2048]{1,0:T(8,128)(2,1)} custom-call(bf16[768,256]{1,0:T(8,128)(2,1)S(1)} %copy-done.2, bf16[256,2048]{1,0:T(8,128)(2,1)} %bitcast.11.back), custom_call_target="tpu_custom_call" | custom-call | flops 805306368 | bytes 4194304 | tf_op jit(solution)/shard_map/token_gradient/pallas_call | solution.py:314
  197.0 2.1 weight_gradients.22.mine
  201.2 2.4 %weight_gradients.23 = (f32[128,1,768]{2,1,0:T(1,128)}, f32[128,1,768]{2,1,0:T(1,128)}, f32[128,1,768]{2,1,0:T(1,128)}) custom-call(bf16[128,2304]{1,0:T(8,128)(2,1)} %collective-permute-done.7.a, bf16[128,2304]{1,0:T(8,128)(2,1)} %collective-permute-done.11.b, f32[128,2304]{1,0:T(8,128)S(1)} %weight_gradients.22.mine), custom_call_target="tpu_custom_call" | custom-call | flops 1179648 | bytes 3538944 | tf_op jit(solution)/shard_map/weight_gradients/pallas_call | solution.py:295
  (52 shorter events, 14.1 us)
Async XLA Ops:
  7.2 5.0 %copy-start = (bf16[768,2048]{1,0:T(8,128)(2,1)S(1)}, bf16[768,2048]{1,0:T(8,128)(2,1)}, u32[]{:S(2)}) copy-start(bf16[768,2048]{1,0:T(8,128)(2,1)} %param.13) | copy-start | bytes 9437188
  7.2 67.1 %all-gather.2.cloned.1.call-start = ((), (), s32[]{:S(2)}) async-start(), calls=%async_computation.4 | async-start | bytes 10027008 | tf_op jit(solution)/shard_map/gather_weights/all_gather | solution.py:353
  12.2 25.5 %copy-start.3 = (f32[1,16,1,16]{3,2,1,0:T(1,128)S(1)}, f32[1,16,1,16]{3,2,1,0:T(1,128)}, u32[]{:S(2)}) copy-start(f32[1,16,1,16]{3,2,1,0:T(1,128)} %param.17) | copy-start | bytes 3076
  36.4 3.0 %collective-permute-start = (bf16[256,2048]{1,0:T(8,128)(2,1)}, bf16[256,2048]{1,0:T(8,128)(2,1)}, u32[]{:S(2)}, u32[]{:S(2)}) collective-permute-start(bf16[256,2048]{1,0:T(8,128)(2,1)} %bitcast.2.x.refs_0_.refs_1_), channel_id=1, source_target_pairs={{0,16},{16,0},{32,48},{48,32},{64,80},{80,64},{96,112},{112,96},{1... | collective-permute-start | bytes 3145736 | tf_op jit(solution)/shard_map/rows_out/ppermute | solution.py:349
  78.8 4.1 %copy-start.1 = (f32[256,1536]{1,0:T(8,128)}, f32[256,1536]{1,0:T(8,128)S(1)}, u32[]{:S(2)}) copy-start(f32[256,1536]{1,0:T(8,128)S(1)} %get-tuple-element.18.pre_ref) | copy-start | bytes 4718596
  82.9 23.6 %all-to-all-start.1 = ((bf16[16,16,2048]{2,1,0:T(8,128)(2,1)}), bf16[16,16,2048]{2,1,0:T(8,128)(2,1)}, u32[]{:S(2)}, u32[]{:S(2)}) async-start(bf16[16,16,2048]{2,1,0:T(8,128)(2,1)} %bitcast.19), calls=%async_computation.1 | async-start | bytes 2097152 | tf_op jit(solution)/shard_map/combine/all_to_all | solution.py:18
  91.8 4.7 %collective-permute-start.1 = (bf16[256,768]{1,0:T(8,128)(2,1)S(1)}, bf16[256,768]{1,0:T(8,128)(2,1)}, u32[]{:S(2)}, u32[]{:S(2)}) collective-permute-start(bf16[256,768]{1,0:T(8,128)(2,1)S(1)} %get-tuple-element.17.h.refs_5_.refs_9_), channel_id=1, source_target_pairs={{0,16},{16,0},{32,48},{48,32},{64,80},{80,64},{96,112},{112,96},{1... | collective-permute-start | bytes 1179656 | tf_op jit(solution)/shard_map/forward/ppermute | solution.py:349
  131.0 7.3 %collective-permute-start.2 = (bf16[256,2048]{1,0:T(8,128)(2,1)}, bf16[256,2048]{1,0:T(8,128)(2,1)}, u32[]{:S(2)}, u32[]{:S(2)}) collective-permute-start(bf16[256,2048]{1,0:T(8,128)(2,1)} %bitcast.9.x.refs_1_.refs_2_.refs_3_), channel_id=1, source_target_pairs={{0,16},{16,0},{32,48},{48,32},{64,80},{80,64},{96,112},{112,96},{1... | collective-permute-start | bytes 3145736 | tf_op jit(solution)/shard_map/combine/ppermute | solution.py:349
  135.6 2.8 %collective-permute-start.3 = (bf16[2,256,768]{2,1,0:T(8,128)(2,1)}, bf16[2,256,768]{2,1,0:T(8,128)(2,1)}, u32[]{:S(2)}, u32[]{:S(2)}) collective-permute-start(bf16[2,256,768]{2,1,0:T(8,128)(2,1)} %backward.2.x.refs_4_.refs_8_), channel_id=1, source_target_pairs={{0,16},{16,0},{32,48},{48,32},{64,80},{80,64},{96,112},{112,96},{1... | collective-permute-start | bytes 2359304 | tf_op jit(solution)/shard_map/backward/ppermute | solution.py:349
  138.3 5.4 %copy-start.6 = (s32[2]{0:T(128)S(1)}, s32[2]{0:T(128)}, u32[]{:S(2)}) copy-start(s32[2]{0:T(128)} %constant.49.clone) | copy-start | bytes 28
  140.5 10.6 %collective-permute-start.4 = (bf16[64,2304]{1,0:T(8,128)(2,1)S(1)}, bf16[64,2304]{1,0:T(8,128)(2,1)S(1)}, u32[]{:S(2)}, u32[]{:S(2)}) collective-permute-start(bf16[64,2304]{1,0:T(8,128)(2,1)S(1)} %get-tuple-element.19), channel_id=1, source_target_pairs={{0,32},{16,48},{32,64},{48,80},{64,96},{80,112},{96,128},{112,144}... | collective-permute-start | bytes 884744 | tf_op jit(solution)/shard_map/weight_gradients/ppermute | solution.py:346
  140.6 10.7 %collective-permute-start.8 = (bf16[64,2304]{1,0:T(8,128)(2,1)S(1)}, bf16[64,2304]{1,0:T(8,128)(2,1)S(1)}, u32[]{:S(2)}, u32[]{:S(2)}) collective-permute-start(bf16[64,2304]{1,0:T(8,128)(2,1)S(1)} %get-tuple-element.23), channel_id=1, source_target_pairs={{0,224},{16,240},{32,0},{48,16},{64,32},{80,48},{96,64},{112,80},{... | collective-permute-start | bytes 884744 | tf_op jit(solution)/shard_map/weight_gradients/ppermute | solution.py:346
  146.9 7.9 %copy-start.4 = (s32[2]{0:T(128)S(1)}, s32[2]{0:T(128)}, u32[]{:S(2)}) copy-start(s32[2]{0:T(128)} %constant.51.clone) | copy-start | bytes 28
  146.9 7.9 %copy-start.5 = (s32[2]{0:T(128)S(1)}, s32[2]{0:T(128)}, u32[]{:S(2)}) copy-start(s32[2]{0:T(128)} %constant.50.clone) | copy-start | bytes 28
  151.1 16.1 %collective-permute-start.5 = (bf16[128,2304]{1,0:T(8,128)(2,1)S(1)}, bf16[128,2304]{1,0:T(8,128)(2,1)S(1)}, u32[]{:S(2)}, u32[]{:S(2)}) collective-permute-start(bf16[128,2304]{1,0:T(8,128)(2,1)S(1)} %weight_gradients.14), channel_id=1, source_target_pairs={{0,32},{16,48},{32,64},{48,80},{64,96},{80,112},{96,128},{112,144}... | collective-permute-start | bytes 1769480 | tf_op jit(solution)/shard_map/weight_gradients/ppermute | solution.py:346
  151.3 16.8 %collective-permute-start.9 = (bf16[128,2304]{1,0:T(8,128)(2,1)S(1)}, bf16[128,2304]{1,0:T(8,128)(2,1)S(1)}, u32[]{:S(2)}, u32[]{:S(2)}) collective-permute-start(bf16[128,2304]{1,0:T(8,128)(2,1)S(1)} %weight_gradients.19), channel_id=1, source_target_pairs={{0,224},{16,240},{32,0},{48,16},{64,32},{80,48},{96,64},{112,80},{... | collective-permute-start | bytes 1769480 | tf_op jit(solution)/shard_map/weight_gradients/ppermute | solution.py:346
  168.1 15.4 %collective-permute-start.6 = (bf16[128,2304]{1,0:T(8,128)(2,1)}, bf16[128,2304]{1,0:T(8,128)(2,1)}, u32[]{:S(2)}, u32[]{:S(2)}) collective-permute-start(bf16[128,2304]{1,0:T(8,128)(2,1)} %weight_gradients.16), channel_id=1, source_target_pairs={{0,32},{16,48},{32,64},{48,80},{64,96},{80,112},{96,128},{112,144}... | collective-permute-start | bytes 1769480 | tf_op jit(solution)/shard_map/weight_gradients/ppermute | solution.py:346
  169.0 16.5 %collective-permute-start.10 = (bf16[128,2304]{1,0:T(8,128)(2,1)}, bf16[128,2304]{1,0:T(8,128)(2,1)}, u32[]{:S(2)}, u32[]{:S(2)}) collective-permute-start(bf16[128,2304]{1,0:T(8,128)(2,1)} %weight_gradients.20), channel_id=1, source_target_pairs={{0,224},{16,240},{32,0},{48,16},{64,32},{80,48},{96,64},{112,80},{... | collective-permute-start | bytes 1769480 | tf_op jit(solution)/shard_map/weight_gradients/ppermute | solution.py:346
  172.3 20.4 %all-to-all-start.3 = ((bf16[16,16,2048]{2,1,0:T(8,128)(2,1)}), bf16[16,16,2048]{2,1,0:T(8,128)(2,1)}, u32[]{:S(2)}, u32[]{:S(2)}) async-start(bf16[16,16,2048]{2,1,0:T(8,128)(2,1)} %bitcast.17), calls=%async_computation.3 | async-start | bytes 2097152 | tf_op jit(solution)/shard_map/token_gradient/all_to_all | solution.py:18
  185.5 14.5 %collective-permute-start.7 = (bf16[128,2304]{1,0:T(8,128)(2,1)}, bf16[128,2304]{1,0:T(8,128)(2,1)}, u32[]{:S(2)}, u32[]{:S(2)}) collective-permute-start(bf16[128,2304]{1,0:T(8,128)(2,1)} %weight_gradients.18), channel_id=1, source_target_pairs={{0,32},{16,48},{32,64},{48,80},{64,96},{80,112},{96,128},{112,144}... | collective-permute-start | bytes 1769480 | tf_op jit(solution)/shard_map/weight_gradients/ppermute | solution.py:346
  187.5 13.7 %collective-permute-start.11 = (bf16[128,2304]{1,0:T(8,128)(2,1)}, bf16[128,2304]{1,0:T(8,128)(2,1)}, u32[]{:S(2)}, u32[]{:S(2)}) collective-permute-start(bf16[128,2304]{1,0:T(8,128)(2,1)} %weight_gradients.21), channel_id=1, source_target_pairs={{0,224},{16,240},{32,0},{48,16},{64,32},{80,48},{96,64},{112,80},{... | collective-permute-start | bytes 1769480 | tf_op jit(solution)/shard_map/weight_gradients/ppermute | solution.py:346
  192.7 1.0 copy-start.2
Sparse Core Ops, SparseCore 0:
  10.4 63.7 all-gather.1

commit v6 on v5

--- a/solution.py
+++ b/solution.py
@@ -275,7 +275,7 @@
         ]
         + [UNREAD] * len(after),
         pl.BlockSpec((tall, width), lambda i: (0, 0)),
-        shape(tall, width, BF16),
+        pltpu.VMEM((tall, width), BF16),
         tall * width,
         8 * tall * width,
     )(came, term, *map(in_hbm, after))
@@ -322,7 +322,7 @@
         shape(held, width, BF16),
         2 * held * slots * width,
         2 * (held + slots) * width,
-    )(names, came_back)
+    )(in_hbm(names), in_hbm(came_back))
 
 
 def on_device(

time: 212 us -> 212 us (level)
  no operation moved by 1% of the time
where the time goes in v6:
time: 212 us; the launch traced here: 211 us
  waiting for transfers between devices  62.2 us (29%)
  Pallas kernels  49.3 us (23%)
  blocking collectives  44.3 us (21%)
  starting transfers between devices  26.7 us (13%)
  between operations  14.2 us (7%)
  other arithmetic  6.07 us (3%)
  matrix products  4.91 us (2%)
  local copies, waits for them, and re-layouts  2.8 us (1%)
    all_to_all x2, blocking collectives, exchange(): lax.all_to_all(block, 'expert', split_axis=0, concat_axis=0, tiled=True)  44.3 us
    all_gather x1, waiting for transfers between devices, on_device(): full = lax.all_gather(own, 'dp', axis=0, tiled=True)  34.9 us
    ppermute x8, waiting for transfers between devices, along(): return lax.ppermute(array, 'dp', pairs)  13.7 us
    ppermute x8, starting transfers between devices, along(): return lax.ppermute(array, 'dp', pairs)  13.3 us
    pallas_call x5, Pallas kernels, chip_terms(): call(body, (1,), columns * 4 + [pair, whole] * 2, [sums] * number, [shape...  13.3 us
    all_to_all x2, starting transfers between devices, exchange(): lax.all_to_all(block, 'expert', split_axis=0, concat_axis=0, tiled=True)  12.8 us
    all_to_all x2, waiting for transfers between devices, exchange(): lax.all_to_all(block, 'expert', split_axis=0, concat_axis=0, tiled=True)  11.1 us
    pallas_call x6, Pallas kernels, add_term(): call(body, (1,), [pl.BlockSpec((part, width), lambda i: (0, 0)), pl.Block...  5.98 us
  transfers between devices with their start and end apart: 15, of which 10 were waited for; matrix products, arithmetic and copies ran while one was open for 7% of the time, Pallas kernels for 15%

profile of v6, /device:TPU:2, one launch (start us, length us, event | category | flops | bytes accessed | tf_op | source)
XLA Modules:
  0.0 210.5 jit_solution(9793602267034793271)
XLA Ops:
  7.2 2.1 %gather_weights.1 = bf16[128,2304]{1,0:T(8,128)(2,1)} custom-call(bf16[128,768]{1,0:T(8,128)(2,1)} %bitcast.21, bf16[128,768]{1,0:T(8,128)(2,1)} %bitcast.22, bf16[128,768]{1,0:T(8,128)(2,1)} %bitcast.23), custom_call_target="tpu_custom_call" | custom-call | bytes 1179648 | tf_op jit(solution)/shard_map/gather_weights/pallas_call | solution.py:61
  13.2 23.2 %all_to_all.20 = bf16[16,16,2048]{2,1,0:T(8,128)(2,1)} all-to-all(bf16[16,16,2048]{2,1,0:T(8,128)(2,1)S(1)} %bitcast.20), channel_id=1, replica_groups=mesh['dp'=16,'expert'=16] {'expert'}, dimensions={0} | all-to-all | bytes 2097152 | tf_op jit(solution)/shard_map/rows_out/all_to_all | solution.py:18
  39.4 34.9 %all-gather.2.cloned.1.call-done.w.wd.wg.wu = bf16[2048,2304]{1,0:T(8,128)(2,1)} async-done(((bf16[128,2304]{1,0:T(8,128)(2,1)}), bf16[2048,2304]{1,0:T(8,128)(2,1)}) %all-gather.2.cloned.1.call-update) | async-done | bytes 9437200 | tf_op jit(solution)/shard_map/gather_weights/all_gather | solution.py:353
  74.2 4.6 %forward.2 = (f32[256,1536]{1,0:T(8,128)S(1)}, bf16[256,768]{1,0:T(8,128)(2,1)S(1)}) custom-call(bf16[256,2048]{1,0:T(8,128)(2,1)} %bitcast.2.x.refs_0_.refs_1_, bf16[2048,2304]{1,0:T(8,128)(2,1)} %all-gather.2.cloned.1.call-done.w.wd.wg.wu, bf16[256,2048]{1,0:T(8,128)(2,1)} %collective-permute-done._.refs_2_.refs_4_.refs_5_), custom_call_target="tpu_custom_call" | custom-call | flops 1610612736 | bytes 9306112 | tf_op jit(solution)/shard_map/forward/pallas_call | solution.py:101
  78.8 4.0 %forward.3 = bf16[256,2048]{1,0:T(8,128)(2,1)} custom-call(bf16[256,768]{1,0:T(8,128)(2,1)S(1)} %get-tuple-element.17.h.refs_5_.refs_9_, bf16[2048,2304]{1,0:T(8,128)(2,1)} %all-gather.2.cloned.1.call-done.w.wd.wg.wu), custom_call_target="tpu_custom_call" | custom-call | flops 805306368 | bytes 4587520 | tf_op jit(solution)/shard_map/forward/pallas_call | solution.py:124
  82.9 7.3 %all-to-all-start.1 = ((bf16[16,16,2048]{2,1,0:T(8,128)(2,1)}), bf16[16,16,2048]{2,1,0:T(8,128)(2,1)}, u32[]{:S(2)}, u32[]{:S(2)}) async-start(bf16[16,16,2048]{2,1,0:T(8,128)(2,1)} %bitcast.19), calls=%async_computation.1 | async-start | bytes 2097152 | tf_op jit(solution)/shard_map/combine/all_to_all | solution.py:18
  90.2 1.6 broadcast_select_fusion.w
  92.6 3.9 %convolution_convert_fusion.goal = bf16[256,2048]{1,0:T(8,128)(2,1)} fusion(bf16[768,2048]{1,0:T(8,128)(2,1)} %param.14, s32[256]{0:T(256)S(1)} %eq.37, pred[256]{0:T(512)(128)(4,1)S(1)} %lt.49), kind=kOutput, calls=%fused_computation | convolution fusion | flops 806223872 | bytes 4195584 | tf_op jit(solution)/shard_map/rows_out/dot_general | solution.py:22
  96.5 10.0 %all-to-all-done.1 = bf16[16,16,2048]{2,1,0:T(8,128)(2,1)} async-done(((bf16[16,16,2048]{2,1,0:T(8,128)(2,1)}), bf16[16,16,2048]{2,1,0:T(8,128)(2,1)}, u32[]{:S(2)}, u32[]{:S(2)}) %all-to-all-start.1) | async-done | bytes 1048608 | tf_op jit(solution)/shard_map/combine/all_to_all | solution.py:18
  106.5 3.4 %combine.1 = bf16[256,2048]{1,0:T(8,128)(2,1)} custom-call(bf16[256,256]{1,0:T(8,128)(2,1)} %get-tuple-element.33.high, bf16[256,256]{1,0:T(8,128)(2,1)} %get-tuple-element.32.low, f32[256,1]{1,0:T(8,128)} %broadcast_select_fusion.w, bf16[256,2048]{1,0:T(8,128)(2,1)} %bitcast.7.back, bf16[256,2048]{1,0:T(8,128)(2,1)} %convolution_convert_fusion.goal, ...), custom_call_target="tpu_custom_call" | custom-call | flops 536870912 | bytes 3145728 | tf_op jit(solution)/shard_map/combine/pallas_call | solution.py:149
  109.9 21.1 %all_to_all.21 = bf16[16,16,2048]{2,1,0:T(8,128)(2,1)} all-to-all(bf16[16,16,2048]{2,1,0:T(8,128)(2,1)} %bitcast.18), channel_id=1, replica_groups=mesh['dp'=16,'expert'=16] {'expert'}, dimensions={0} | all-to-all | bytes 2097152 | tf_op jit(solution)/shard_map/combine/all_to_all | solution.py:18
  131.0 4.5 %backward.2.x.refs_4_.refs_8_ = bf16[2,256,768]{2,1,0:T(8,128)(2,1)} custom-call(bf16[256,2048]{1,0:T(8,128)(2,1)} %bitcast.9.x.refs_1_.refs_2_.refs_3_, bf16[2048,2304]{1,0:T(8,128)(2,1)} %all-gather.2.cloned.1.call-done.w.wd.wg.wu, f32[256,1536]{1,0:T(8,128)} %copy-done.1), custom_call_target="tpu_custom_call" | custom-call | flops 805306368 | bytes 6553600 | tf_op jit(solution)/shard_map/backward/pallas_call | solution.py:176
  136.1 2.3 %collective-permute-done.3.refs_6_.refs_10_ = bf16[2,256,768]{2,1,0:T(8,128)(2,1)} collective-permute-done((bf16[2,256,768]{2,1,0:T(8,128)(2,1)}, bf16[2,256,768]{2,1,0:T(8,128)(2,1)}, u32[]{:S(2)}, u32[]{:S(2)}) %collective-permute-start.3) | collective-permute-done | bytes 786464 | tf_op jit(solution)/shard_map/backward/ppermute | solution.py:349
  138.3 2.1 weight_gradients.12
  140.5 3.2 %collective-permute-start.8 = (bf16[64,2304]{1,0:T(8,128)(2,1)S(1)}, bf16[64,2304]{1,0:T(8,128)(2,1)S(1)}, u32[]{:S(2)}, u32[]{:S(2)}) collective-permute-start(bf16[64,2304]{1,0:T(8,128)(2,1)S(1)} %get-tuple-element.23), channel_id=1, source_target_pairs={{0,224},{16,240},{32,0},{48,16},{64,32},{80,48},{96,64},{112,80},{... | collective-permute-start | bytes 884744 | tf_op jit(solution)/shard_map/weight_gradients/ppermute | solution.py:346
  143.8 3.0 %weight_gradients.13 = (f32[128,2304]{1,0:T(8,128)S(1)}, f32[128,2304]{1,0:T(8,128)S(1)}) custom-call(s32[2]{0:T(128)S(1)} %multiply_add_fusion.2.names, bf16[256,2048]{1,0:T(8,128)(2,1)} %bitcast.2.x.refs_0_.refs_1_, bf16[256,2048]{1,0:T(8,128)(2,1)} %bitcast.2.x.refs_0_.refs_1_, bf16[256,2048]{1,0:T(8,128)(2,1)} %bitcast.9.x.refs_1_.refs_2_.refs_3_, ...), custom_call_target="tpu_custom_call" | custom-call | flops 603979776 | bytes 5242880 | tf_op jit(solution)/shard_map/weight_gradients/pallas_call | solution.py:242
  146.9 4.2 %collective-permute-done.4.a = bf16[64,2304]{1,0:T(8,128)(2,1)S(1)} collective-permute-done((bf16[64,2304]{1,0:T(8,128)(2,1)S(1)}, bf16[64,2304]{1,0:T(8,128)(2,1)S(1)}, u32[]{:S(2)}, u32[]{:S(2)}) %collective-permute-start.4) | collective-permute-done | bytes 294944 | tf_op jit(solution)/shard_map/weight_gradients/ppermute | solution.py:346
  151.3 3.5 %collective-permute-start.9 = (bf16[128,2304]{1,0:T(8,128)(2,1)S(1)}, bf16[128,2304]{1,0:T(8,128)(2,1)S(1)}, u32[]{:S(2)}, u32[]{:S(2)}) collective-permute-start(bf16[128,2304]{1,0:T(8,128)(2,1)S(1)} %weight_gradients.19), channel_id=1, source_target_pairs={{0,224},{16,240},{32,0},{48,16},{64,32},{80,48},{96,64},{112,80},{... | collective-permute-start | bytes 1769480 | tf_op jit(solution)/shard_map/weight_gradients/ppermute | solution.py:346
  154.8 5.4 %backward.3.refs_0_ = bf16[256,2048]{1,0:T(8,128)(2,1)} custom-call(bf16[2,256,768]{2,1,0:T(8,128)(2,1)} %backward.2.x.refs_4_.refs_8_, bf16[2048,2304]{1,0:T(8,128)(2,1)} %all-gather.2.cloned.1.call-done.w.wd.wg.wu, bf16[2048,2304]{1,0:T(8,128)(2,1)} %all-gather.2.cloned.1.call-done.w.wd.wg.wu), custom_call_target="tpu_custom_call" | custom-call | flops 1610612736 | bytes 8126464 | tf_op jit(solution)/shard_map/backward/pallas_call | solution.py:201
  160.2 3.0 %weight_gradients.15 = (f32[128,2304]{1,0:T(8,128)S(1)}, f32[128,2304]{1,0:T(8,128)S(1)}) custom-call(s32[2]{0:T(128)S(1)} %get-tuple-element.35.names, bf16[256,2048]{1,0:T(8,128)(2,1)} %bitcast.2.x.refs_0_.refs_1_, bf16[256,2048]{1,0:T(8,128)(2,1)} %bitcast.2.x.refs_0_.refs_1_, bf16[256,2048]{1,0:T(8,128)(2,1)} %bitcast.9.x.refs_1_.refs_2_.refs_3_, ...), custom_call_target="tpu_custom_call" | custom-call | flops 603979776 | bytes 5242880 | tf_op jit(solution)/shard_map/weight_gradients/pallas_call | solution.py:242
  163.3 3.9 %collective-permute-done.5.a = bf16[128,2304]{1,0:T(8,128)(2,1)S(1)} collective-permute-done((bf16[128,2304]{1,0:T(8,128)(2,1)S(1)}, bf16[128,2304]{1,0:T(8,128)(2,1)S(1)}, u32[]{:S(2)}, u32[]{:S(2)}) %collective-permute-start.5) | collective-permute-done | bytes 589856 | tf_op jit(solution)/shard_map/weight_gradients/ppermute | solution.py:346
  169.0 3.2 %collective-permute-start.10 = (bf16[128,2304]{1,0:T(8,128)(2,1)}, bf16[128,2304]{1,0:T(8,128)(2,1)}, u32[]{:S(2)}, u32[]{:S(2)}) collective-permute-start(bf16[128,2304]{1,0:T(8,128)(2,1)} %weight_gradients.20), channel_id=1, source_target_pairs={{0,224},{16,240},{32,0},{48,16},{64,32},{80,48},{96,64},{112,80},{... | collective-permute-start | bytes 1769480 | tf_op jit(solution)/shard_map/weight_gradients/ppermute | solution.py:346
  172.3 5.5 %all-to-all-start.3 = ((bf16[16,16,2048]{2,1,0:T(8,128)(2,1)}), bf16[16,16,2048]{2,1,0:T(8,128)(2,1)}, u32[]{:S(2)}, u32[]{:S(2)}) async-start(bf16[16,16,2048]{2,1,0:T(8,128)(2,1)} %bitcast.17), calls=%async_computation.3 | async-start | bytes 2097152 | tf_op jit(solution)/shard_map/token_gradient/all_to_all | solution.py:18
  177.8 3.0 %weight_gradients.17 = (f32[128,2304]{1,0:T(8,128)S(1)}, f32[128,2304]{1,0:T(8,128)S(1)}) custom-call(s32[2]{0:T(128)S(1)} %get-tuple-element.34.names, bf16[256,2048]{1,0:T(8,128)(2,1)} %bitcast.2.x.refs_0_.refs_1_, bf16[256,2048]{1,0:T(8,128)(2,1)} %bitcast.2.x.refs_0_.refs_1_, bf16[256,2048]{1,0:T(8,128)(2,1)} %bitcast.9.x.refs_1_.refs_2_.refs_3_, ...), custom_call_target="tpu_custom_call" | custom-call | flops 603979776 | bytes 5242880 | tf_op jit(solution)/shard_map/weight_gradients/pallas_call | solution.py:242
  180.9 2.7 %collective-permute-done.6.a = bf16[128,2304]{1,0:T(8,128)(2,1)} collective-permute-done((bf16[128,2304]{1,0:T(8,128)(2,1)}, bf16[128,2304]{1,0:T(8,128)(2,1)}, u32[]{:S(2)}, u32[]{:S(2)}) %collective-permute-start.6) | collective-permute-done | bytes 589856 | tf_op jit(solution)/shard_map/weight_gradients/ppermute | solution.py:346
  183.5 2.0 weight_gradients.18
  185.5 2.0 weight_gradients.21
  187.5 3.2 %collective-permute-start.11 = (bf16[128,2304]{1,0:T(8,128)(2,1)}, bf16[128,2304]{1,0:T(8,128)(2,1)}, u32[]{:S(2)}, u32[]{:S(2)}) collective-permute-start(bf16[128,2304]{1,0:T(8,128)(2,1)} %weight_gradients.21), channel_id=1, source_target_pairs={{0,224},{16,240},{32,0},{48,16},{64,32},{80,48},{96,64},{112,80},{... | collective-permute-start | bytes 1769480 | tf_op jit(solution)/shard_map/weight_gradients/ppermute | solution.py:346
  192.7 3.5 %token_gradient.1 = bf16[768,2048]{1,0:T(8,128)(2,1)} custom-call(bf16[768,256]{1,0:T(8,128)(2,1)} %fusion.which, bf16[256,2048]{1,0:T(8,128)(2,1)} %bitcast.11.back), custom_call_target="tpu_custom_call" | custom-call | flops 805306368 | bytes 4194304 | tf_op jit(solution)/shard_map/token_gradient/pallas_call | solution.py:314
  196.2 2.1 weight_gradients.22.mine
  198.3 1.7 collective-permute-done.7.a
  201.3 2.4 %weight_gradients.23 = (f32[128,1,768]{2,1,0:T(1,128)}, f32[128,1,768]{2,1,0:T(1,128)}, f32[128,1,768]{2,1,0:T(1,128)}) custom-call(bf16[128,2304]{1,0:T(8,128)(2,1)} %collective-permute-done.7.a, bf16[128,2304]{1,0:T(8,128)(2,1)} %collective-permute-done.11.b, f32[128,2304]{1,0:T(8,128)S(1)} %weight_gradients.22.mine), custom_call_target="tpu_custom_call" | custom-call | flops 1179648 | bytes 3538944 | tf_op jit(solution)/shard_map/weight_gradients/pallas_call | solution.py:295
  (50 shorter events, 13.6 us)
Async XLA Ops:
  7.2 5.0 %copy-start = (bf16[768,2048]{1,0:T(8,128)(2,1)S(1)}, bf16[768,2048]{1,0:T(8,128)(2,1)}, u32[]{:S(2)}) copy-start(bf16[768,2048]{1,0:T(8,128)(2,1)} %param.13) | copy-start | bytes 9437188
  7.2 67.1 %all-gather.2.cloned.1.call-start = ((), (), s32[]{:S(2)}) async-start(), calls=%async_computation.4 | async-start | bytes 10027008 | tf_op jit(solution)/shard_map/gather_weights/all_gather | solution.py:353
  12.2 25.5 %copy-start.2 = (f32[1,16,1,16]{3,2,1,0:T(1,128)S(1)}, f32[1,16,1,16]{3,2,1,0:T(1,128)}, u32[]{:S(2)}) copy-start(f32[1,16,1,16]{3,2,1,0:T(1,128)} %param.17) | copy-start | bytes 3076
  36.4 3.0 %collective-permute-start = (bf16[256,2048]{1,0:T(8,128)(2,1)}, bf16[256,2048]{1,0:T(8,128)(2,1)}, u32[]{:S(2)}, u32[]{:S(2)}) collective-permute-start(bf16[256,2048]{1,0:T(8,128)(2,1)} %bitcast.2.x.refs_0_.refs_1_), channel_id=1, source_target_pairs={{0,16},{16,0},{32,48},{48,32},{64,80},{80,64},{96,112},{112,96},{1... | collective-permute-start | bytes 3145736 | tf_op jit(solution)/shard_map/rows_out/ppermute | solution.py:349
  78.8 4.1 %copy-start.1 = (f32[256,1536]{1,0:T(8,128)}, f32[256,1536]{1,0:T(8,128)S(1)}, u32[]{:S(2)}) copy-start(f32[256,1536]{1,0:T(8,128)S(1)} %get-tuple-element.18.pre_ref) | copy-start | bytes 4718596
  82.9 23.6 %all-to-all-start.1 = ((bf16[16,16,2048]{2,1,0:T(8,128)(2,1)}), bf16[16,16,2048]{2,1,0:T(8,128)(2,1)}, u32[]{:S(2)}, u32[]{:S(2)}) async-start(bf16[16,16,2048]{2,1,0:T(8,128)(2,1)} %bitcast.19), calls=%async_computation.1 | async-start | bytes 2097152 | tf_op jit(solution)/shard_map/combine/all_to_all | solution.py:18
  91.8 4.7 %collective-permute-start.1 = (bf16[256,768]{1,0:T(8,128)(2,1)S(1)}, bf16[256,768]{1,0:T(8,128)(2,1)}, u32[]{:S(2)}, u32[]{:S(2)}) collective-permute-start(bf16[256,768]{1,0:T(8,128)(2,1)S(1)} %get-tuple-element.17.h.refs_5_.refs_9_), channel_id=1, source_target_pairs={{0,16},{16,0},{32,48},{48,32},{64,80},{80,64},{96,112},{112,96},{1... | collective-permute-start | bytes 1179656 | tf_op jit(solution)/shard_map/forward/ppermute | solution.py:349
  131.0 7.3 %collective-permute-start.2 = (bf16[256,2048]{1,0:T(8,128)(2,1)}, bf16[256,2048]{1,0:T(8,128)(2,1)}, u32[]{:S(2)}, u32[]{:S(2)}) collective-permute-start(bf16[256,2048]{1,0:T(8,128)(2,1)} %bitcast.9.x.refs_1_.refs_2_.refs_3_), channel_id=1, source_target_pairs={{0,16},{16,0},{32,48},{48,32},{64,80},{80,64},{96,112},{112,96},{1... | collective-permute-start | bytes 3145736 | tf_op jit(solution)/shard_map/combine/ppermute | solution.py:349
  135.6 2.8 %collective-permute-start.3 = (bf16[2,256,768]{2,1,0:T(8,128)(2,1)}, bf16[2,256,768]{2,1,0:T(8,128)(2,1)}, u32[]{:S(2)}, u32[]{:S(2)}) collective-permute-start(bf16[2,256,768]{2,1,0:T(8,128)(2,1)} %backward.2.x.refs_4_.refs_8_), channel_id=1, source_target_pairs={{0,16},{16,0},{32,48},{48,32},{64,80},{80,64},{96,112},{112,96},{1... | collective-permute-start | bytes 2359304 | tf_op jit(solution)/shard_map/backward/ppermute | solution.py:349
  138.3 5.4 %copy-start.5 = (s32[2]{0:T(128)S(1)}, s32[2]{0:T(128)}, u32[]{:S(2)}) copy-start(s32[2]{0:T(128)} %constant.49.clone) | copy-start | bytes 28
  140.4 10.6 %collective-permute-start.4 = (bf16[64,2304]{1,0:T(8,128)(2,1)S(1)}, bf16[64,2304]{1,0:T(8,128)(2,1)S(1)}, u32[]{:S(2)}, u32[]{:S(2)}) collective-permute-start(bf16[64,2304]{1,0:T(8,128)(2,1)S(1)} %get-tuple-element.19), channel_id=1, source_target_pairs={{0,32},{16,48},{32,64},{48,80},{64,96},{80,112},{96,128},{112,144}... | collective-permute-start | bytes 884744 | tf_op jit(solution)/shard_map/weight_gradients/ppermute | solution.py:346
  140.5 10.7 %collective-permute-start.8 = (bf16[64,2304]{1,0:T(8,128)(2,1)S(1)}, bf16[64,2304]{1,0:T(8,128)(2,1)S(1)}, u32[]{:S(2)}, u32[]{:S(2)}) collective-permute-start(bf16[64,2304]{1,0:T(8,128)(2,1)S(1)} %get-tuple-element.23), channel_id=1, source_target_pairs={{0,224},{16,240},{32,0},{48,16},{64,32},{80,48},{96,64},{112,80},{... | collective-permute-start | bytes 884744 | tf_op jit(solution)/shard_map/weight_gradients/ppermute | solution.py:346
  146.8 7.9 %copy-start.3 = (s32[2]{0:T(128)S(1)}, s32[2]{0:T(128)}, u32[]{:S(2)}) copy-start(s32[2]{0:T(128)} %constant.51.clone) | copy-start | bytes 28
  146.9 7.9 %copy-start.4 = (s32[2]{0:T(128)S(1)}, s32[2]{0:T(128)}, u32[]{:S(2)}) copy-start(s32[2]{0:T(128)} %constant.50.clone) | copy-start | bytes 28
  151.1 16.1 %collective-permute-start.5 = (bf16[128,2304]{1,0:T(8,128)(2,1)S(1)}, bf16[128,2304]{1,0:T(8,128)(2,1)S(1)}, u32[]{:S(2)}, u32[]{:S(2)}) collective-permute-start(bf16[128,2304]{1,0:T(8,128)(2,1)S(1)} %weight_gradients.14), channel_id=1, source_target_pairs={{0,32},{16,48},{32,64},{48,80},{64,96},{80,112},{96,128},{112,144}... | collective-permute-start | bytes 1769480 | tf_op jit(solution)/shard_map/weight_gradients/ppermute | solution.py:346
  151.3 16.8 %collective-permute-start.9 = (bf16[128,2304]{1,0:T(8,128)(2,1)S(1)}, bf16[128,2304]{1,0:T(8,128)(2,1)S(1)}, u32[]{:S(2)}, u32[]{:S(2)}) collective-permute-start(bf16[128,2304]{1,0:T(8,128)(2,1)S(1)} %weight_gradients.19), channel_id=1, source_target_pairs={{0,224},{16,240},{32,0},{48,16},{64,32},{80,48},{96,64},{112,80},{... | collective-permute-start | bytes 1769480 | tf_op jit(solution)/shard_map/weight_gradients/ppermute | solution.py:346
  168.1 15.4 %collective-permute-start.6 = (bf16[128,2304]{1,0:T(8,128)(2,1)}, bf16[128,2304]{1,0:T(8,128)(2,1)}, u32[]{:S(2)}, u32[]{:S(2)}) collective-permute-start(bf16[128,2304]{1,0:T(8,128)(2,1)} %weight_gradients.16), channel_id=1, source_target_pairs={{0,32},{16,48},{32,64},{48,80},{64,96},{80,112},{96,128},{112,144}... | collective-permute-start | bytes 1769480 | tf_op jit(solution)/shard_map/weight_gradients/ppermute | solution.py:346
  169.0 16.5 %collective-permute-start.10 = (bf16[128,2304]{1,0:T(8,128)(2,1)}, bf16[128,2304]{1,0:T(8,128)(2,1)}, u32[]{:S(2)}, u32[]{:S(2)}) collective-permute-start(bf16[128,2304]{1,0:T(8,128)(2,1)} %weight_gradients.20), channel_id=1, source_target_pairs={{0,224},{16,240},{32,0},{48,16},{64,32},{80,48},{96,64},{112,80},{... | collective-permute-start | bytes 1769480 | tf_op jit(solution)/shard_map/weight_gradients/ppermute | solution.py:346
  172.3 20.4 %all-to-all-start.3 = ((bf16[16,16,2048]{2,1,0:T(8,128)(2,1)}), bf16[16,16,2048]{2,1,0:T(8,128)(2,1)}, u32[]{:S(2)}, u32[]{:S(2)}) async-start(bf16[16,16,2048]{2,1,0:T(8,128)(2,1)} %bitcast.17), calls=%async_computation.3 | async-start | bytes 2097152 | tf_op jit(solution)/shard_map/token_gradient/all_to_all | solution.py:18
  185.5 14.5 %collective-permute-start.7 = (bf16[128,2304]{1,0:T(8,128)(2,1)}, bf16[128,2304]{1,0:T(8,128)(2,1)}, u32[]{:S(2)}, u32[]{:S(2)}) collective-permute-start(bf16[128,2304]{1,0:T(8,128)(2,1)} %weight_gradients.18), channel_id=1, source_target_pairs={{0,32},{16,48},{32,64},{48,80},{64,96},{80,112},{96,128},{112,144}... | collective-permute-start | bytes 1769480 | tf_op jit(solution)/shard_map/weight_gradients/ppermute | solution.py:346
  187.5 13.8 %collective-permute-start.11 = (bf16[128,2304]{1,0:T(8,128)(2,1)}, bf16[128,2304]{1,0:T(8,128)(2,1)}, u32[]{:S(2)}, u32[]{:S(2)}) collective-permute-start(bf16[128,2304]{1,0:T(8,128)(2,1)} %weight_gradients.21), channel_id=1, source_target_pairs={{0,224},{16,240},{32,0},{48,16},{64,32},{80,48},{96,64},{112,80},{... | collective-permute-start | bytes 1769480 | tf_op jit(solution)/shard_map/weight_gradients/ppermute | solution.py:346
Sparse Core Ops, SparseCore 0:
  10.4 63.7 all-gather.1
